TPU v7x, 512 devices: a whole 4x4x16 slice. The times are simulated.
512 devices in a mesh: dp: 64 (over z, y), seq: 8 (over x, core).
Axes of the slice: x: 4, y: 4, z: 16, core: 2. Of those that a mesh axis runs over, the one named last changes fastest.
Arguments:
- q_in: bfloat16 [65536, 3072], P(('dp', 'seq')), may hold values from -48 to 48
- k_in: bfloat16 [65536, 3072], P(('dp', 'seq')), may hold values from -48 to 48
- v_in: bfloat16 [65536, 3072], P(('dp', 'seq')), may hold values from -6 to 6
- gain_q: float32 [3072], P('dp'), may hold values from 0.5 to 2
- gain_k: float32 [3072], P('dp'), may hold values from 0.5 to 2
- clip_ids: int32 [64, 1024], P('dp'), may hold values from 0 to 3, never falling along the last dimension, each value on 1 to 512 neighbouring positions
Outputs:
- d_q: bfloat16 [65536, 3072], P(('dp', 'seq'))
- d_k: bfloat16 [65536, 3072], P(('dp', 'seq'))
- d_v: bfloat16 [65536, 3072], P(('dp', 'seq'))
- d_gain_q: float32 [3072], P('dp')
- d_gain_k: float32 [3072], P('dp')
All inputs are finite; a program needn't handle non-finite values.
Results may differ from a plain program's by a relative error of at most 0.012.
The roundings to bfloat16 on the way count: a program that leaves them out, or rounds other values in their place, can miss the bound.
Values may be sent and summed in bfloat16 or wider, within the bound.
No kernel may reach another device: no remote copies, remote signals or barrier semaphores. Data moves between devices by JAX's collectives and lax.ppermute only.
A program may use at most 64 MiB of HBM per device.

v0:
```python
import jax
import jax.numpy as jnp
from jax import lax
from jax.sharding import PartitionSpec as P

HD = 128
QB = 512


EPS = 1e-06


def normalize(x, gain):
    xf = x.astype(jnp.float32)
    inv = lax.rsqrt(jnp.mean(xf * xf, axis=1, keepdims=True) + EPS)
    hat = xf * inv
    return ((hat * gain).astype(jnp.bfloat16), inv, hat)


def norm_back(dnorm, gain, inv, hat):
    df = dnorm.astype(jnp.float32)
    dhat = df * gain
    grad = inv * (dhat - hat * jnp.mean(dhat * hat, axis=1, keepdims=True))
    return (grad.astype(jnp.bfloat16), jnp.sum(df * hat, axis=0))


def softmax_parts(scores, same):
    scores = jnp.where(same, scores, -1e30)
    top = jnp.max(scores, axis=1, keepdims=True)
    expo = jnp.where(same, jnp.exp(scores - top), 0.0)
    return expo / jnp.sum(expo, axis=1, keepdims=True)


def attend(q_heads, k_heads, v_heads, ids):
    group, local_width = q_heads.shape
    heads = local_width // HD
    block = min(QB, group)
    blocks = group // block
    scale = HD ** (-0.5)
    block_ids = jnp.arange(blocks, dtype=jnp.int32)

    def one_head(head, buffers):
        offset = head * HD
        q_one = lax.dynamic_slice_in_dim(q_heads, offset, HD, 1)
        k_one = lax.dynamic_slice_in_dim(k_heads, offset, HD, 1)
        v_one = lax.dynamic_slice_in_dim(v_heads, offset, HD, 1)

        def step(carry, index):
            acc_k, acc_v = carry
            first = index * block
            q_block = lax.dynamic_slice_in_dim(q_one, first, block, 0)
            ids_q = lax.dynamic_slice_in_dim(ids, first, block, 0)
            same = ids_q[:, None] == ids[None, :]
            scores = (
                jnp.einsum("qd,kd->qk", q_block, k_one, preferred_element_type=jnp.float32) * scale
            )
            probs = softmax_parts(scores, same)
            probs_b = probs.astype(jnp.bfloat16)
            attn = jnp.dot(probs_b, v_one, preferred_element_type=jnp.float32).astype(jnp.bfloat16)
            part_v = jnp.einsum("qk,qd->kd", probs_b, attn, preferred_element_type=jnp.float32)
            dprobs = jnp.einsum("qd,kd->qk", attn, v_one, preferred_element_type=jnp.float32)
            delta = jnp.sum(probs * dprobs, axis=1, keepdims=True)
            dscore = (probs * (dprobs - delta) * scale).astype(jnp.bfloat16)
            grad_q = jnp.dot(dscore, k_one, preferred_element_type=jnp.float32).astype(jnp.bfloat16)
            part_k = jnp.einsum("qk,qd->kd", dscore, q_block, preferred_element_type=jnp.float32)
            return ((acc_k + part_k, acc_v + part_v), grad_q)

        zeros = jnp.zeros((group, HD), jnp.float32)
        (acc_k, acc_v), grad_blocks = lax.scan(step, (zeros, zeros), block_ids)
        grad_q = grad_blocks.reshape(group, HD)
        buf_q, buf_k, buf_v = buffers
        buf_q = lax.dynamic_update_slice_in_dim(buf_q, grad_q, offset, 1)
        buf_k = lax.dynamic_update_slice_in_dim(buf_k, acc_k.astype(jnp.bfloat16), offset, 1)
        buf_v = lax.dynamic_update_slice_in_dim(buf_v, acc_v.astype(jnp.bfloat16), offset, 1)
        return (buf_q, buf_k, buf_v)

    empty = jnp.zeros((group, local_width), jnp.bfloat16)
    return lax.fori_loop(0, heads, one_head, (empty, empty, empty))


def local(q_in, k_in, v_in, gain_q, gain_k, clip_ids):
    full_q, full_k = (
        lax.all_gather(gain_q, "dp", axis=0, tiled=True),
        lax.all_gather(gain_k, "dp", axis=0, tiled=True),
    )
    ids = clip_ids[0]
    q_norm, inv_q, hat_q = normalize(q_in, full_q)
    k_norm, inv_k, hat_k = normalize(k_in, full_k)
    q_heads, k_heads, v_heads = (
        lax.all_to_all(q_norm, "seq", split_axis=1, concat_axis=0, tiled=True),
        lax.all_to_all(k_norm, "seq", split_axis=1, concat_axis=0, tiled=True),
        lax.all_to_all(v_in, "seq", split_axis=1, concat_axis=0, tiled=True),
    )
    dq_heads, dk_heads, dv_heads = attend(q_heads, k_heads, v_heads, ids)
    dq_norm, dk_norm, d_v = (
        lax.all_to_all(dq_heads, "seq", split_axis=0, concat_axis=1, tiled=True),
        lax.all_to_all(dk_heads, "seq", split_axis=0, concat_axis=1, tiled=True),
        lax.all_to_all(dv_heads, "seq", split_axis=0, concat_axis=1, tiled=True),
    )
    d_q, part_q = norm_back(dq_norm, full_q, inv_q, hat_q)
    d_k, part_k = norm_back(dk_norm, full_k, inv_k, hat_k)
    whole_q, whole_k = lax.psum((part_q, part_k), "seq")
    d_gain_q, d_gain_k = (
        lax.psum_scatter(whole_q, "dp", scatter_dimension=0, tiled=True),
        lax.psum_scatter(whole_k, "dp", scatter_dimension=0, tiled=True),
    )
    return (d_q, d_k, d_v, d_gain_q, d_gain_k)


def solution(mesh):
    in_specs = (
        P(("dp", "seq"), None),
        P(("dp", "seq"), None),
        P(("dp", "seq"), None),
        P("dp"),
        P("dp"),
        P("dp", None),
    )
    out_specs = (
        P(("dp", "seq"), None),
        P(("dp", "seq"), None),
        P(("dp", "seq"), None),
        P("dp"),
        P("dp"),
    )
    return jax.shard_map(local, mesh=mesh, in_specs=in_specs, out_specs=out_specs, check_vma=False)
```

profile of v0, /device:TPU:1, one launch (start us, length us, event | category | flops | bytes accessed | tf_op | source)
XLA Modules:
  0.0 752.5 jit_solution(9093994664955280005)
XLA Ops:
  0.7 1.6 copy.20
  5.4 231.5 %all-reduce.5 = (f32[3072]{0:T(1024)S(1)}, f32[3072]{0:T(1024)S(1)}) all-reduce(f32[3072]{0:T(1024)S(1)} %dynamic-update-slice, f32[3072]{0:T(1024)S(1)} %dynamic-update-slice.1), channel_id=1, replica_groups=mesh['dp'=64,'seq'=8] {'dp'}, use_global_device_ids=true, to_apply=%add | all-reduce | flops 6144 | bytes 49152
  236.9 1.6 fusion.22
  238.5 1.2 copy.19
  239.7 60.2 %all-to-all-start = ((bf16[128,8,384]{2,0,1:T(8,128)(2,1)}), bf16[128,8,384]{2,0,1:T(8,128)(2,1)S(1)}, u32[]{:S(2)}, u32[]{:S(2)}) async-start(bf16[128,8,384]{2,0,1:T(8,128)(2,1)} %copy.19), calls=%async_computation | async-start | bytes 1572864 | tf_op jit(solution)/shard_map/all_to_all | solution.py:90
  300.0 1.2 copy.21
  301.1 11.1 %all-to-all-done = bf16[128,8,384]{2,0,1:T(8,128)(2,1)S(1)} async-done(((bf16[128,8,384]{2,0,1:T(8,128)(2,1)}), bf16[128,8,384]{2,0,1:T(8,128)(2,1)S(1)}, u32[]{:S(2)}, u32[]{:S(2)}) %all-to-all-start) | async-done | bytes 786464 | tf_op jit(solution)/shard_map/all_to_all | solution.py:90
  312.2 4.3 all-to-all-start.1
  317.5 11.3 %all-to-all-done.1 = bf16[128,8,384]{2,0,1:T(8,128)(2,1)S(1)} async-done(((bf16[128,8,384]{2,0,1:T(8,128)(2,1)}), bf16[128,8,384]{2,0,1:T(8,128)(2,1)S(1)}, u32[]{:S(2)}, u32[]{:S(2)}) %all-to-all-start.1) | async-done | bytes 786464 | tf_op jit(solution)/shard_map/all_to_all | solution.py:91
  328.9 5.0 all-to-all-start.2
  333.8 12.4 %all-to-all-done.2 = bf16[128,8,384]{2,0,1:T(8,128)(2,1)} async-done(((bf16[128,8,384]{2,0,1:T(8,128)(2,1)}), bf16[128,8,384]{2,0,1:T(8,128)(2,1)}, u32[]{:S(2)}, u32[]{:S(2)}) %all-to-all-start.2) | async-done | bytes 786464 | tf_op jit(solution)/shard_map/all_to_all | solution.py:92
  349.1 66.7 %while.55 = (s32[]{:T(128)}, bf16[1024,384]{1,0:T(8,128)(2,1)}, bf16[1024,384]{1,0:T(8,128)(2,1)}, bf16[1024,384]{1,0:T(8,128)(2,1)}, bf16[1024,384]{1,0:T(8,128...) while((s32[]{:T(128)}, bf16[1024,384]{1,0:T(8,128)(2,1)}, ...), condition=%wide.region_8.9_spmd.clone, body=%wide.region_2.8_spmd.clone.sunk | while | flops 821950976 | bytes 65322440 | solution.py:78
  349.2 1.2 constant_dynamic-slice_fusion.8
  350.4 18.4 %while.56 = (s32[]{:T(128)}, f32[1024,128]{1,0:T(8,128)S(1)}, f32[1024,128]{1,0:T(8,128)S(1)}, bf16[2,512,128]{2,1,0:T(8,128)(2,1)}, s32[2]{0:T(128)S(1)}, /*ind...) while((s32[]{:T(128)}, f32[1024,128]{1,0:T(8,128)S(1)}, ...), condition=%wide.region_7.7_spmd.clone, body=%wide.region_3.6_spmd.clone.sunk | while | flops 821688832 | bytes 49069044 | solution.py:69
  356.5 1.1 multiply_convert_fusion.2
  358.5 1.1 fusion.74
  364.6 1.1 copy-done.1
  365.7 1.1 multiply_convert_fusion.2
  367.7 1.1 fusion.74
  369.7 1.7 constant_dynamic-update-slice_fusion.2
  371.4 1.2 constant_dynamic-slice_fusion.8
  372.7 18.4 %while.56 = (s32[]{:T(128)}, f32[1024,128]{1,0:T(8,128)S(1)}, f32[1024,128]{1,0:T(8,128)S(1)}, bf16[2,512,128]{2,1,0:T(8,128)(2,1)}, s32[2]{0:T(128)S(1)}, /*ind...) while((s32[]{:T(128)}, f32[1024,128]{1,0:T(8,128)S(1)}, ...), condition=%wide.region_7.7_spmd.clone, body=%wide.region_3.6_spmd.clone.sunk | while | flops 821688832 | bytes 49069044 | solution.py:69
  378.7 1.1 multiply_convert_fusion.2
  380.8 1.1 fusion.74
  386.8 1.1 copy-done.1
  387.9 1.1 multiply_convert_fusion.2
  389.9 1.1 fusion.74
  391.9 1.7 constant_dynamic-update-slice_fusion.2
  393.7 1.2 constant_dynamic-slice_fusion.8
  394.9 18.4 %while.56 = (s32[]{:T(128)}, f32[1024,128]{1,0:T(8,128)S(1)}, f32[1024,128]{1,0:T(8,128)S(1)}, bf16[2,512,128]{2,1,0:T(8,128)(2,1)}, s32[2]{0:T(128)S(1)}, /*ind...) while((s32[]{:T(128)}, f32[1024,128]{1,0:T(8,128)S(1)}, ...), condition=%wide.region_7.7_spmd.clone, body=%wide.region_3.6_spmd.clone.sunk | while | flops 821688832 | bytes 49069044 | solution.py:69
  401.0 1.1 multiply_convert_fusion.2
  403.0 1.1 fusion.74
  409.1 1.1 copy-done.1
  410.1 1.1 multiply_convert_fusion.2
  412.2 1.1 fusion.74
  414.1 1.7 constant_dynamic-update-slice_fusion.2
  415.8 16.7 %all_to_all.102 = bf16[8,128,384]{2,1,0:T(8,128)(2,1)S(1)} all-to-all(bf16[8,128,384]{2,1,0:T(8,128)(2,1)} %bitcast.93), channel_id=1, replica_groups=mesh['dp'=64,'seq'=8] {'seq'}, dimensions={0} | all-to-all | bytes 1572864 | tf_op jit(solution)/shard_map/all_to_all | solution.py:97
  432.5 4.5 all-to-all-start.3
  439.1 10.2 %all-to-all-done.3 = bf16[8,128,384]{2,1,0:T(8,128)(2,1)S(1)} async-done(((bf16[8,128,384]{2,1,0:T(8,128)(2,1)}), bf16[8,128,384]{2,1,0:T(8,128)(2,1)S(1)}, u32[]{:S(2)}, u32[]{:S(2)}) %all-to-all-start.3) | async-done | bytes 786464 | tf_op jit(solution)/shard_map/all_to_all | solution.py:96
  450.2 5.0 all-to-all-start.5
  455.1 1.5 copy.23
  457.7 219.5 %all-reduce.4 = (f32[3072]{0:T(1024)S(1)}, f32[3072]{0:T(1024)S(1)}) all-reduce(f32[3072]{0:T(1024)S(1)} %get-tuple-element.306, f32[3072]{0:T(1024)S(1)} %get-tuple-element.304), channel_id=2, replica_groups=mesh['dp'=64,'seq'=8] {'dp'}, use_global_device_ids=true, to_apply=%region_13.14.clone | all-reduce | flops 6144 | bytes 49152
  677.3 1.4 fusion.33
  678.7 2.3 copy.27
  681.5 1.2 copy.26
  682.6 1.5 copy.25
  684.1 1.2 copy.28
  685.3 67.2 %all-reduce.6 = (f32[48]{0:T(128)}, f32[48]{0:T(128)}) all-reduce(f32[48]{0:T(128)S(1)} %dynamic-slice.3, f32[48]{0:T(128)S(1)} %dynamic-slice.5), channel_id=1, replica_groups=mesh['dp'=64,'seq'=8] {'seq'}, use_global_device_ids=true, to_apply=%region_12.13 | all-reduce | flops 96 | bytes 768 | tf_op jit(solution)/shard_map/psum | solution.py:102
  (253 shorter events, 47.8 us)
Async XLA Ops:
  0.6 2.1 copy-start.16
  0.7 2.9 copy-start.26
  0.7 4.2 copy-start.27
  0.7 4.4 copy-start.28
  2.3 236.2 %copy-start.9 = (bf16[128,3072]{0,1:T(8,128)(2,1)}, bf16[128,3072]{0,1:T(8,128)(2,1)S(1)}, u32[]{:S(2)}) copy-start(bf16[128,3072]{0,1:T(8,128)(2,1)S(1)} %copy.20) | copy-start | bytes 2359300
  2.7 235.8 %copy-start.24 = (f32[128]{0:T(128)}, f32[128]{0:T(128)S(1)}, u32[]{:S(2)}) copy-start(f32[128]{0:T(128)S(1)} %add_rsqrt_fusion) | copy-start | bytes 1540
  3.1 236.6 %copy-start.7 = (bf16[128,3072]{0,1:T(8,128)(2,1)}, bf16[128,3072]{0,1:T(8,128)(2,1)S(1)}, u32[]{:S(2)}) copy-start(bf16[128,3072]{0,1:T(8,128)(2,1)S(1)} %copy.18) | copy-start | bytes 2359300
  3.5 236.1 %copy-start.22 = (f32[128]{0:T(128)}, f32[128]{0:T(128)S(1)}, u32[]{:S(2)}) copy-start(f32[128]{0:T(128)S(1)} %add_rsqrt_fusion.1) | copy-start | bytes 1540
  236.9 2.8 copy-start.18
  236.9 2.8 copy-start.20
  239.7 76.9 %copy-start.17 = (bf16[128,3072]{1,0:T(8,128)(2,1)S(1)}, bf16[128,3072]{1,0:T(8,128)(2,1)}, u32[]{:S(2)}) copy-start(bf16[128,3072]{1,0:T(8,128)(2,1)} %param.12) | copy-start | bytes 2359300
  239.7 72.5 %all-to-all-start = ((bf16[128,8,384]{2,0,1:T(8,128)(2,1)}), bf16[128,8,384]{2,0,1:T(8,128)(2,1)S(1)}, u32[]{:S(2)}, u32[]{:S(2)}) async-start(bf16[128,8,384]{2,0,1:T(8,128)(2,1)} %copy.19), calls=%async_computation | async-start | bytes 1572864 | tf_op jit(solution)/shard_map/all_to_all | solution.py:90
  312.2 16.6 %all-to-all-start.1 = ((bf16[128,8,384]{2,0,1:T(8,128)(2,1)}), bf16[128,8,384]{2,0,1:T(8,128)(2,1)S(1)}, u32[]{:S(2)}, u32[]{:S(2)}) async-start(bf16[128,8,384]{2,0,1:T(8,128)(2,1)} %copy.21), calls=%async_computation.1 | async-start | bytes 1572864 | tf_op jit(solution)/shard_map/all_to_all | solution.py:91
  317.5 31.6 %copy-start.6 = (s32[1,1024]{1,0:T(1,128)S(1)}, s32[1,1024]{1,0:T(1,128)}, u32[]{:S(2)}) copy-start(s32[1,1024]{1,0:T(1,128)} %param.15) | copy-start | bytes 12292
  328.9 17.4 %all-to-all-start.2 = ((bf16[128,8,384]{2,0,1:T(8,128)(2,1)}), bf16[128,8,384]{2,0,1:T(8,128)(2,1)}, u32[]{:S(2)}, u32[]{:S(2)}) async-start(bf16[128,8,384]{2,0,1:T(8,128)(2,1)} %bitcast.56), calls=%async_computation.2 | async-start | bytes 1572864 | tf_op jit(solution)/shard_map/all_to_all | solution.py:92
  350.5 1.9 copy-start.2
  350.5 1.9 copy-start.4
  350.5 2.6 copy-start.29
  357.6 2.0 copy-start.30
  359.6 1.9 copy-start.2
  359.6 1.9 copy-start.4
  359.6 2.6 copy-start.29
  366.8 2.0 copy-start.30
  368.8 2.5 copy-start.12
  368.8 2.5 copy-start.14
  372.7 1.9 copy-start.2
  372.7 2.6 copy-start.29
  379.8 2.0 copy-start.30
  381.9 1.9 copy-start.4
  381.9 2.6 copy-start.29
  389.0 2.0 copy-start.30
  391.0 2.5 copy-start.12
  391.0 2.5 copy-start.14
  394.9 2.6 copy-start.29
  402.1 2.0 copy-start.30
  404.1 1.9 copy-start.4
  404.1 2.6 copy-start.29
  411.2 2.0 copy-start.30
  413.3 2.5 copy-start.12
  413.3 2.5 copy-start.14
  415.8 22.2 %copy-start.10 = (bf16[128,3072]{0,1:T(8,128)(2,1)S(1)}, bf16[128,3072]{0,1:T(8,128)(2,1)}, u32[]{:S(2)}) copy-start(bf16[128,3072]{0,1:T(8,128)(2,1)} %copy-done.9) | copy-start | bytes 2359300
  415.8 22.2 %copy-start.21 = (f32[3072]{0:T(1024)S(1)}, f32[3072]{0:T(1024)}, u32[]{:S(2)}) copy-start(f32[3072]{0:T(1024)} %copy-done.20) | copy-start | bytes 36868
  415.8 22.2 %copy-start.25 = (f32[128]{0:T(128)S(1)}, f32[128]{0:T(128)}, u32[]{:S(2)}) copy-start(f32[128]{0:T(128)} %copy-done.24) | copy-start | bytes 1540
  432.5 16.8 %all-to-all-start.3 = ((bf16[8,128,384]{2,1,0:T(8,128)(2,1)}), bf16[8,128,384]{2,1,0:T(8,128)(2,1)S(1)}, u32[]{:S(2)}, u32[]{:S(2)}) async-start(bf16[8,128,384]{2,1,0:T(8,128)(2,1)} %bitcast.92), calls=%async_computation.3 | async-start | bytes 1572864 | tf_op jit(solution)/shard_map/all_to_all | solution.py:96
  438.0 18.6 %copy-start.8 = (bf16[128,3072]{0,1:T(8,128)(2,1)S(1)}, bf16[128,3072]{0,1:T(8,128)(2,1)}, u32[]{:S(2)}) copy-start(bf16[128,3072]{0,1:T(8,128)(2,1)} %copy-done.7) | copy-start | bytes 2359300
  438.1 18.6 %copy-start.19 = (f32[3072]{0:T(1024)S(1)}, f32[3072]{0:T(1024)}, u32[]{:S(2)}) copy-start(f32[3072]{0:T(1024)} %copy-done.18) | copy-start | bytes 36868
  438.1 18.6 %copy-start.23 = (f32[128]{0:T(128)S(1)}, f32[128]{0:T(128)}, u32[]{:S(2)}) copy-start(f32[128]{0:T(128)} %copy-done.22) | copy-start | bytes 1540
  450.2 232.5 %all-to-all-start.5 = ((bf16[8,128,384]{2,1,0:T(8,128)(2,1)}), bf16[8,128,384]{2,1,0:T(8,128)(2,1)}, u32[]{:S(2)}, u32[]{:S(2)}) async-start(bf16[8,128,384]{2,1,0:T(8,128)(2,1)} %bitcast.94), calls=%async_computation.5 | async-start | bytes 1572864 | tf_op jit(solution)/shard_map/all_to_all | solution.py:98
  (36 other events, 48.8 us)
where the time goes:
time: 754 us; the launch traced here: 753 us
  blocking collectives  535 us (71%)
  starting transfers between devices  79 us (10%)
  waiting for transfers between devices  45.1 us (6%)
  local copies, waits for them, and re-layouts  39.7 us (5%)
  other arithmetic  23.9 us (3%)
  matrix products  23.4 us (3%)
    unnamed x2, blocking collectives  451 us
    psum x1, blocking collectives, local(): whole_q, whole_k = lax.psum((part_q, part_k), 'seq')  67.2 us
    all_to_all x1, starting transfers between devices, local(): lax.all_to_all(q_norm, 'seq', split_axis=1, concat_axis=0, tiled=True)  60.2 us
    all_to_all x1, blocking collectives, local(): lax.all_to_all(dk_heads, 'seq', split_axis=0, concat_axis=1, tiled=True)  16.7 us
  transfers between devices with their start and end apart: 5, of which 4 were waited for; matrix products, arithmetic and copies ran while one was open for 2% of the time, Pallas kernels for 0%

commit v1 on v0

v1 whole, which is shorter than its diff:
```python
import jax
import jax.numpy as jnp
from jax import lax
from jax.experimental import pallas as pl
from jax.experimental.pallas import tpu as pltpu
from jax.sharding import PartitionSpec as P

H = 24
HD = 128
TOK = 128
N_SEQ = 8
HEADS = H // N_SEQ
G = TOK * N_SEQ
WIDTH = H * HD
BQ = 256
EXTRA = 16
ROWS = 3 * TOK + EXTRA
EPS = 1e-06
SCALE = HD ** (-0.5)
LOG2E = 1.4426950408889634
SHARD = 48


def split3(x):
    hi = x.astype(jnp.bfloat16).astype(jnp.float32)
    mid = (x - hi).astype(jnp.bfloat16).astype(jnp.float32)
    return (hi, mid, x - hi - mid)


def extra_rows(row_a, row_b):
    at = lax.broadcasted_iota(jnp.int32, (EXTRA, HD), 0)
    out = jnp.zeros((EXTRA, HD), jnp.float32)
    for index, piece in enumerate(split3(row_a) + split3(row_b)):
        out = jnp.where(at == index, piece, out)
    return out.astype(jnp.bfloat16)


def join3(extra):
    x = extra.astype(jnp.float32)
    return ((x[0:1] + x[1:2]) + x[2:3], (x[3:4] + x[4:5]) + x[5:6])


def column(row):
    return jnp.transpose(jnp.broadcast_to(row, (HD, HD)))


def pack_kernel(q_ref, k_ref, v_ref, *outs):
    pays, inv_refs = outs[:HEADS], outs[HEADS:]
    rows = []
    for ref, inv_ref in zip((q_ref, k_ref), inv_refs):
        total = jnp.zeros((TOK, HD), jnp.float32)
        for h in range(H):
            x = ref[:, h * HD:(h + 1) * HD].astype(jnp.float32)
            total = total + x * x
        inv = lax.rsqrt(jnp.sum(total, axis=1, keepdims=True) * (1.0 / WIDTH) + EPS)
        inv = jnp.broadcast_to(inv, (TOK, HD))
        inv_ref[...] = inv
        rows.append(jnp.transpose(inv)[0:1])
    extra = extra_rows(rows[0], rows[1])
    for c in range(HEADS):
        for s in range(N_SEQ):
            h = s * HEADS + c
            for n, ref in enumerate((q_ref, k_ref, v_ref)):
                pays[c][s, n * TOK:(n + 1) * TOK] = ref[:, h * HD:(h + 1) * HD]
            pays[c][s, 3 * TOK:] = extra


def nt(a, b):
    return lax.dot_general(a, b, (((1,), (1,)), ((), ())), preferred_element_type=jnp.float32)


def nn(a, b):
    return jnp.dot(a, b, preferred_element_type=jnp.float32)


def attend_kernel(pay_ref, gain_ref, ids_ref, out_ref, dg_ref, qn, kn, vv, dq, acc_k, acc_v):
    gq, gk = gain_ref[0:1], gain_ref[1:2]

    def hats(j):
        iq, ik = join3(pay_ref[j, 3 * TOK:])
        q = pay_ref[j, 0:TOK].astype(jnp.float32) * column(iq)
        k = pay_ref[j, TOK:2 * TOK].astype(jnp.float32) * column(ik)
        return (q, k)

    for j in range(N_SEQ):
        q, k = hats(j)
        at = slice(j * TOK, (j + 1) * TOK)
        qn[at] = (q * gq).astype(jnp.bfloat16)
        kn[at] = (k * gk).astype(jnp.bfloat16)
        vv[at] = pay_ref[j, 2 * TOK:3 * TOK]
    acc_k[...] = jnp.zeros_like(acc_k)
    acc_v[...] = jnp.zeros_like(acc_v)
    ids = ids_ref[...]

    for b in range(G // BQ):
        at = slice(b * BQ, (b + 1) * BQ)
        same = jnp.concatenate(
            [column(ids[:, t:t + HD]) for t in range(b * BQ, (b + 1) * BQ, HD)], axis=0)[:, 0:1] == ids
        qb = qn[at]
        s = jnp.where(same, nt(qb, kn[...]), -1e30)
        top = jnp.max(s, axis=1, keepdims=True)
        e = jnp.exp2((s - top) * (SCALE * LOG2E))
        p = e * (1.0 / jnp.sum(e, axis=1, keepdims=True))
        pb = p.astype(jnp.bfloat16)
        attn = nn(pb, vv[...])
        attn_b = attn.astype(jnp.bfloat16)
        dp = nt(attn_b, vv[...])
        delta = jnp.sum(p * dp, axis=1, keepdims=True)
        ds = (p * (dp - delta) * SCALE).astype(jnp.bfloat16)
        dq[at] = nn(ds, kn[...]).astype(jnp.bfloat16)
        acc_v[...] += nn(jnp.transpose(attn_b), pb)
        acc_k[...] += nn(jnp.transpose(qb), ds)

    sum_q = jnp.zeros((1, HD), jnp.float32)
    sum_k = jnp.zeros((1, HD), jnp.float32)
    extra = extra_rows(gq, gk)
    for j in range(N_SEQ):
        at = slice(j * TOK, (j + 1) * TOK)
        q, k = hats(j)
        one_q = dq[at]
        one_k = jnp.transpose(acc_k[:, at]).astype(jnp.bfloat16)
        sum_q = sum_q + jnp.sum(one_q.astype(jnp.float32) * q, axis=0, keepdims=True)
        sum_k = sum_k + jnp.sum(one_k.astype(jnp.float32) * k, axis=0, keepdims=True)
        out_ref[j, 0:TOK] = one_q
        out_ref[j, TOK:2 * TOK] = one_k
        out_ref[j, 2 * TOK:3 * TOK] = jnp.transpose(acc_v[:, at]).astype(jnp.bfloat16)
        out_ref[j, 3 * TOK:] = extra
    dg_ref[0:1] = sum_q
    dg_ref[1:2] = sum_k


def final_kernel(q_ref, k_ref, inv_q_ref, inv_k_ref, *refs):
    pays, (dq_ref, dk_ref, dv_ref) = refs[:HEADS], refs[HEADS:]
    pairs = [(s, c, s * HEADS + c) for s in range(N_SEQ) for c in range(HEADS)]
    for n, (ref, inv_ref, out_ref) in enumerate(
            ((q_ref, inv_q_ref, dq_ref), (k_ref, inv_k_ref, dk_ref))):
        inv = inv_ref[...]

        def parts(s, c, h):
            gain = join3(pays[c][s, 3 * TOK:])[n]
            dhat = pays[c][s, n * TOK:(n + 1) * TOK].astype(jnp.float32) * gain
            return (dhat, ref[:, h * HD:(h + 1) * HD].astype(jnp.float32) * inv)

        total = jnp.zeros((TOK, HD), jnp.float32)
        for s, c, h in pairs:
            dhat, hat = parts(s, c, h)
            total = total + dhat * hat
        mean = jnp.sum(total, axis=1, keepdims=True) * (1.0 / WIDTH)
        for s, c, h in pairs:
            dhat, hat = parts(s, c, h)
            out_ref[:, h * HD:(h + 1) * HD] = (inv * (dhat - hat * mean)).astype(jnp.bfloat16)
    for s, c, h in pairs:
        dv_ref[:, h * HD:(h + 1) * HD] = pays[c][s, 2 * TOK:3 * TOK]


def shape(dims, dtype=jnp.bfloat16):
    return jax.ShapeDtypeStruct(dims, dtype)


PARAMS = pltpu.CompilerParams(vmem_limit_bytes=48 * 1024 * 1024)


def local(q_in, k_in, v_in, gain_q, gain_k, clip_ids):
    n_dp = lax.axis_size("dp")
    blocks = [list(range(b, b + N_SEQ)) for b in range(0, n_dp, N_SEQ)]
    swap = [((b * 8 + i) * 8 + s, (s * 8 + i) * 8 + b) for b in range(8) for i in range(8) for s in range(8)]

    gain = lax.ppermute(jnp.stack([gain_q, gain_k]), ("dp", "seq"), swap)
    gain = lax.all_to_all(jnp.broadcast_to(gain, (N_SEQ, 2, SHARD)), "dp", 0, 0,
                          axis_index_groups=blocks, tiled=True)
    gain = jnp.transpose(gain, (1, 0, 2)).reshape(2, HEADS * HD)

    pay = shape((N_SEQ, ROWS, HD))
    inv = shape((TOK, HD), jnp.float32)
    *pays, inv_q, inv_k = pl.pallas_call(
        pack_kernel, out_shape=[pay] * HEADS + [inv] * 2, compiler_params=PARAMS, name="pack",
    )(q_in, k_in, v_in)

    backs, sums = [], []
    for c in range(HEADS):
        got = lax.all_to_all(pays[c], "seq", 0, 0, tiled=True)
        back, dg = pl.pallas_call(
            attend_kernel,
            out_shape=[pay, shape((2, HD), jnp.float32)],
            scratch_shapes=[pltpu.VMEM((G, HD), jnp.bfloat16)] * 4 + [pltpu.VMEM((HD, G), jnp.float32)] * 2,
            compiler_params=PARAMS, name="attend",
            cost_estimate=pl.CostEstimate(flops=12 * G * G * HD, bytes_accessed=1600000, transcendentals=G * G),
        )(got, gain[:, c * HD:(c + 1) * HD], clip_ids)
        backs.append(lax.all_to_all(back, "seq", 0, 0, tiled=True))
        sums.append(dg)

    part = jnp.transpose(jnp.concatenate(sums, axis=1).reshape(2, N_SEQ, SHARD), (1, 0, 2))
    part = jnp.sum(lax.all_to_all(part, "dp", 0, 0, axis_index_groups=blocks, tiled=True), axis=0)
    part = lax.ppermute(part, ("dp", "seq"), swap)
    part = jnp.sum(lax.all_to_all(jnp.broadcast_to(part, (N_SEQ, 2, SHARD)), "seq", 0, 0, tiled=True), axis=0)

    out = shape((TOK, WIDTH))
    d_q, d_k, d_v = pl.pallas_call(
        final_kernel, out_shape=[out] * 3, compiler_params=PARAMS, name="final",
    )(q_in, k_in, inv_q, inv_k, *backs)
    return (d_q, d_k, d_v, part[0], part[1])


def solution(mesh):
    rows = P(("dp", "seq"), None)
    return jax.shard_map(
        local, mesh=mesh,
        in_specs=(rows, rows, rows, P("dp"), P("dp"), P("dp", None)),
        out_specs=(rows, rows, rows, P("dp"), P("dp")), check_vma=False)
```

time: 754 us -> 179 us (0.24)
  blocking collectives: 535 us -> 107 us
  starting transfers between devices: 79 us -> 24.8 us
  local copies, waits for them, and re-layouts: 39.7 us -> 8.05 us
  waiting for transfers between devices: 45.1 us -> 14.8 us
  other arithmetic: 23.9 us -> 0.05 us
  matrix products: 23.4 us -> 0 us
  Pallas kernels: 0 us -> 22.4 us
    unnamed x2 -> x0, blocking collectives: 451 us -> none
    all_to_all x1 -> x6, blocking collectives: 16.7 us -> 107 us  [the longest x2 45.1 us: local(): got = lax.all_to_all(pays[c], 'seq', 0, 0, tiled=True)]
    psum x1 -> x0, blocking collectives: 67.2 us -> none  [local(): whole_q, whole_k = lax.psum((part_q, part_k), 'seq')]
    all_to_all x5 -> x3, starting transfers between devices: 79 us -> 13.7 us  [the longest x1 5.54 us: local(): lax.all_to_all(jnp.broadcast_to(gain, (N_SEQ, 2, SHARD)), 'dp', 0, 0, axi...]
    all_to_all x5 -> x3, waiting for transfers between devices: 45.1 us -> 12.3 us  [the longest x1 12.1 us: local(): backs.append(lax.all_to_all(back, 'seq', 0, 0, tiled=True))]
    dot_general x36 -> x0, matrix products: 23.4 us -> none  [the longest x6 6.55 us: step(): jnp.dot(dscore, k_one, preferred_element_type=jnp.float32)]
    pallas_call x0 -> x5, Pallas kernels: none -> 22.4 us  [the longest x3 17.7 us: local(): pl.pallas_call(attend_kernel, out_shape=[pay, shape((2, HD), jnp.float32)...]
    ppermute x0 -> x2, starting transfers between devices: none -> 11.1 us  [the longest x1 6.28 us: local(): gain = lax.ppermute(jnp.stack([gain_q, gain_k]), ('dp', 'seq'), swap)]
  transfers between devices with their start and end apart: 5 -> 5, of which waited for: 4 -> 4; matrix products, arithmetic and copies ran while one was open for 2% -> 0% of each run, Pallas kernels for 0% -> 7%
where the time goes in v1:
time: 179 us; the launch traced here: 178 us
  blocking collectives  107 us (60%)
  starting transfers between devices  24.8 us (14%)
  Pallas kernels  22.4 us (13%)
  waiting for transfers between devices  14.8 us (8%)
  local copies, waits for them, and re-layouts  8.05 us (4%)
    all_to_all x2, blocking collectives, local(): got = lax.all_to_all(pays[c], 'seq', 0, 0, tiled=True)  45.1 us
    all_to_all x2, blocking collectives, local(): backs.append(lax.all_to_all(back, 'seq', 0, 0, tiled=True))  32.1 us
    all_to_all x1, blocking collectives, local(): lax.all_to_all(jnp.broadcast_to(part, (N_SEQ, 2, SHARD)), 'seq', 0, 0, ti...  21 us
    pallas_call x3, Pallas kernels, local(): pl.pallas_call(attend_kernel, out_shape=[pay, shape((2, HD), jnp.float32)...  17.7 us
    all_to_all x1, waiting for transfers between devices, local(): backs.append(lax.all_to_all(back, 'seq', 0, 0, tiled=True))  12.1 us
    all_to_all x1, blocking collectives, local(): lax.all_to_all(part, 'dp', 0, 0, axis_index_groups=blocks, tiled=True)  9.1 us
    unnamed x18, local copies, waits for them, and re-layouts  6.75 us
    ppermute x1, starting transfers between devices, local(): gain = lax.ppermute(jnp.stack([gain_q, gain_k]), ('dp', 'seq'), swap)  6.28 us
  transfers between devices with their start and end apart: 5, of which 4 were waited for; matrix products, arithmetic and copies ran while one was open for 0% of the time, Pallas kernels for 7%

profile of v1, /device:TPU:1, one launch (start us, length us, event | category | flops | bytes accessed | tf_op | source)
XLA Modules:
  0.0 178.0 jit_solution(13572004633421068146)
XLA Ops:
  0.6 0.0 copy-start.7
  0.6 0.0 copy-start.8
  0.7 0.6 copy-done.7
  1.3 0.0 copy-done.8
  1.3 6.3 %collective-permute-start = (f32[2,48]{1,0:T(2,128)S(1)}, f32[2,48]{1,0:T(2,128)S(1)}, u32[]{:S(2)}, u32[]{:S(2)}) collective-permute-start(f32[2,48]{1,0:T(2,128)S(1)} %pad_maximum_fusion.1), channel_id=1, source_target_pairs={{0,0},{1,64},{2,128},{3,192},{4,256},{5,320},{6,384},{7,448},{8,8}... | collective-permute-start | bytes 1160 | tf_op jit(solution)/shard_map/ppermute | solution.py:168
  7.6 1.2 collective-permute-done
  8.8 0.6 broadcast_in_dim.6
  9.4 5.5 %all-to-all-start.1 = ((f32[8,2,48]{2,1,0:T(2,128)}), f32[8,2,48]{2,1,0:T(2,128)S(1)}, u32[]{:S(2)}, u32[]{:S(2)}) async-start(f32[8,2,48]{2,1,0:T(2,128)} %broadcast_in_dim.6), calls=%async_computation.1 | async-start | bytes 16384 | tf_op jit(solution)/shard_map/all_to_all | solution.py:169
  15.0 0.0 copy-start
  15.0 1.1 copy-done
  16.1 0.0 copy-start.2
  16.1 1.1 copy-done.2
  17.3 0.0 copy-start.5
  17.3 1.1 copy-done.5
  18.4 1.6 pack.1
  20.0 0.0 all-to-all-done.1
  20.0 29.1 %all_to_all.45.pay_ref = bf16[8,400,128]{2,1,0:T(8,128)(2,1)S(1)} all-to-all(bf16[8,400,128]{2,1,0:T(8,128)(2,1)S(1)} %get-tuple-element.21), channel_id=1, replica_groups=mesh['dp'=64,'seq'=8] {'seq'}, dimensions={0} | all-to-all | bytes 1638400 | tf_op jit(solution)/shard_map/all_to_all | solution.py:181
  49.1 16.0 %all_to_all.46.pay_ref = bf16[8,400,128]{2,1,0:T(8,128)(2,1)S(1)} all-to-all(bf16[8,400,128]{2,1,0:T(8,128)(2,1)S(1)} %get-tuple-element.23), channel_id=1, replica_groups=mesh['dp'=64,'seq'=8] {'seq'}, dimensions={0} | all-to-all | bytes 1638400 | tf_op jit(solution)/shard_map/all_to_all | solution.py:181
  65.1 4.0 %all-to-all-start.5 = ((bf16[8,400,128]{2,1,0:T(8,128)(2,1)}), bf16[8,400,128]{2,1,0:T(8,128)(2,1)S(1)}, u32[]{:S(2)}, u32[]{:S(2)}) async-start(bf16[8,400,128]{2,1,0:T(8,128)(2,1)} %get-tuple-element.25), calls=%async_computation.5 | async-start | bytes 1638400 | tf_op jit(solution)/shard_map/all_to_all | solution.py:181
  69.1 0.1 reshape.16
  69.2 0.0 copy-start.6
  69.2 0.7 copy-done.6
  69.9 5.8 %attend.3 = (bf16[8,400,128]{2,1,0:T(8,128)(2,1)S(1)}, f32[2,128]{1,0:T(2,128)S(1)}) custom-call(bf16[8,400,128]{2,1,0:T(8,128)(2,1)S(1)} %all_to_all.45.pay_ref, f32[2,128]{1,0:T(2,128)S(1)} %get-tuple-element.35.gain_ref, s32[1,1024]{1,0:T(1,128)S(1)} %copy-done.6), custom_call_target="tpu_custom_call" | custom-call | flops 1610612736 | bytes 1600000 | tf_op jit(solution)/shard_map/attend/pallas_call | solution.py:182
  75.7 5.8 %attend.4 = (bf16[8,400,128]{2,1,0:T(8,128)(2,1)S(1)}, f32[2,128]{1,0:T(2,128)S(1)}) custom-call(bf16[8,400,128]{2,1,0:T(8,128)(2,1)S(1)} %all_to_all.46.pay_ref, f32[2,128]{1,0:T(2,128)S(1)} %get-tuple-element.34.gain_ref, s32[1,1024]{1,0:T(1,128)S(1)} %copy-done.6), custom_call_target="tpu_custom_call" | custom-call | flops 1610612736 | bytes 1600000 | tf_op jit(solution)/shard_map/attend/pallas_call | solution.py:182
  81.6 0.2 all-to-all-done.5.pay_ref
  81.8 6.0 %attend.5 = (bf16[8,400,128]{2,1,0:T(8,128)(2,1)S(1)}, f32[2,128]{1,0:T(2,128)S(1)}) custom-call(bf16[8,400,128]{2,1,0:T(8,128)(2,1)S(1)} %all-to-all-done.5.pay_ref, f32[2,128]{1,0:T(2,128)S(1)} %get-tuple-element.33.gain_ref, s32[1,1024]{1,0:T(1,128)S(1)} %copy-done.6), custom_call_target="tpu_custom_call" | custom-call | flops 1610612736 | bytes 1600000 | tf_op jit(solution)/shard_map/attend/pallas_call | solution.py:182
  87.8 0.0 copy-start.4
  87.8 0.9 copy-done.4
  88.7 0.1 reshape.17
  88.8 9.1 %all_to_all.47 = f32[8,2,48]{2,1,0:T(2,128)S(1)} all-to-all(f32[8,2,48]{2,1,0:T(2,128)S(1)} %bitcast.11), channel_id=1, replica_groups={{0,8,16,24,32,40,48,56},{64,72,80,88,96,104,112,120},{128,136,144,152,1..., dimensions={0} | all-to-all | bytes 6144 | tf_op jit(solution)/shard_map/all_to_all | solution.py:193
  97.9 4.8 %collective-permute-start.1 = (f32[2,48]{1,0:T(2,128)S(1)}, f32[2,48]{1,0:T(2,128)S(1)}, u32[]{:S(2)}, u32[]{:S(2)}) collective-permute-start(f32[2,48]{1,0:T(2,128)S(1)} %reduce_sum.18), channel_id=1, source_target_pairs={{0,0},{1,64},{2,128},{3,192},{4,256},{5,320},{6,384},{7,448},{8,8}... | collective-permute-start | bytes 1160 | tf_op jit(solution)/shard_map/ppermute | solution.py:194
  102.7 1.2 collective-permute-done.1
  104.0 21.0 %all_to_all.48 = f32[8,2,48]{2,1,0:T(2,128)S(1)} all-to-all(f32[8,2,48]{2,1,0:T(2,128)S(1)} %broadcast_in_dim.7), channel_id=1, replica_groups=mesh['dp'=64,'seq'=8] {'seq'}, dimensions={0} | all-to-all | bytes 6144 | tf_op jit(solution)/shard_map/all_to_all | solution.py:195
  125.0 16.1 %all_to_all.49.refs_0_ = bf16[8,400,128]{2,1,0:T(8,128)(2,1)S(1)} all-to-all(bf16[8,400,128]{2,1,0:T(8,128)(2,1)S(1)} %get-tuple-element.22), channel_id=1, replica_groups=mesh['dp'=64,'seq'=8] {'seq'}, dimensions={0} | all-to-all | bytes 1638400 | tf_op jit(solution)/shard_map/all_to_all | solution.py:189
  141.1 16.0 %all_to_all.50.refs_1_ = bf16[8,400,128]{2,1,0:T(8,128)(2,1)S(1)} all-to-all(bf16[8,400,128]{2,1,0:T(8,128)(2,1)S(1)} %get-tuple-element.24), channel_id=1, replica_groups=mesh['dp'=64,'seq'=8] {'seq'}, dimensions={0} | all-to-all | bytes 1638400 | tf_op jit(solution)/shard_map/all_to_all | solution.py:189
  157.0 0.0 copy-start.1
  157.0 4.2 %all-to-all-start.6 = ((bf16[8,400,128]{2,1,0:T(8,128)(2,1)}), bf16[8,400,128]{2,1,0:T(8,128)(2,1)S(1)}, u32[]{:S(2)}, u32[]{:S(2)}) async-start(bf16[8,400,128]{2,1,0:T(8,128)(2,1)} %copy-done.4), calls=%async_computation.6 | async-start | bytes 1638400 | tf_op jit(solution)/shard_map/all_to_all | solution.py:189
  161.2 0.5 slice_bitcast_fusion
  161.7 12.1 %all-to-all-done.6.refs_2_ = bf16[8,400,128]{2,1,0:T(8,128)(2,1)S(1)} async-done(((bf16[8,400,128]{2,1,0:T(8,128)(2,1)}), bf16[8,400,128]{2,1,0:T(8,128)(2,1)S(1)}, u32[]{:S(2)}, u32[]{:S(2)}) %all-to-all-start.6) | async-done | bytes 819232 | tf_op jit(solution)/shard_map/all_to_all | solution.py:189
  173.9 0.0 copy-done.1
  173.9 0.0 copy-start.3
  173.9 1.1 copy-done.3
  175.0 3.0 %final.1 = (bf16[128,3072]{1,0:T(8,128)(2,1)}, bf16[128,3072]{1,0:T(8,128)(2,1)}, bf16[128,3072]{1,0:T(8,128)(2,1)}) custom-call(bf16[128,3072]{1,0:T(8,128)(2,1)S(1)} %copy-done.1, bf16[128,3072]{1,0:T(8,128)(2,1)S(1)} %copy-done.3, f32[128,128]{1,0:T(8,128)S(1)} %get-tuple-element.19.inv_q_ref, f32[128,128]{1,0:T(8,128)S(1)} %get-tuple-element.20.inv_k_ref, ...), custom_call_target="tpu_custom_call" | custom-call | tf_op jit(solution)/shard_map/final/pallas_call | solution.py:198
  (8 shorter events, 0.1 us)
Async XLA Ops:
  0.6 0.7 copy-start.7
  0.6 0.7 copy-start.8
  1.3 7.5 %collective-permute-start = (f32[2,48]{1,0:T(2,128)S(1)}, f32[2,48]{1,0:T(2,128)S(1)}, u32[]{:S(2)}, u32[]{:S(2)}) collective-permute-start(f32[2,48]{1,0:T(2,128)S(1)} %pad_maximum_fusion.1), channel_id=1, source_target_pairs={{0,0},{1,64},{2,128},{3,192},{4,256},{5,320},{6,384},{7,448},{8,8}... | collective-permute-start | bytes 1160 | tf_op jit(solution)/shard_map/ppermute | solution.py:168
  9.4 10.6 %all-to-all-start.1 = ((f32[8,2,48]{2,1,0:T(2,128)}), f32[8,2,48]{2,1,0:T(2,128)S(1)}, u32[]{:S(2)}, u32[]{:S(2)}) async-start(f32[8,2,48]{2,1,0:T(2,128)} %broadcast_in_dim.6), calls=%async_computation.1 | async-start | bytes 16384 | tf_op jit(solution)/shard_map/all_to_all | solution.py:169
  15.0 1.1 copy-start
  16.1 1.1 copy-start.2
  17.3 1.1 copy-start.5
  65.1 16.7 %all-to-all-start.5 = ((bf16[8,400,128]{2,1,0:T(8,128)(2,1)}), bf16[8,400,128]{2,1,0:T(8,128)(2,1)S(1)}, u32[]{:S(2)}, u32[]{:S(2)}) async-start(bf16[8,400,128]{2,1,0:T(8,128)(2,1)} %get-tuple-element.25), calls=%async_computation.5 | async-start | bytes 1638400 | tf_op jit(solution)/shard_map/all_to_all | solution.py:181
  69.2 0.7 copy-start.6
  87.8 0.9 copy-start.4
  97.9 6.1 %collective-permute-start.1 = (f32[2,48]{1,0:T(2,128)S(1)}, f32[2,48]{1,0:T(2,128)S(1)}, u32[]{:S(2)}, u32[]{:S(2)}) collective-permute-start(f32[2,48]{1,0:T(2,128)S(1)} %reduce_sum.18), channel_id=1, source_target_pairs={{0,0},{1,64},{2,128},{3,192},{4,256},{5,320},{6,384},{7,448},{8,8}... | collective-permute-start | bytes 1160 | tf_op jit(solution)/shard_map/ppermute | solution.py:194
  157.0 16.8 %copy-start.1 = (bf16[128,3072]{1,0:T(8,128)(2,1)S(1)}, bf16[128,3072]{1,0:T(8,128)(2,1)}, u32[]{:S(2)}) copy-start(bf16[128,3072]{1,0:T(8,128)(2,1)} %q_ref.3) | copy-start | bytes 2359300
  157.0 16.8 %all-to-all-start.6 = ((bf16[8,400,128]{2,1,0:T(8,128)(2,1)}), bf16[8,400,128]{2,1,0:T(8,128)(2,1)S(1)}, u32[]{:S(2)}, u32[]{:S(2)}) async-start(bf16[8,400,128]{2,1,0:T(8,128)(2,1)} %copy-done.4), calls=%async_computation.6 | async-start | bytes 1638400 | tf_op jit(solution)/shard_map/all_to_all | solution.py:189
  173.9 1.1 copy-start.3

commit v2 on v1

v2 whole, which is shorter than its diff:
```python
import jax
import jax.numpy as jnp
from jax import lax
from jax.experimental import pallas as pl
from jax.experimental.pallas import tpu as pltpu
from jax.sharding import PartitionSpec as P

H = 24
HD = 128
TOK = 128
N_SEQ = 8
HEADS = H // N_SEQ
G = TOK * N_SEQ
WIDTH = H * HD
BQ = 256
WINDOWS = (512, 640, 768, 1024)
EXTRA = 16
BODY = 3 * TOK * HEADS
EPS = 1e-06
SCALE = HD ** (-0.5)
LOG2E = 1.4426950408889634
SHARD = 48


def split3(x):
    hi = x.astype(jnp.bfloat16).astype(jnp.float32)
    mid = (x - hi).astype(jnp.bfloat16).astype(jnp.float32)
    return (hi, mid, x - hi - mid)


def extra_rows(rows, size):
    at = lax.broadcasted_iota(jnp.int32, (size, HD), 0)
    out = jnp.zeros((size, HD), jnp.float32)
    for index, piece in enumerate([piece for row in rows for piece in split3(row)]):
        out = jnp.where(at == index, piece, out)
    return out.astype(jnp.bfloat16)


def join3(extra, n):
    x = extra[3 * n:3 * n + 3]
    return (x[0:1] + x[1:2]) + x[2:3]


def column(row):
    return jnp.transpose(jnp.broadcast_to(row, (HD, HD)))


def body(c, n):
    return slice((c * 3 + n) * TOK, (c * 3 + n + 1) * TOK)


def pack_kernel(q_ref, k_ref, v_ref, pay_ref, inv_q_ref, inv_k_ref, mark_ref, held, extra, sems):
    loads = []
    for n, ref in enumerate((q_ref, k_ref)):
        loads.append(pltpu.make_async_copy(ref, held.at[n], sems.at[n]))
        loads[n].start()
    copies = []
    for s in range(N_SEQ):
        for c in range(HEADS):
            h = s * HEADS + c
            for n, ref in enumerate((q_ref, k_ref, v_ref)):
                copies.append(pltpu.make_async_copy(
                    ref.at[:, h * HD:(h + 1) * HD], pay_ref.at[s, body(c, n)], sems.at[2 + len(copies)]))
                copies[-1].start()
    rows = []
    for n, inv_ref in enumerate((inv_q_ref, inv_k_ref)):
        loads[n].wait()
        total = jnp.zeros((TOK, HD), jnp.float32)
        for h in range(H):
            x = held[n, :, h * HD:(h + 1) * HD].astype(jnp.float32)
            total = total + x * x
        inv = lax.rsqrt(jnp.sum(total, axis=1, keepdims=True) * (1.0 / WIDTH) + EPS)
        inv = jnp.broadcast_to(inv, (TOK, HD))
        inv_ref[...] = inv
        rows.append(jnp.transpose(inv)[0:1])
    mark_ref[...] = jnp.zeros_like(mark_ref)
    extra[...] = extra_rows(rows, EXTRA)
    for s in range(N_SEQ):
        copies.append(pltpu.make_async_copy(extra, pay_ref.at[s, BODY:], sems.at[2 + len(copies)]))
        copies[-1].start()
    for copy in copies:
        copy.wait()


def nt(a, b):
    return lax.dot_general(a, b, (((1,), (1,)), ((), ())), preferred_element_type=jnp.float32)


def nn(a, b):
    return jnp.dot(a, b, preferred_element_type=jnp.float32)


def attend_kernel(lo_ref, hi_ref, pay_ref, gain_ref, ids_ref, out_ref, dg_ref,
                  qn, kn, vv, dq, acc_k, acc_v, mq, mk, outs, sems):
    for j in range(N_SEQ):
        extra = pay_ref[j, BODY:].astype(jnp.float32)
        at = slice(j * TOK, (j + 1) * TOK)
        mq[at] = column(join3(extra, 0))
        mk[at] = column(join3(extra, 1))
    gains = [[gain_ref[n:n + 1, c * HD:(c + 1) * HD] for n in range(2)] for c in range(HEADS)]
    extra = extra_rows([row for pair in gains for row in pair], 2 * EXTRA)
    for j in range(N_SEQ):
        outs[j, BODY:] = extra

    def hats(c, j):
        at = slice(j * TOK, (j + 1) * TOK)
        return (pay_ref[j, body(c, 0)].astype(jnp.float32) * mq[at],
                pay_ref[j, body(c, 1)].astype(jnp.float32) * mk[at])

    for c in range(HEADS):
        for j in range(N_SEQ):
            q, k = hats(c, j)
            at = slice(j * TOK, (j + 1) * TOK)
            qn[c, at] = (q * gains[c][0]).astype(jnp.bfloat16)
            kn[c, at] = (k * gains[c][1]).astype(jnp.bfloat16)
            vv[c, at] = pay_ref[j, body(c, 2)]
    acc_k[...] = jnp.zeros_like(acc_k)
    acc_v[...] = jnp.zeros_like(acc_v)

    def block(b, first, width):
        first = pl.multiple_of(first, TOK)
        rows = pl.ds(pl.multiple_of(b * BQ, BQ), BQ)
        keys = pl.ds(first, width)
        own = [column(ids_ref[:, pl.ds(pl.multiple_of(b * BQ + t, HD), HD)])[:, 0:1] for t in range(0, BQ, HD)]
        same = jnp.concatenate(own, axis=0) == ids_ref[:, keys]
        for c in range(HEADS):
            qb, kb, vb = qn[c, rows], kn[c, keys], vv[c, keys]
            s = jnp.where(same, nt(qb, kb), -1e30)
            top = jnp.max(s, axis=1, keepdims=True)
            e = jnp.exp2((s - top) * (SCALE * LOG2E))
            p = e * (1.0 / jnp.sum(e, axis=1, keepdims=True))
            pb = p.astype(jnp.bfloat16)
            attn = nn(pb, vb).astype(jnp.bfloat16)
            dp = nt(attn, vb)
            delta = jnp.sum(p * dp, axis=1, keepdims=True)
            ds = (p * (dp - delta) * SCALE).astype(jnp.bfloat16)
            dq[c, rows] = nn(ds, kb).astype(jnp.bfloat16)
            acc_v[c, :, keys] += nn(jnp.transpose(attn), pb)
            acc_k[c, :, keys] += nn(jnp.transpose(qb), ds)

    def step(b, carry):
        low = lo_ref[b] // TOK * TOK
        span = hi_ref[b] - low
        done = None
        for width in WINDOWS:
            fits = span <= width
            now = fits if done is None else jnp.logical_and(fits, jnp.logical_not(done))
            done = fits

            @pl.when(now)
            def _():
                block(b, jnp.minimum(low, G - width), width)
        return carry

    lax.fori_loop(0, G // BQ, step, 0)

    copies = []
    for j in range(N_SEQ):
        at = slice(j * TOK, (j + 1) * TOK)
        for c in range(HEADS):
            outs[j, body(c, 0)] = dq[c, at]
            outs[j, body(c, 1)] = jnp.transpose(acc_k[c, :, at]).astype(jnp.bfloat16)
            outs[j, body(c, 2)] = jnp.transpose(acc_v[c, :, at]).astype(jnp.bfloat16)
        copies.append(pltpu.make_async_copy(outs.at[j], out_ref.at[j], sems.at[j]))
        copies[j].start()
    for c in range(HEADS):
        sums = [jnp.zeros((1, HD), jnp.float32)] * 2
        for j in range(N_SEQ):
            hat = hats(c, j)
            sums = [sums[n] + jnp.sum(outs[j, body(c, n)].astype(jnp.float32) * hat[n], axis=0, keepdims=True)
                    for n in range(2)]
        for n in range(2):
            dg_ref[n:n + 1, c * HD:(c + 1) * HD] = sums[n]
    for copy in copies:
        copy.wait()


def final_kernel(q_ref, k_ref, inv_q_ref, inv_k_ref, pay_ref, dq_ref, dk_ref, dv_ref):
    pairs = [(s, c, slice((s * HEADS + c) * HD, (s * HEADS + c + 1) * HD))
             for s in range(N_SEQ) for c in range(HEADS)]
    extras = [pay_ref[s, BODY:].astype(jnp.float32) for s in range(N_SEQ)]
    for n, (ref, inv_ref, out_ref) in enumerate(
            ((q_ref, inv_q_ref, dq_ref), (k_ref, inv_k_ref, dk_ref))):
        inv = inv_ref[...]

        def parts(s, c, cols):
            dhat = pay_ref[s, body(c, n)].astype(jnp.float32) * join3(extras[s], 2 * c + n)
            return (dhat, ref[:, cols].astype(jnp.float32) * inv)

        total = jnp.zeros((TOK, HD), jnp.float32)
        for pair in pairs:
            dhat, hat = parts(*pair)
            total = total + dhat * hat
        mean = jnp.sum(total, axis=1, keepdims=True) * (1.0 / WIDTH)
        for pair in pairs:
            dhat, hat = parts(*pair)
            out_ref[:, pair[2]] = (inv * (dhat - hat * mean)).astype(jnp.bfloat16)
    for s, c, cols in pairs:
        dv_ref[:, cols] = pay_ref[s, body(c, 2)]


def hold_kernel(x_ref, after_ref, out_ref):
    out_ref[...] = x_ref[...]


def hold(x, after):
    return pl.pallas_call(
        hold_kernel, out_shape=shape(x.shape, jnp.float32),
        in_specs=[pl.BlockSpec(memory_space=pltpu.VMEM), pl.BlockSpec(memory_space=pl.ANY)],
        name="hold", cost_estimate=pl.CostEstimate(flops=1 << 36, bytes_accessed=1 << 27, transcendentals=0),
    )(x, after)


def shape(dims, dtype=jnp.bfloat16):
    return jax.ShapeDtypeStruct(dims, dtype)


PARAMS = pltpu.CompilerParams(vmem_limit_bytes=48 * 1024 * 1024)


def swapped():
    return [((b * 8 + i) * 8 + s, (s * 8 + i) * 8 + b) for b in range(8) for i in range(8) for s in range(8)]


def sum_four(x, axis, pairs):
    one, two, three = (lax.ppermute(x, axis, pairs(k)) for k in (1, 2, 3))
    return (x + two) + (one + three)


def over_z(x):
    return x + lax.ppermute(x, "dp", [(d, d ^ 4) for d in range(64)])


def over_y(x):
    return sum_four(x, "dp", lambda k: [(d, d // 4 * 4 + (d + k) % 4) for d in range(64)])


def over_core(x):
    return x + lax.ppermute(x, "seq", [(s, s ^ 1) for s in range(8)])


def over_x(x):
    return sum_four(x, "seq", lambda k: [(s, (s + 2 * k) % 8) for s in range(8)])


def spread(pair):
    pad = jnp.zeros(pair.shape[:-2] + (16,), jnp.float32)
    return jnp.concatenate([pair[..., 0, :], pad, pair[..., 1, :], pad], axis=-1)


def windows(ids):
    first = ids[:, 0::BQ]
    last = ids[:, BQ - 1::BQ]
    lo = jnp.sum((ids[0][:, None] < first).astype(jnp.int32), axis=0)
    hi = jnp.sum((ids[0][:, None] <= last).astype(jnp.int32), axis=0)
    return (lo, hi)


def local(q_in, k_in, v_in, gain_q, gain_k, clip_ids):
    place = lax.axis_index("dp") % 8
    sent = shape((N_SEQ, BODY + EXTRA, HD))
    back = shape((N_SEQ, BODY + 2 * EXTRA, HD))
    inv = shape((TOK, HD), jnp.float32)
    here = pl.BlockSpec(memory_space=pltpu.VMEM)
    there = pl.BlockSpec(memory_space=pl.ANY)

    row = spread(jnp.stack([gain_q, gain_k]))[None]
    rows = jnp.where(lax.broadcasted_iota(jnp.int32, (8, HD), 0) == place, row, 0.0)
    rows = over_z(rows)

    pay, inv_q, inv_k, mark = pl.pallas_call(
        pack_kernel, out_shape=[sent, inv, inv, shape((8, HD), jnp.float32)],
        in_specs=[there] * 3, out_specs=[there, here, here, here],
        scratch_shapes=[pltpu.VMEM((2, TOK, WIDTH), jnp.bfloat16), pltpu.VMEM((EXTRA, HD), jnp.bfloat16),
                        pltpu.SemaphoreType.DMA((2 + 3 * H + N_SEQ,))],
        compiler_params=PARAMS, name="pack",
    )(q_in, k_in, v_in)
    got = lax.all_to_all(pay, "seq", 0, 0, tiled=True)
    rows = lax.ppermute(over_y(hold(rows, mark)), ("dp", "seq"), swapped())
    gain = jnp.stack([rows[:, 0:SHARD].reshape(-1), rows[:, 64:64 + SHARD].reshape(-1)])
    lo, hi = windows(clip_ids)

    half = pltpu.VMEM((HEADS, G, HD), jnp.bfloat16)
    full = pltpu.VMEM((G, HD), jnp.float32)
    turn = pltpu.VMEM((HEADS, HD, G), jnp.float32)
    few = pl.BlockSpec(memory_space=pltpu.SMEM)
    pay, dg = pl.pallas_call(
        attend_kernel, out_shape=[back, shape((2, HEADS * HD), jnp.float32)],
        in_specs=[few, few, here, here, here], out_specs=[there, here],
        scratch_shapes=[half] * 4 + [turn] * 2 + [full] * 2 + [
            pltpu.VMEM(back.shape, jnp.bfloat16), pltpu.SemaphoreType.DMA((N_SEQ,))],
        compiler_params=PARAMS, name="attend",
    )(lo, hi, got, gain, clip_ids)
    got = lax.all_to_all(pay, "seq", 0, 0, tiled=True)

    part = hold(spread(jnp.transpose(dg.reshape(2, N_SEQ, SHARD), (1, 0, 2))), dg)
    part = lax.ppermute(over_y(over_z(part)), ("dp", "seq"), swapped())
    part = over_x(over_core(part))
    part = lax.dynamic_index_in_dim(part, place, 0, keepdims=False)

    out = shape((TOK, WIDTH))
    d_q, d_k, d_v = pl.pallas_call(
        final_kernel, out_shape=[out] * 3, compiler_params=PARAMS, name="final",
    )(q_in, k_in, inv_q, inv_k, got)
    return (d_q, d_k, d_v, part[0:SHARD], part[64:64 + SHARD])


def solution(mesh):
    rows = P(("dp", "seq"), None)
    return jax.shard_map(
        local, mesh=mesh,
        in_specs=(rows, rows, rows, P("dp"), P("dp"), P("dp", None)),
        out_specs=(rows, rows, rows, P("dp"), P("dp")), check_vma=False)
```

time: 179 us -> 137 us (0.77)
  blocking collectives: 107 us -> 0 us
  starting transfers between devices: 24.8 us -> 75.4 us
  waiting for transfers between devices: 14.8 us -> 19.8 us
  other arithmetic: 0.05 us -> 3.79 us
  Pallas kernels: 22.4 us -> 25.7 us
    all_to_all x6 -> x0, blocking collectives: 107 us -> none  [the longest x2 45.1 us: local(): got = lax.all_to_all(pays[c], 'seq', 0, 0, tiled=True)]
    ppermute x2 -> x14, starting transfers between devices: 11.1 us -> 61.7 us  [the longest x9 43 us: sum_four(): one, two, three = (lax.ppermute(x, axis, pairs(k)) for k in (1, 2, 3))]
    ppermute x2 -> x14, waiting for transfers between devices: 2.49 us -> 10.5 us  [the longest x9 3.51 us: sum_four(): one, two, three = (lax.ppermute(x, axis, pairs(k)) for k in (1, 2, 3))]
    pallas_call x4, Pallas kernels: 19.3 us -> 22.7 us  [the longest x1 17.9 us: local(): pl.pallas_call(attend_kernel, out_shape=[back, shape((2, HEADS * HD), jnp...]
    all_to_all x3 -> x2, waiting for transfers between devices: 12.3 us -> 9.26 us  [local(): got = lax.all_to_all(pay, 'seq', 0, 0, tiled=True)]
    add x0 -> x6, other arithmetic: none -> 2.06 us  [the longest x2 1.35 us: over_z(): return x + lax.ppermute(x, 'dp', [(d, d ^ 4) for d in range(64)])]
    unnamed x18 -> x20, local copies, waits for them, and re-layouts: 6.75 us -> 8.46 us
    all_to_all x3 -> x2, starting transfers between devices: 13.7 us -> 13.8 us  [local(): got = lax.all_to_all(pay, 'seq', 0, 0, tiled=True)]
  transfers between devices with their start and end apart: 5 -> 16, of which waited for: 4 -> 8; matrix products, arithmetic and copies ran while one was open for 0% -> 3% of each run, Pallas kernels for 7% -> 4%
where the time goes in v2:
time: 137 us; the launch traced here: 135 us
  starting transfers between devices  75.4 us (55%)
  Pallas kernels  25.7 us (19%)
  waiting for transfers between devices  19.8 us (14%)
  local copies, waits for them, and re-layouts  9.56 us (7%)
  other arithmetic  3.79 us (3%)
    ppermute x9, starting transfers between devices, sum_four(): one, two, three = (lax.ppermute(x, axis, pairs(k)) for k in (1, 2, 3))  43 us
    pallas_call x1, Pallas kernels, local(): pl.pallas_call(attend_kernel, out_shape=[back, shape((2, HEADS * HD), jnp...  17.9 us
    all_to_all x2, starting transfers between devices, local(): got = lax.all_to_all(pay, 'seq', 0, 0, tiled=True)  13.8 us
    all_to_all x2, waiting for transfers between devices, local(): got = lax.all_to_all(pay, 'seq', 0, 0, tiled=True)  9.26 us
    unnamed x20, local copies, waits for them, and re-layouts  8.46 us
    ppermute x2, starting transfers between devices, over_z(): return x + lax.ppermute(x, 'dp', [(d, d ^ 4) for d in range(64)])  6.27 us
    ppermute x1, starting transfers between devices, local(): rows = lax.ppermute(over_y(hold(rows, mark)), ('dp', 'seq'), swapped())  5.87 us
    ppermute x1, starting transfers between devices, local(): part = lax.ppermute(over_y(over_z(part)), ('dp', 'seq'), swapped())  4.66 us
  transfers between devices with their start and end apart: 16, of which 8 were waited for; matrix products, arithmetic and copies ran while one was open for 3% of the time, Pallas kernels for 4%

profile of v2, /device:TPU:1, one launch (start us, length us, event | category | flops | bytes accessed | tf_op | source)
XLA Modules:
  0.0 135.2 jit_solution(8107667333799041419)
XLA Ops:
  0.7 0.8 pad_maximum_fusion.2
  1.5 4.4 %collective-permute-start = (f32[8,128]{1,0:T(8,128)S(1)}, f32[8,128]{1,0:T(8,128)S(1)}, u32[]{:S(2)}, u32[]{:S(2)}) collective-permute-start(f32[8,128]{1,0:T(8,128)S(1)} %broadcast_select_fusion), channel_id=1, source_target_pairs={{0,32},{8,40},{16,48},{24,56},{32,0},{40,8},{48,16},{56,24},{64,96... | collective-permute-start | bytes 12296 | tf_op jit(solution)/shard_map/ppermute | solution.py:231
  5.9 1.1 copy-done
  7.0 1.1 copy-done.2
  8.1 1.1 copy-done.6
  9.3 2.2 %pack.1 = (bf16[8,1168,128]{2,1,0:T(8,128)(2,1)S(1)}, f32[128,128]{1,0:T(8,128)S(1)}, f32[128,128]{1,0:T(8,128)S(1)}, f32[8,128]{1,0:T(8,128)S(1)}) custom-call(bf16[128,3072]{1,0:T(8,128)(2,1)S(1)} %copy-done, bf16[128,3072]{1,0:T(8,128)(2,1)S(1)} %copy-done.2, bf16[128,3072]{1,0:T(8,128)(2,1)S(1)} %copy-done.6), custom_call_target="tpu_custom_call" | custom-call | tf_op jit(solution)/shard_map/pack/pallas_call | solution.py:271
  11.5 1.4 %copy-done.5 = bf16[8,1168,128]{2,1,0:T(8,128)(2,1)} copy-done((bf16[8,1168,128]{2,1,0:T(8,128)(2,1)}, bf16[8,1168,128]{2,1,0:T(8,128)(2,1)S(1)}, u32[]{:S(2)}) %copy-start.5) | copy-done | bytes 2392088
  12.9 0.6 copy-done.9
  13.5 7.9 %all-to-all-start = ((bf16[8,1168,128]{2,1,0:T(8,128)(2,1)}), bf16[8,1168,128]{2,1,0:T(8,128)(2,1)S(1)}, u32[]{:S(2)}, u32[]{:S(2)}) async-start(bf16[8,1168,128]{2,1,0:T(8,128)(2,1)} %copy-done.5), calls=%async_computation | async-start | bytes 4784128 | tf_op jit(solution)/shard_map/all_to_all | solution.py:278
  21.4 0.7 fusion.x_ref
  22.1 1.3 hold.2
  23.4 2.1 %collective-permute-start.1 = (f32[8,128]{1,0:T(8,128)}, f32[8,128]{1,0:T(8,128)S(1)}, u32[]{:S(2)}, u32[]{:S(2)}) collective-permute-start(f32[8,128]{1,0:T(8,128)} %hold.2), channel_id=1, source_target_pairs={{0,16},{8,24},{16,0},{24,8},{32,48},{40,56},{48,32},{56,40},{64,80... | collective-permute-start | bytes 12296 | tf_op jit(solution)/shard_map/ppermute | solution.py:226
  25.5 2.3 %collective-permute-start.2 = (f32[8,128]{1,0:T(8,128)}, f32[8,128]{1,0:T(8,128)S(1)}, u32[]{:S(2)}, u32[]{:S(2)}) collective-permute-start(f32[8,128]{1,0:T(8,128)} %hold.2), channel_id=1, source_target_pairs={{0,8},{8,16},{16,24},{24,0},{32,40},{40,48},{48,56},{56,32},{64,72... | collective-permute-start | bytes 12296 | tf_op jit(solution)/shard_map/ppermute | solution.py:226
  27.8 4.2 %collective-permute-start.3 = (f32[8,128]{1,0:T(8,128)}, f32[8,128]{1,0:T(8,128)S(1)}, u32[]{:S(2)}, u32[]{:S(2)}) collective-permute-start(f32[8,128]{1,0:T(8,128)} %hold.2), channel_id=1, source_target_pairs={{0,24},{8,0},{16,8},{24,16},{32,56},{40,32},{48,40},{56,48},{64,88... | collective-permute-start | bytes 12296 | tf_op jit(solution)/shard_map/ppermute | solution.py:226
  32.1 0.1 slice.30
  32.1 0.1 slice.31
  32.3 1.1 collective-permute-done.3
  33.3 0.7 add_add_fusion.2
  34.0 5.9 %collective-permute-start.4 = (f32[8,128]{1,0:T(8,128)S(1)}, f32[8,128]{1,0:T(8,128)S(1)}, u32[]{:S(2)}, u32[]{:S(2)}) collective-permute-start(f32[8,128]{1,0:T(8,128)S(1)} %add_add_fusion.2), channel_id=1, source_target_pairs={{0,0},{1,64},{2,128},{3,192},{4,256},{5,320},{6,384},{7,448},{8,8}... | collective-permute-start | bytes 12296 | tf_op jit(solution)/shard_map/ppermute | solution.py:279
  39.9 0.2 convert_reduce_fusion
  40.1 1.4 %collective-permute-done.4 = f32[8,128]{1,0:T(8,128)S(1)} collective-permute-done((f32[8,128]{1,0:T(8,128)S(1)}, f32[8,128]{1,0:T(8,128)S(1)}, u32[]{:S(2)}, u32[]{:S(2)}) %collective-permute-start.4) | collective-permute-done | bytes 4128 | tf_op jit(solution)/shard_map/ppermute | solution.py:279
  41.5 0.1 stack_reshape.6
  41.6 0.1 stack_reshape.7
  41.7 9.3 %all-to-all-done.pay_ref = bf16[8,1168,128]{2,1,0:T(8,128)(2,1)S(1)} async-done(((bf16[8,1168,128]{2,1,0:T(8,128)(2,1)}), bf16[8,1168,128]{2,1,0:T(8,128)(2,1)S(1)}, u32[]{:S(2)}, u32[]{:S(2)}) %all-to-all-start) | async-done | bytes 2392096 | tf_op jit(solution)/shard_map/all_to_all | solution.py:278
  51.0 17.9 %attend.1 = (bf16[8,1184,128]{2,1,0:T(8,128)(2,1)S(1)}, f32[2,384]{1,0:T(2,128)S(1)}) custom-call(s32[4]{0:T(128)S(1)} %get-tuple-element.24.lo_ref, s32[4]{0:T(128)S(1)} %get-tuple-element.23.hi_ref, bf16[8,1168,128]{2,1,0:T(8,128)(2,1)S(1)} %all-to-all-done.pay_ref, f32[2,384]{1,0:T(2,128)S(1)} %pad_maximum_fusion.1.gain_ref, s32[1,1024]{1,0:T(1,128)S(1)} %copy-done.7), custom_call_target="tpu_custom_call" | custom-call | tf_op jit(solution)/shard_map/attend/pallas_call | solution.py:287
  68.9 1.4 %copy-done.4 = bf16[8,1184,128]{2,1,0:T(8,128)(2,1)} copy-done((bf16[8,1184,128]{2,1,0:T(8,128)(2,1)}, bf16[8,1184,128]{2,1,0:T(8,128)(2,1)S(1)}, u32[]{:S(2)}) %copy-start.4) | copy-done | bytes 2424856
  70.4 0.5 copy-done.8
  70.9 5.8 %all-to-all-start.1 = ((bf16[8,1184,128]{2,1,0:T(8,128)(2,1)}), bf16[8,1184,128]{2,1,0:T(8,128)(2,1)S(1)}, u32[]{:S(2)}, u32[]{:S(2)}) async-start(bf16[8,1184,128]{2,1,0:T(8,128)(2,1)} %copy-done.4), calls=%async_computation.1 | async-start | bytes 4849664 | tf_op jit(solution)/shard_map/all_to_all | solution.py:294
  76.7 0.7 pad_maximum_fusion.x_ref
  77.4 1.4 %hold.3 = f32[8,128]{1,0:T(8,128)} custom-call(f32[8,128]{1,0:T(8,128)} %pad_maximum_fusion.x_ref, f32[2,384]{1,0:T(2,128)} %copy-done.8), custom_call_target="tpu_custom_call" | custom-call | flops 68719476736 | bytes 134217728 | tf_op jit(solution)/shard_map/hold/pallas_call | solution.py:207
  78.7 1.9 %collective-permute-start.5 = (f32[8,128]{1,0:T(8,128)}, f32[8,128]{1,0:T(8,128)S(1)}, u32[]{:S(2)}, u32[]{:S(2)}) collective-permute-start(f32[8,128]{1,0:T(8,128)} %hold.3), channel_id=1, source_target_pairs={{0,32},{8,40},{16,48},{24,56},{32,0},{40,8},{48,16},{56,24},{64,96... | collective-permute-start | bytes 12296 | tf_op jit(solution)/shard_map/ppermute | solution.py:231
  80.6 2.9 %collective-permute-done.5 = f32[8,128]{1,0:T(8,128)S(1)} collective-permute-done((f32[8,128]{1,0:T(8,128)}, f32[8,128]{1,0:T(8,128)S(1)}, u32[]{:S(2)}, u32[]{:S(2)}) %collective-permute-start.5) | collective-permute-done | bytes 4128 | tf_op jit(solution)/shard_map/ppermute | solution.py:231
  83.6 0.7 add.49
  84.3 3.9 %collective-permute-start.6 = (f32[8,128]{1,0:T(8,128)S(1)}, f32[8,128]{1,0:T(8,128)S(1)}, u32[]{:S(2)}, u32[]{:S(2)}) collective-permute-start(f32[8,128]{1,0:T(8,128)S(1)} %add.49), channel_id=1, source_target_pairs={{0,16},{8,24},{16,0},{24,8},{32,48},{40,56},{48,32},{56,40},{64,80... | collective-permute-start | bytes 12296 | tf_op jit(solution)/shard_map/ppermute | solution.py:226
  88.2 3.6 %collective-permute-start.7 = (f32[8,128]{1,0:T(8,128)S(1)}, f32[8,128]{1,0:T(8,128)S(1)}, u32[]{:S(2)}, u32[]{:S(2)}) collective-permute-start(f32[8,128]{1,0:T(8,128)S(1)} %add.49), channel_id=1, source_target_pairs={{0,8},{8,16},{16,24},{24,0},{32,40},{40,48},{48,56},{56,32},{64,72... | collective-permute-start | bytes 12296 | tf_op jit(solution)/shard_map/ppermute | solution.py:226
  91.8 2.9 %collective-permute-start.8 = (f32[8,128]{1,0:T(8,128)S(1)}, f32[8,128]{1,0:T(8,128)S(1)}, u32[]{:S(2)}, u32[]{:S(2)}) collective-permute-start(f32[8,128]{1,0:T(8,128)S(1)} %add.49), channel_id=1, source_target_pairs={{0,24},{8,0},{16,8},{24,16},{32,56},{40,32},{48,40},{56,48},{64,88... | collective-permute-start | bytes 12296 | tf_op jit(solution)/shard_map/ppermute | solution.py:226
  94.7 1.7 %collective-permute-done.8 = f32[8,128]{1,0:T(8,128)S(1)} collective-permute-done((f32[8,128]{1,0:T(8,128)S(1)}, f32[8,128]{1,0:T(8,128)S(1)}, u32[]{:S(2)}, u32[]{:S(2)}) %collective-permute-start.8) | collective-permute-done | bytes 4128 | tf_op jit(solution)/shard_map/ppermute | solution.py:226
  96.5 4.7 %collective-permute-start.9 = (f32[8,128]{1,0:T(8,128)S(1)}, f32[8,128]{1,0:T(8,128)S(1)}, u32[]{:S(2)}, u32[]{:S(2)}) collective-permute-start(f32[8,128]{1,0:T(8,128)S(1)} %add_add_fusion.1), channel_id=1, source_target_pairs={{0,0},{1,64},{2,128},{3,192},{4,256},{5,320},{6,384},{7,448},{8,8}... | collective-permute-start | bytes 12296 | tf_op jit(solution)/shard_map/ppermute | solution.py:297
  101.1 1.6 %collective-permute-done.9 = f32[8,128]{1,0:T(8,128)S(1)} collective-permute-done((f32[8,128]{1,0:T(8,128)S(1)}, f32[8,128]{1,0:T(8,128)S(1)}, u32[]{:S(2)}, u32[]{:S(2)}) %collective-permute-start.9) | collective-permute-done | bytes 4128 | tf_op jit(solution)/shard_map/ppermute | solution.py:297
  102.7 1.9 %collective-permute-start.10 = (f32[8,128]{1,0:T(8,128)S(1)}, f32[8,128]{1,0:T(8,128)S(1)}, u32[]{:S(2)}, u32[]{:S(2)}) collective-permute-start(f32[8,128]{1,0:T(8,128)S(1)} %collective-permute-done.9), channel_id=1, source_target_pairs={{0,1},{1,0},{2,3},{3,2},{4,5},{5,4},{6,7},{7,6},{8,9},{9,8},{10,11... | collective-permute-start | bytes 12296 | tf_op jit(solution)/shard_map/ppermute | solution.py:239
  104.6 1.1 collective-permute-done.10
  105.8 17.4 %collective-permute-start.11 = (f32[8,128]{1,0:T(8,128)S(1)}, f32[8,128]{1,0:T(8,128)S(1)}, u32[]{:S(2)}, u32[]{:S(2)}) collective-permute-start(f32[8,128]{1,0:T(8,128)S(1)} %add.53), channel_id=1, source_target_pairs={{0,4},{1,5},{2,6},{3,7},{4,0},{5,1},{6,2},{7,3},{8,12},{9,13},{10,... | collective-permute-start | bytes 12296 | tf_op jit(solution)/shard_map/ppermute | solution.py:226
  123.2 1.9 %collective-permute-start.12 = (f32[8,128]{1,0:T(8,128)S(1)}, f32[8,128]{1,0:T(8,128)S(1)}, u32[]{:S(2)}, u32[]{:S(2)}) collective-permute-start(f32[8,128]{1,0:T(8,128)S(1)} %add.53), channel_id=1, source_target_pairs={{0,2},{1,3},{2,4},{3,5},{4,6},{5,7},{6,0},{7,1},{8,10},{9,11},{10,... | collective-permute-start | bytes 12296 | tf_op jit(solution)/shard_map/ppermute | solution.py:226
  125.1 4.6 %collective-permute-start.13 = (f32[8,128]{1,0:T(8,128)S(1)}, f32[8,128]{1,0:T(8,128)S(1)}, u32[]{:S(2)}, u32[]{:S(2)}) collective-permute-start(f32[8,128]{1,0:T(8,128)S(1)} %add.53), channel_id=1, source_target_pairs={{0,6},{1,7},{2,0},{3,1},{4,2},{5,3},{6,4},{7,5},{8,14},{9,15},{10,... | collective-permute-start | bytes 12296 | tf_op jit(solution)/shard_map/ppermute | solution.py:226
  129.7 0.7 collective-permute-done.13
  130.5 0.6 slice_bitcast_fusion.2
  131.1 1.1 copy-done.3
  132.2 3.0 %final.1 = (bf16[128,3072]{1,0:T(8,128)(2,1)}, bf16[128,3072]{1,0:T(8,128)(2,1)}, bf16[128,3072]{1,0:T(8,128)(2,1)}) custom-call(bf16[128,3072]{1,0:T(8,128)(2,1)S(1)} %copy-done.1, bf16[128,3072]{1,0:T(8,128)(2,1)S(1)} %copy-done.3, f32[128,128]{1,0:T(8,128)S(1)} %get-tuple-element.14.inv_q_ref, f32[128,128]{1,0:T(8,128)S(1)} %get-tuple-element.15.inv_k_ref, ...), custom_call_target="tpu_custom_call" | custom-call | tf_op jit(solution)/shard_map/final/pallas_call | solution.py:302
  (32 shorter events, 0.3 us)
Async XLA Ops:
  1.5 20.0 %collective-permute-start = (f32[8,128]{1,0:T(8,128)S(1)}, f32[8,128]{1,0:T(8,128)S(1)}, u32[]{:S(2)}, u32[]{:S(2)}) collective-permute-start(f32[8,128]{1,0:T(8,128)S(1)} %broadcast_select_fusion), channel_id=1, source_target_pairs={{0,32},{8,40},{16,48},{24,56},{32,0},{40,8},{48,16},{56,24},{64,96... | collective-permute-start | bytes 12296 | tf_op jit(solution)/shard_map/ppermute | solution.py:231
  5.9 1.1 copy-start
  7.0 1.1 copy-start.2
  8.1 1.1 copy-start.6
  11.5 1.4 %copy-start.5 = (bf16[8,1168,128]{2,1,0:T(8,128)(2,1)}, bf16[8,1168,128]{2,1,0:T(8,128)(2,1)S(1)}, u32[]{:S(2)}) copy-start(bf16[8,1168,128]{2,1,0:T(8,128)(2,1)S(1)} %get-tuple-element.16) | copy-start | bytes 7176196
  12.9 0.6 copy-start.9
  13.5 37.5 %all-to-all-start = ((bf16[8,1168,128]{2,1,0:T(8,128)(2,1)}), bf16[8,1168,128]{2,1,0:T(8,128)(2,1)S(1)}, u32[]{:S(2)}, u32[]{:S(2)}) async-start(bf16[8,1168,128]{2,1,0:T(8,128)(2,1)} %copy-done.5), calls=%async_computation | async-start | bytes 4784128 | tf_op jit(solution)/shard_map/all_to_all | solution.py:278
  22.1 9.9 %copy-start.7 = (s32[1,1024]{1,0:T(1,128)S(1)}, s32[1,1024]{1,0:T(1,128)}, u32[]{:S(2)}) copy-start(s32[1,1024]{1,0:T(1,128)} %ids_ref.1) | copy-start | bytes 12292
  23.4 8.8 %collective-permute-start.1 = (f32[8,128]{1,0:T(8,128)}, f32[8,128]{1,0:T(8,128)S(1)}, u32[]{:S(2)}, u32[]{:S(2)}) collective-permute-start(f32[8,128]{1,0:T(8,128)} %hold.2), channel_id=1, source_target_pairs={{0,16},{8,24},{16,0},{24,8},{32,48},{40,56},{48,32},{56,40},{64,80... | collective-permute-start | bytes 12296 | tf_op jit(solution)/shard_map/ppermute | solution.py:226
  25.5 6.7 %collective-permute-start.2 = (f32[8,128]{1,0:T(8,128)}, f32[8,128]{1,0:T(8,128)S(1)}, u32[]{:S(2)}, u32[]{:S(2)}) collective-permute-start(f32[8,128]{1,0:T(8,128)} %hold.2), channel_id=1, source_target_pairs={{0,8},{8,16},{16,24},{24,0},{32,40},{40,48},{48,56},{56,32},{64,72... | collective-permute-start | bytes 12296 | tf_op jit(solution)/shard_map/ppermute | solution.py:226
  27.8 5.5 %collective-permute-start.3 = (f32[8,128]{1,0:T(8,128)}, f32[8,128]{1,0:T(8,128)S(1)}, u32[]{:S(2)}, u32[]{:S(2)}) collective-permute-start(f32[8,128]{1,0:T(8,128)} %hold.2), channel_id=1, source_target_pairs={{0,24},{8,0},{16,8},{24,16},{32,56},{40,32},{48,40},{56,48},{64,88... | collective-permute-start | bytes 12296 | tf_op jit(solution)/shard_map/ppermute | solution.py:226
  34.0 7.4 %collective-permute-start.4 = (f32[8,128]{1,0:T(8,128)S(1)}, f32[8,128]{1,0:T(8,128)S(1)}, u32[]{:S(2)}, u32[]{:S(2)}) collective-permute-start(f32[8,128]{1,0:T(8,128)S(1)} %add_add_fusion.2), channel_id=1, source_target_pairs={{0,0},{1,64},{2,128},{3,192},{4,256},{5,320},{6,384},{7,448},{8,8}... | collective-permute-start | bytes 12296 | tf_op jit(solution)/shard_map/ppermute | solution.py:279
  68.9 1.4 %copy-start.4 = (bf16[8,1184,128]{2,1,0:T(8,128)(2,1)}, bf16[8,1184,128]{2,1,0:T(8,128)(2,1)S(1)}, u32[]{:S(2)}) copy-start(bf16[8,1184,128]{2,1,0:T(8,128)(2,1)S(1)} %get-tuple-element.18) | copy-start | bytes 7274500
  70.3 0.6 copy-start.8
  70.9 60.2 %all-to-all-start.1 = ((bf16[8,1184,128]{2,1,0:T(8,128)(2,1)}), bf16[8,1184,128]{2,1,0:T(8,128)(2,1)S(1)}, u32[]{:S(2)}, u32[]{:S(2)}) async-start(bf16[8,1184,128]{2,1,0:T(8,128)(2,1)} %copy-done.4), calls=%async_computation.1 | async-start | bytes 4849664 | tf_op jit(solution)/shard_map/all_to_all | solution.py:294
  77.4 53.7 %copy-start.1 = (bf16[128,3072]{1,0:T(8,128)(2,1)S(1)}, bf16[128,3072]{1,0:T(8,128)(2,1)}, u32[]{:S(2)}) copy-start(bf16[128,3072]{1,0:T(8,128)(2,1)} %q_ref.3) | copy-start | bytes 2359300
  78.7 4.8 %collective-permute-start.5 = (f32[8,128]{1,0:T(8,128)}, f32[8,128]{1,0:T(8,128)S(1)}, u32[]{:S(2)}, u32[]{:S(2)}) collective-permute-start(f32[8,128]{1,0:T(8,128)} %hold.3), channel_id=1, source_target_pairs={{0,32},{8,40},{16,48},{24,56},{32,0},{40,8},{48,16},{56,24},{64,96... | collective-permute-start | bytes 12296 | tf_op jit(solution)/shard_map/ppermute | solution.py:231
  84.3 10.5 %collective-permute-start.6 = (f32[8,128]{1,0:T(8,128)S(1)}, f32[8,128]{1,0:T(8,128)S(1)}, u32[]{:S(2)}, u32[]{:S(2)}) collective-permute-start(f32[8,128]{1,0:T(8,128)S(1)} %add.49), channel_id=1, source_target_pairs={{0,16},{8,24},{16,0},{24,8},{32,48},{40,56},{48,32},{56,40},{64,80... | collective-permute-start | bytes 12296 | tf_op jit(solution)/shard_map/ppermute | solution.py:226
  88.2 6.5 %collective-permute-start.7 = (f32[8,128]{1,0:T(8,128)S(1)}, f32[8,128]{1,0:T(8,128)S(1)}, u32[]{:S(2)}, u32[]{:S(2)}) collective-permute-start(f32[8,128]{1,0:T(8,128)S(1)} %add.49), channel_id=1, source_target_pairs={{0,8},{8,16},{16,24},{24,0},{32,40},{40,48},{48,56},{56,32},{64,72... | collective-permute-start | bytes 12296 | tf_op jit(solution)/shard_map/ppermute | solution.py:226
  91.8 4.6 %collective-permute-start.8 = (f32[8,128]{1,0:T(8,128)S(1)}, f32[8,128]{1,0:T(8,128)S(1)}, u32[]{:S(2)}, u32[]{:S(2)}) collective-permute-start(f32[8,128]{1,0:T(8,128)S(1)} %add.49), channel_id=1, source_target_pairs={{0,24},{8,0},{16,8},{24,16},{32,56},{40,32},{48,40},{56,48},{64,88... | collective-permute-start | bytes 12296 | tf_op jit(solution)/shard_map/ppermute | solution.py:226
  96.5 6.3 %collective-permute-start.9 = (f32[8,128]{1,0:T(8,128)S(1)}, f32[8,128]{1,0:T(8,128)S(1)}, u32[]{:S(2)}, u32[]{:S(2)}) collective-permute-start(f32[8,128]{1,0:T(8,128)S(1)} %add_add_fusion.1), channel_id=1, source_target_pairs={{0,0},{1,64},{2,128},{3,192},{4,256},{5,320},{6,384},{7,448},{8,8}... | collective-permute-start | bytes 12296 | tf_op jit(solution)/shard_map/ppermute | solution.py:297
  102.7 3.0 %collective-permute-start.10 = (f32[8,128]{1,0:T(8,128)S(1)}, f32[8,128]{1,0:T(8,128)S(1)}, u32[]{:S(2)}, u32[]{:S(2)}) collective-permute-start(f32[8,128]{1,0:T(8,128)S(1)} %collective-permute-done.9), channel_id=1, source_target_pairs={{0,1},{1,0},{2,3},{3,2},{4,5},{5,4},{6,7},{7,6},{8,9},{9,8},{10,11... | collective-permute-start | bytes 12296 | tf_op jit(solution)/shard_map/ppermute | solution.py:239
  105.8 24.0 %collective-permute-start.11 = (f32[8,128]{1,0:T(8,128)S(1)}, f32[8,128]{1,0:T(8,128)S(1)}, u32[]{:S(2)}, u32[]{:S(2)}) collective-permute-start(f32[8,128]{1,0:T(8,128)S(1)} %add.53), channel_id=1, source_target_pairs={{0,4},{1,5},{2,6},{3,7},{4,0},{5,1},{6,2},{7,3},{8,12},{9,13},{10,... | collective-permute-start | bytes 12296 | tf_op jit(solution)/shard_map/ppermute | solution.py:226
  123.2 6.5 %collective-permute-start.12 = (f32[8,128]{1,0:T(8,128)S(1)}, f32[8,128]{1,0:T(8,128)S(1)}, u32[]{:S(2)}, u32[]{:S(2)}) collective-permute-start(f32[8,128]{1,0:T(8,128)S(1)} %add.53), channel_id=1, source_target_pairs={{0,2},{1,3},{2,4},{3,5},{4,6},{5,7},{6,0},{7,1},{8,10},{9,11},{10,... | collective-permute-start | bytes 12296 | tf_op jit(solution)/shard_map/ppermute | solution.py:226
  125.1 5.3 %collective-permute-start.13 = (f32[8,128]{1,0:T(8,128)S(1)}, f32[8,128]{1,0:T(8,128)S(1)}, u32[]{:S(2)}, u32[]{:S(2)}) collective-permute-start(f32[8,128]{1,0:T(8,128)S(1)} %add.53), channel_id=1, source_target_pairs={{0,6},{1,7},{2,0},{3,1},{4,2},{5,3},{6,4},{7,5},{8,14},{9,15},{10,... | collective-permute-start | bytes 12296 | tf_op jit(solution)/shard_map/ppermute | solution.py:226
  131.1 1.1 copy-start.3

commit v3 on v2

--- a/solution.py
+++ b/solution.py
@@ -90,6 +90,33 @@
     return jnp.dot(a, b, preferred_element_type=jnp.float32)
 
 
+def gather_lanes(rows):
+    lane = lax.broadcasted_iota(jnp.int32, (8, HD), 1)
+    out = []
+    for n in range(2):
+        part = jnp.where(lane < SHARD, pltpu.roll(rows, (HD - 64 * n) % HD, 1), 0.0)
+        part = jnp.concatenate([part, jnp.zeros((8, (HEADS - 1) * HD), jnp.float32)], axis=1)
+        total = part[0:1]
+        for j in range(1, 8):
+            total = total + pltpu.roll(part, SHARD * j, 1)[j:j + 1]
+        out.append(total)
+    return out
+
+
+def spread_lanes(wide):
+    lane = lax.broadcasted_iota(jnp.int32, (8, HD), 1)
+    at = lax.broadcasted_iota(jnp.int32, (8, HD), 0)
+    out = jnp.zeros((8, HD), jnp.float32)
+    for n in range(2):
+        x = jnp.broadcast_to(wide[n], (8, HEADS * HD))
+        for j in range(8):
+            part = pltpu.roll(x, (HEADS * HD - SHARD * j) % (HEADS * HD), 1)[:, 0:HD]
+            part = pltpu.roll(part, 64 * n, 1)
+            keep = jnp.logical_and(at == j, jnp.logical_and(lane >= 64 * n, lane < 64 * n + SHARD))
+            out = jnp.where(keep, part, out)
+    return out
+
+
 def attend_kernel(lo_ref, hi_ref, pay_ref, gain_ref, ids_ref, out_ref, dg_ref,
                   qn, kn, vv, dq, acc_k, acc_v, mq, mk, outs, sems):
     for j in range(N_SEQ):
@@ -97,7 +124,8 @@
         at = slice(j * TOK, (j + 1) * TOK)
         mq[at] = column(join3(extra, 0))
         mk[at] = column(join3(extra, 1))
-    gains = [[gain_ref[n:n + 1, c * HD:(c + 1) * HD] for n in range(2)] for c in range(HEADS)]
+    wide = gather_lanes(gain_ref[...])
+    gains = [[wide[n][:, c * HD:(c + 1) * HD] for n in range(2)] for c in range(HEADS)]
     extra = extra_rows([row for pair in gains for row in pair], 2 * EXTRA)
     for j in range(N_SEQ):
         outs[j, BODY:] = extra
@@ -123,20 +151,42 @@
         keys = pl.ds(first, width)
         own = [column(ids_ref[:, pl.ds(pl.multiple_of(b * BQ + t, HD), HD)])[:, 0:1] for t in range(0, BQ, HD)]
         same = jnp.concatenate(own, axis=0) == ids_ref[:, keys]
-        for c in range(HEADS):
-            qb, kb, vb = qn[c, rows], kn[c, keys], vv[c, keys]
-            s = jnp.where(same, nt(qb, kb), -1e30)
+        qb = [qn[c, rows] for c in range(HEADS)]
+        kb = [kn[c, keys] for c in range(HEADS)]
+        vb = [vv[c, keys] for c in range(HEADS)]
+        val = {}
+
+        def score(c):
+            val["s", c] = nt(qb[c], kb[c])
+
+        def soft(c):
+            s = jnp.where(same, val["s", c], -1e30)
             top = jnp.max(s, axis=1, keepdims=True)
             e = jnp.exp2((s - top) * (SCALE * LOG2E))
-            p = e * (1.0 / jnp.sum(e, axis=1, keepdims=True))
-            pb = p.astype(jnp.bfloat16)
-            attn = nn(pb, vb).astype(jnp.bfloat16)
-            dp = nt(attn, vb)
+            val["p", c] = e * (1.0 / jnp.sum(e, axis=1, keepdims=True))
+            val["pb", c] = val["p", c].astype(jnp.bfloat16)
+
+        def mix(c):
+            val["a", c] = nn(val["pb", c], vb[c]).astype(jnp.bfloat16)
+
+        def back(c):
+            val["dp", c] = nt(val["a", c], vb[c])
+
+        def less(c):
+            p, dp = val["p", c], val["dp", c]
             delta = jnp.sum(p * dp, axis=1, keepdims=True)
-            ds = (p * (dp - delta) * SCALE).astype(jnp.bfloat16)
-            dq[c, rows] = nn(ds, kb).astype(jnp.bfloat16)
-            acc_v[c, :, keys] += nn(jnp.transpose(attn), pb)
-            acc_k[c, :, keys] += nn(jnp.transpose(qb), ds)
+            val["ds", c] = (p * (dp - delta) * SCALE).astype(jnp.bfloat16)
+
+        def values(c):
+            acc_v[c, :, keys] += nn(jnp.transpose(val["a", c]), val["pb", c])
+
+        def grads(c):
+            dq[c, rows] = nn(val["ds", c], kb[c]).astype(jnp.bfloat16)
+            acc_k[c, :, keys] += nn(jnp.transpose(qb[c]), val["ds", c])
+
+        for stage in (score, soft, mix, back, less, values, grads):
+            for c in range(HEADS):
+                stage(c)
 
     def step(b, carry):
         low = lo_ref[b] // TOK * TOK
@@ -159,44 +209,59 @@
         at = slice(j * TOK, (j + 1) * TOK)
         for c in range(HEADS):
             outs[j, body(c, 0)] = dq[c, at]
-            outs[j, body(c, 1)] = jnp.transpose(acc_k[c, :, at]).astype(jnp.bfloat16)
-            outs[j, body(c, 2)] = jnp.transpose(acc_v[c, :, at]).astype(jnp.bfloat16)
+            outs[j, body(c, 1)] = jnp.transpose(acc_k[c, :, at].astype(jnp.bfloat16))
+            outs[j, body(c, 2)] = jnp.transpose(acc_v[c, :, at].astype(jnp.bfloat16))
         copies.append(pltpu.make_async_copy(outs.at[j], out_ref.at[j], sems.at[j]))
         copies[j].start()
+    wide = [[], []]
     for c in range(HEADS):
-        sums = [jnp.zeros((1, HD), jnp.float32)] * 2
+        sums = [jnp.zeros((TOK, HD), jnp.float32)] * 2
         for j in range(N_SEQ):
             hat = hats(c, j)
-            sums = [sums[n] + jnp.sum(outs[j, body(c, n)].astype(jnp.float32) * hat[n], axis=0, keepdims=True)
-                    for n in range(2)]
+            sums = [sums[n] + outs[j, body(c, n)].astype(jnp.float32) * hat[n] for n in range(2)]
         for n in range(2):
-            dg_ref[n:n + 1, c * HD:(c + 1) * HD] = sums[n]
+            wide[n].append(jnp.sum(sums[n], axis=0, keepdims=True))
+    dg_ref[...] = spread_lanes([jnp.concatenate(rows, axis=1) for rows in wide])
     for copy in copies:
         copy.wait()
 
 
-def final_kernel(q_ref, k_ref, inv_q_ref, inv_k_ref, pay_ref, dq_ref, dk_ref, dv_ref):
+def final_kernel(q_ref, k_ref, inv_q_ref, inv_k_ref, pay_ref, dq_ref, dk_ref, dv_ref, held, outs, sems):
     pairs = [(s, c, slice((s * HEADS + c) * HD, (s * HEADS + c + 1) * HD))
              for s in range(N_SEQ) for c in range(HEADS)]
+    loads = [pltpu.make_async_copy(ref, held.at[n], sems.at[n]) for n, ref in enumerate((q_ref, k_ref))]
+    for load in loads:
+        load.start()
+    copies = []
+    for s, c, cols in pairs:
+        copies.append(pltpu.make_async_copy(
+            pay_ref.at[s, body(c, 2)], dv_ref.at[:, cols], sems.at[2 + len(copies)]))
+        copies[-1].start()
     extras = [pay_ref[s, BODY:].astype(jnp.float32) for s in range(N_SEQ)]
-    for n, (ref, inv_ref, out_ref) in enumerate(
-            ((q_ref, inv_q_ref, dq_ref), (k_ref, inv_k_ref, dk_ref))):
+    for n, (inv_ref, out_ref) in enumerate(((inv_q_ref, dq_ref), (inv_k_ref, dk_ref))):
+        loads[n].wait()
         inv = inv_ref[...]
 
         def parts(s, c, cols):
             dhat = pay_ref[s, body(c, n)].astype(jnp.float32) * join3(extras[s], 2 * c + n)
-            return (dhat, ref[:, cols].astype(jnp.float32) * inv)
+            return (dhat, held[n, :, cols].astype(jnp.float32) * inv)
 
         total = jnp.zeros((TOK, HD), jnp.float32)
         for pair in pairs:
             dhat, hat = parts(*pair)
             total = total + dhat * hat
         mean = jnp.sum(total, axis=1, keepdims=True) * (1.0 / WIDTH)
-        for pair in pairs:
-            dhat, hat = parts(*pair)
-            out_ref[:, pair[2]] = (inv * (dhat - hat * mean)).astype(jnp.bfloat16)
-    for s, c, cols in pairs:
-        dv_ref[:, cols] = pay_ref[s, body(c, 2)]
+        for s in range(N_SEQ):
+            for pair in pairs[s * HEADS:(s + 1) * HEADS]:
+                dhat, hat = parts(*pair)
+                outs[n, :, pair[2]] = (inv * (dhat - hat * mean)).astype(jnp.bfloat16)
+            if s % 4 == 3:
+                cols = slice((s - 3) * HEADS * HD, (s + 1) * HEADS * HD)
+                copies.append(pltpu.make_async_copy(
+                    outs.at[n, :, cols], out_ref.at[:, cols], sems.at[2 + len(copies)]))
+                copies[-1].start()
+    for copy in copies:
+        copy.wait()
 
 
 def hold_kernel(x_ref, after_ref, out_ref):
@@ -206,8 +271,7 @@
 def hold(x, after):
     return pl.pallas_call(
         hold_kernel, out_shape=shape(x.shape, jnp.float32),
-        in_specs=[pl.BlockSpec(memory_space=pltpu.VMEM), pl.BlockSpec(memory_space=pl.ANY)],
-        name="hold", cost_estimate=pl.CostEstimate(flops=1 << 36, bytes_accessed=1 << 27, transcendentals=0),
+        in_specs=[HERE, HERE], out_specs=HERE, name="hold", cost_estimate=pl.CostEstimate(flops=1 << 36, bytes_accessed=1 << 27, transcendentals=0),
     )(x, after)
 
 
@@ -215,7 +279,13 @@
     return jax.ShapeDtypeStruct(dims, dtype)
 
 
-PARAMS = pltpu.CompilerParams(vmem_limit_bytes=48 * 1024 * 1024)
+def params(mib):
+    return pltpu.CompilerParams(vmem_limit_bytes=mib * 1024 * 1024)
+
+
+HERE = pl.BlockSpec(memory_space=pltpu.VMEM)
+THERE = pl.BlockSpec(memory_space=pltpu.HBM)
+SCALARS = pl.BlockSpec(memory_space=pltpu.SMEM)
 
 
 def swapped():
@@ -246,6 +316,20 @@
 def spread(pair):
     pad = jnp.zeros(pair.shape[:-2] + (16,), jnp.float32)
     return jnp.concatenate([pair[..., 0, :], pad, pair[..., 1, :], pad], axis=-1)
+
+
+def attend_call(lo, hi, got, gain, ids):
+    back = shape((N_SEQ, BODY + 2 * EXTRA, HD))
+    half = pltpu.VMEM((HEADS, G, HD), jnp.bfloat16)
+    full = pltpu.VMEM((G, HD), jnp.float32)
+    turn = pltpu.VMEM((HEADS, HD, G), jnp.float32)
+    return pl.pallas_call(
+        attend_kernel, out_shape=[back, shape((8, HD), jnp.float32)],
+        in_specs=[SCALARS, SCALARS, HERE, HERE, HERE], out_specs=[THERE, HERE],
+        scratch_shapes=[half] * 4 + [turn] * 2 + [full] * 2 + [
+            pltpu.VMEM(back.shape, jnp.bfloat16), pltpu.SemaphoreType.DMA((N_SEQ,))],
+        compiler_params=params(60), name="attend",
+    )(lo, hi, got, gain, ids)
 
 
 def windows(ids):
@@ -258,49 +342,40 @@
 
 def local(q_in, k_in, v_in, gain_q, gain_k, clip_ids):
     place = lax.axis_index("dp") % 8
-    sent = shape((N_SEQ, BODY + EXTRA, HD))
-    back = shape((N_SEQ, BODY + 2 * EXTRA, HD))
     inv = shape((TOK, HD), jnp.float32)
-    here = pl.BlockSpec(memory_space=pltpu.VMEM)
-    there = pl.BlockSpec(memory_space=pl.ANY)
+    pair = pltpu.VMEM((2, TOK, WIDTH), jnp.bfloat16)
 
     row = spread(jnp.stack([gain_q, gain_k]))[None]
     rows = jnp.where(lax.broadcasted_iota(jnp.int32, (8, HD), 0) == place, row, 0.0)
     rows = over_z(rows)
 
     pay, inv_q, inv_k, mark = pl.pallas_call(
-        pack_kernel, out_shape=[sent, inv, inv, shape((8, HD), jnp.float32)],
-        in_specs=[there] * 3, out_specs=[there, here, here, here],
-        scratch_shapes=[pltpu.VMEM((2, TOK, WIDTH), jnp.bfloat16), pltpu.VMEM((EXTRA, HD), jnp.bfloat16),
+        pack_kernel,
+        out_shape=[shape((N_SEQ, BODY + EXTRA, HD)), inv, inv, shape((8, HD), jnp.float32)],
+        in_specs=[THERE] * 3, out_specs=[THERE, HERE, HERE, HERE],
+        scratch_shapes=[pair, pltpu.VMEM((EXTRA, HD), jnp.bfloat16),
                         pltpu.SemaphoreType.DMA((2 + 3 * H + N_SEQ,))],
-        compiler_params=PARAMS, name="pack",
+        compiler_params=params(62), name="pack",
     )(q_in, k_in, v_in)
     got = lax.all_to_all(pay, "seq", 0, 0, tiled=True)
     rows = lax.ppermute(over_y(hold(rows, mark)), ("dp", "seq"), swapped())
-    gain = jnp.stack([rows[:, 0:SHARD].reshape(-1), rows[:, 64:64 + SHARD].reshape(-1)])
     lo, hi = windows(clip_ids)
-
-    half = pltpu.VMEM((HEADS, G, HD), jnp.bfloat16)
-    full = pltpu.VMEM((G, HD), jnp.float32)
-    turn = pltpu.VMEM((HEADS, HD, G), jnp.float32)
-    few = pl.BlockSpec(memory_space=pltpu.SMEM)
-    pay, dg = pl.pallas_call(
-        attend_kernel, out_shape=[back, shape((2, HEADS * HD), jnp.float32)],
-        in_specs=[few, few, here, here, here], out_specs=[there, here],
-        scratch_shapes=[half] * 4 + [turn] * 2 + [full] * 2 + [
-            pltpu.VMEM(back.shape, jnp.bfloat16), pltpu.SemaphoreType.DMA((N_SEQ,))],
-        compiler_params=PARAMS, name="attend",
-    )(lo, hi, got, gain, clip_ids)
+    pay, part = attend_call(lo, hi, got, rows, clip_ids)
+
+    blocks = [list(range(b, b + 8)) for b in range(0, 64, 8)]
+    part = lax.all_to_all(part, "dp", 0, 0, axis_index_groups=blocks, tiled=True)
+    part = jnp.sum(part, axis=0, keepdims=True)
+    pay, part = lax.optimization_barrier((pay, part))
     got = lax.all_to_all(pay, "seq", 0, 0, tiled=True)
-
-    part = hold(spread(jnp.transpose(dg.reshape(2, N_SEQ, SHARD), (1, 0, 2))), dg)
-    part = lax.ppermute(over_y(over_z(part)), ("dp", "seq"), swapped())
-    part = over_x(over_core(part))
-    part = lax.dynamic_index_in_dim(part, place, 0, keepdims=False)
+    part = hold(part, part)
+    part = over_x(over_core(lax.ppermute(part, ("dp", "seq"), swapped())))[0]
 
     out = shape((TOK, WIDTH))
     d_q, d_k, d_v = pl.pallas_call(
-        final_kernel, out_shape=[out] * 3, compiler_params=PARAMS, name="final",
+        final_kernel, out_shape=[out] * 3,
+        in_specs=[THERE, THERE, HERE, HERE, HERE], out_specs=[THERE] * 3,
+        scratch_shapes=[pair, pair, pltpu.SemaphoreType.DMA((2 + H + 4,))],
+        compiler_params=params(61), name="final",
     )(q_in, k_in, inv_q, inv_k, got)
     return (d_q, d_k, d_v, part[0:SHARD], part[64:64 + SHARD])
 

time: 137 us -> 193 us (1.41)
  Pallas kernels: 25.7 us -> 94.5 us
  starting transfers between devices: 75.4 us -> 59.5 us
  blocking collectives: 0 us -> 8.45 us
  local copies, waits for them, and re-layouts: 9.56 us -> 3.66 us
    pallas_call x3, Pallas kernels: 23.1 us -> 92 us  [the longest x1 74 us: local(): pl.pallas_call(pack_kernel, out_shape=[shape((N_SEQ, BODY + EXTRA, HD)),...]
    ppermute x9 -> x6, starting transfers between devices: 43 us -> 28 us  [sum_four(): one, two, three = (lax.ppermute(x, axis, pairs(k)) for k in (1, 2, 3))]
    all_to_all x0 -> x1, blocking collectives: none -> 8.45 us  [local(): lax.all_to_all(part, 'dp', 0, 0, axis_index_groups=blocks, tiled=True)]
    unnamed x20 -> x8, local copies, waits for them, and re-layouts: 8.46 us -> 2.88 us
    all_to_all x2, starting transfers between devices: 13.8 us -> 18.5 us  [local(): got = lax.all_to_all(pay, 'seq', 0, 0, tiled=True)]
    ppermute x2 -> x1, waiting for transfers between devices: 2.93 us -> 0.01 us  [over_z(): return x + lax.ppermute(x, 'dp', [(d, d ^ 4) for d in range(64)])]
    ppermute x1, starting transfers between devices: 4.66 us -> 1.91 us  [local(): part = over_x(over_core(lax.ppermute(part, ('dp', 'seq'), swapped())))[0]]
    ppermute x1, waiting for transfers between devices: 1.58 us -> 4.26 us  [local(): part = over_x(over_core(lax.ppermute(part, ('dp', 'seq'), swapped())))[0]]
  transfers between devices with their start and end apart: 16 -> 12, of which waited for: 8 -> 7; matrix products, arithmetic and copies ran while one was open for 3% -> 2% of each run, Pallas kernels for 4% -> 40%
where the time goes in v3:
time: 193 us; the launch traced here: 190 us
  Pallas kernels  94.5 us (49%)
  starting transfers between devices  59.5 us (31%)
  waiting for transfers between devices  20 us (10%)
  blocking collectives  8.45 us (4%)
  local copies, waits for them, and re-layouts  3.66 us (2%)
  other arithmetic  3.47 us (2%)
    pallas_call x1, Pallas kernels, local(): pl.pallas_call(pack_kernel, out_shape=[shape((N_SEQ, BODY + EXTRA, HD)),...  74 us
    ppermute x6, starting transfers between devices, sum_four(): one, two, three = (lax.ppermute(x, axis, pairs(k)) for k in (1, 2, 3))  28 us
    all_to_all x2, starting transfers between devices, local(): got = lax.all_to_all(pay, 'seq', 0, 0, tiled=True)  18.5 us
    pallas_call x1, Pallas kernels, attend_call(): pl.pallas_call(attend_kernel, out_shape=[back, shape((8, HD), jnp.float32...  12.1 us
    all_to_all x2, waiting for transfers between devices, local(): got = lax.all_to_all(pay, 'seq', 0, 0, tiled=True)  9.11 us
    all_to_all x1, blocking collectives, local(): lax.all_to_all(part, 'dp', 0, 0, axis_index_groups=blocks, tiled=True)  8.45 us
    pallas_call x1, Pallas kernels, local(): pl.pallas_call(final_kernel, out_shape=[out] * 3, in_specs=[THERE, THERE,...  5.89 us
    ppermute x1, starting transfers between devices, local(): rows = lax.ppermute(over_y(hold(rows, mark)), ('dp', 'seq'), swapped())  4.77 us
  transfers between devices with their start and end apart: 12, of which 7 were waited for; matrix products, arithmetic and copies ran while one was open for 2% of the time, Pallas kernels for 40%

profile of v3, /device:TPU:1, one launch (start us, length us, event | category | flops | bytes accessed | tf_op | source)
XLA Modules:
  0.0 190.3 jit_solution(17033207305700952932)
XLA Ops:
  0.7 0.8 pad_maximum_fusion
  1.4 0.1 broadcast_select_fusion
  1.5 4.4 %collective-permute-start = (f32[8,128]{1,0:T(8,128)S(1)}, f32[8,128]{1,0:T(8,128)S(1)}, u32[]{:S(2)}, u32[]{:S(2)}) collective-permute-start(f32[8,128]{1,0:T(8,128)S(1)} %broadcast_select_fusion), channel_id=1, source_target_pairs={{0,32},{8,40},{16,48},{24,56},{32,0},{40,8},{48,16},{56,24},{64,96... | collective-permute-start | bytes 12296 | tf_op jit(solution)/shard_map/ppermute | solution.py:301
  5.9 74.0 %pack.1 = (bf16[8,1168,128]{2,1,0:T(8,128)(2,1)}, f32[128,128]{1,0:T(8,128)}, f32[128,128]{1,0:T(8,128)}, f32[8,128]{1,0:T(8,128)}) custom-call(bf16[128,3072]{1,0:T(8,128)(2,1)} %q_ref.3, bf16[128,3072]{1,0:T(8,128)(2,1)} %k_ref.3, bf16[128,3072]{1,0:T(8,128)(2,1)} %v_ref.1), custom_call_target="tpu_custom_call" | custom-call | tf_op jit(solution)/shard_map/pack/pallas_call | solution.py:352
  79.9 8.0 %all-to-all-start = ((bf16[8,1168,128]{2,1,0:T(8,128)(2,1)}), bf16[8,1168,128]{2,1,0:T(8,128)(2,1)S(1)}, u32[]{:S(2)}, u32[]{:S(2)}) async-start(bf16[8,1168,128]{2,1,0:T(8,128)(2,1)} %get-tuple-element.18), calls=%async_computation | async-start | bytes 4784128 | tf_op jit(solution)/shard_map/all_to_all | solution.py:360
  87.8 0.0 collective-permute-done
  87.8 0.7 fusion.x_ref
  88.5 0.0 copy-start.2
  88.5 1.3 hold.2
  89.8 1.9 %collective-permute-start.3 = (f32[8,128]{1,0:T(8,128)}, f32[8,128]{1,0:T(8,128)S(1)}, u32[]{:S(2)}, u32[]{:S(2)}) collective-permute-start(f32[8,128]{1,0:T(8,128)} %hold.2), channel_id=1, source_target_pairs={{0,24},{8,0},{16,8},{24,16},{32,56},{40,32},{48,40},{56,48},{64,88... | collective-permute-start | bytes 12296 | tf_op jit(solution)/shard_map/ppermute | solution.py:296
  91.7 3.4 %collective-permute-start.2 = (f32[8,128]{1,0:T(8,128)}, f32[8,128]{1,0:T(8,128)S(1)}, u32[]{:S(2)}, u32[]{:S(2)}) collective-permute-start(f32[8,128]{1,0:T(8,128)} %hold.2), channel_id=1, source_target_pairs={{0,8},{8,16},{16,24},{24,0},{32,40},{40,48},{48,56},{56,32},{64,72... | collective-permute-start | bytes 12296 | tf_op jit(solution)/shard_map/ppermute | solution.py:296
  95.1 2.1 %collective-permute-start.1 = (f32[8,128]{1,0:T(8,128)}, f32[8,128]{1,0:T(8,128)S(1)}, u32[]{:S(2)}, u32[]{:S(2)}) collective-permute-start(f32[8,128]{1,0:T(8,128)} %hold.2), channel_id=1, source_target_pairs={{0,16},{8,24},{16,0},{24,8},{32,48},{40,56},{48,32},{56,40},{64,80... | collective-permute-start | bytes 12296 | tf_op jit(solution)/shard_map/ppermute | solution.py:296
  97.2 0.0 copy-done.2
  97.2 0.1 slice.18
  97.3 0.1 slice.19
  97.4 0.0 collective-permute-done.3
  97.4 0.4 collective-permute-done.2
  97.8 3.4 %collective-permute-done.1 = f32[8,128]{1,0:T(8,128)S(1)} collective-permute-done((f32[8,128]{1,0:T(8,128)}, f32[8,128]{1,0:T(8,128)S(1)}, u32[]{:S(2)}, u32[]{:S(2)}) %collective-permute-start.1) | collective-permute-done | bytes 4128 | tf_op jit(solution)/shard_map/ppermute | solution.py:296
  101.2 0.7 add_add_fusion
  101.9 4.8 %collective-permute-start.4 = (f32[8,128]{1,0:T(8,128)S(1)}, f32[8,128]{1,0:T(8,128)S(1)}, u32[]{:S(2)}, u32[]{:S(2)}) collective-permute-start(f32[8,128]{1,0:T(8,128)S(1)} %add_add_fusion), channel_id=1, source_target_pairs={{0,0},{1,64},{2,128},{3,192},{4,256},{5,320},{6,384},{7,448},{8,8}... | collective-permute-start | bytes 12296 | tf_op jit(solution)/shard_map/ppermute | solution.py:361
  106.7 0.7 convert_reduce_fusion
  107.4 0.8 collective-permute-done.4.gain_ref
  108.2 0.0 copy-start.3
  108.2 9.1 %all-to-all-done.pay_ref = bf16[8,1168,128]{2,1,0:T(8,128)(2,1)S(1)} async-done(((bf16[8,1168,128]{2,1,0:T(8,128)(2,1)}), bf16[8,1168,128]{2,1,0:T(8,128)(2,1)S(1)}, u32[]{:S(2)}, u32[]{:S(2)}) %all-to-all-start) | async-done | bytes 2392096 | tf_op jit(solution)/shard_map/all_to_all | solution.py:360
  117.3 0.0 copy-start.1
  117.3 0.0 copy-done.3
  117.3 1.4 copy-done.1
  118.8 12.1 %attend.1 = (bf16[8,1184,128]{2,1,0:T(8,128)(2,1)}, f32[8,128]{1,0:T(8,128)}) custom-call(s32[4]{0:T(128)} %get-tuple-element.28.lo_ref, s32[4]{0:T(128)} %get-tuple-element.27.hi_ref, bf16[8,1168,128]{2,1,0:T(8,128)(2,1)} %copy-done.1, f32[8,128]{1,0:T(8,128)} %copy-done.3, s32[1,1024]{1,0:T(1,128)} %ids_ref.1), custom_call_target="tpu_custom_call" | custom-call | tf_op jit(solution)/shard_map/attend/pallas_call | solution.py:326
  130.8 8.5 %all_to_all.19 = f32[8,1,128]{2,1,0:T(1,128)S(1)} all-to-all(f32[8,1,128]{2,1,0:T(1,128)} %bitcast.12), channel_id=1, replica_groups={{0,8,16,24,32,40,48,56},{64,72,80,88,96,104,112,120},{128,136,144,152,1..., dimensions={0} | all-to-all | bytes 8192 | tf_op jit(solution)/shard_map/all_to_all | solution.py:366
  139.3 0.5 reduce_sum.29
  139.8 10.5 %all-to-all-start.2 = ((bf16[8,1184,128]{2,1,0:T(8,128)(2,1)}), bf16[8,1184,128]{2,1,0:T(8,128)(2,1)S(1)}, u32[]{:S(2)}, u32[]{:S(2)}) async-start(bf16[8,1184,128]{2,1,0:T(8,128)(2,1)} %get-tuple-element.22), calls=%async_computation.2 | async-start | bytes 4849664 | tf_op jit(solution)/shard_map/all_to_all | solution.py:369
  150.4 1.2 hold.3
  151.6 1.9 %collective-permute-start.5 = (f32[1,128]{1,0:T(1,128)}, f32[1,128]{1,0:T(1,128)S(1)}, u32[]{:S(2)}, u32[]{:S(2)}) collective-permute-start(f32[1,128]{1,0:T(1,128)} %hold.3), channel_id=1, source_target_pairs={{0,0},{1,64},{2,128},{3,192},{4,256},{5,320},{6,384},{7,448},{8,8}... | collective-permute-start | bytes 1544 | tf_op jit(solution)/shard_map/ppermute | solution.py:371
  153.5 4.3 %collective-permute-done.5 = f32[1,128]{1,0:T(1,128)S(1)} collective-permute-done((f32[1,128]{1,0:T(1,128)}, f32[1,128]{1,0:T(1,128)S(1)}, u32[]{:S(2)}, u32[]{:S(2)}) %collective-permute-start.5) | collective-permute-done | bytes 544 | tf_op jit(solution)/shard_map/ppermute | solution.py:371
  157.8 1.9 %collective-permute-start.6 = (f32[1,128]{1,0:T(1,128)S(1)}, f32[1,128]{1,0:T(1,128)S(1)}, u32[]{:S(2)}, u32[]{:S(2)}) collective-permute-start(f32[1,128]{1,0:T(1,128)S(1)} %collective-permute-done.5), channel_id=1, source_target_pairs={{0,1},{1,0},{2,3},{3,2},{4,5},{5,4},{6,7},{7,6},{8,9},{9,8},{10,11... | collective-permute-start | bytes 1544 | tf_op jit(solution)/shard_map/ppermute | solution.py:309
  159.7 1.1 collective-permute-done.6
  160.8 10.4 %collective-permute-start.9 = (f32[1,128]{1,0:T(1,128)S(1)}, f32[1,128]{1,0:T(1,128)S(1)}, u32[]{:S(2)}, u32[]{:S(2)}) collective-permute-start(f32[1,128]{1,0:T(1,128)S(1)} %add.33), channel_id=1, source_target_pairs={{0,6},{1,7},{2,0},{3,1},{4,2},{5,3},{6,4},{7,5},{8,14},{9,15},{10,... | collective-permute-start | bytes 1544 | tf_op jit(solution)/shard_map/ppermute | solution.py:296
  171.2 1.9 %collective-permute-start.8 = (f32[1,128]{1,0:T(1,128)S(1)}, f32[1,128]{1,0:T(1,128)S(1)}, u32[]{:S(2)}, u32[]{:S(2)}) collective-permute-start(f32[1,128]{1,0:T(1,128)S(1)} %add.33), channel_id=1, source_target_pairs={{0,2},{1,3},{2,4},{3,5},{4,6},{5,7},{6,0},{7,1},{8,10},{9,11},{10,... | collective-permute-start | bytes 1544 | tf_op jit(solution)/shard_map/ppermute | solution.py:296
  173.1 8.3 %collective-permute-start.7 = (f32[1,128]{1,0:T(1,128)S(1)}, f32[1,128]{1,0:T(1,128)S(1)}, u32[]{:S(2)}, u32[]{:S(2)}) collective-permute-start(f32[1,128]{1,0:T(1,128)S(1)} %add.33), channel_id=1, source_target_pairs={{0,4},{1,5},{2,6},{3,7},{4,0},{5,1},{6,2},{7,3},{8,12},{9,13},{10,... | collective-permute-start | bytes 1544 | tf_op jit(solution)/shard_map/ppermute | solution.py:296
  181.4 0.0 collective-permute-done.9
  181.4 0.0 collective-permute-done.8
  181.5 0.9 collective-permute-done.7
  182.4 0.6 slice_bitcast_fusion
  182.9 0.0 all-to-all-done.2.pay_ref
  182.9 0.0 copy-start
  182.9 1.4 copy-done
  184.4 5.9 %final.1 = (bf16[128,3072]{1,0:T(8,128)(2,1)}, bf16[128,3072]{1,0:T(8,128)(2,1)}, bf16[128,3072]{1,0:T(8,128)(2,1)}) custom-call(bf16[128,3072]{1,0:T(8,128)(2,1)} %q_ref.3, bf16[128,3072]{1,0:T(8,128)(2,1)} %k_ref.3, f32[128,128]{1,0:T(8,128)} %get-tuple-element.16.inv_q_ref, f32[128,128]{1,0:T(8,128)} %get-tuple-element.17.inv_k_ref, ...), custom_call_target="tpu_custom_call" | custom-call | tf_op jit(solution)/shard_map/final/pallas_call | solution.py:374
  (4 shorter events, 0.0 us)
Async XLA Ops:
  1.5 86.3 %collective-permute-start = (f32[8,128]{1,0:T(8,128)S(1)}, f32[8,128]{1,0:T(8,128)S(1)}, u32[]{:S(2)}, u32[]{:S(2)}) collective-permute-start(f32[8,128]{1,0:T(8,128)S(1)} %broadcast_select_fusion), channel_id=1, source_target_pairs={{0,32},{8,40},{16,48},{24,56},{32,0},{40,8},{48,16},{56,24},{64,96... | collective-permute-start | bytes 12296 | tf_op jit(solution)/shard_map/ppermute | solution.py:301
  79.9 37.5 %all-to-all-start = ((bf16[8,1168,128]{2,1,0:T(8,128)(2,1)}), bf16[8,1168,128]{2,1,0:T(8,128)(2,1)S(1)}, u32[]{:S(2)}, u32[]{:S(2)}) async-start(bf16[8,1168,128]{2,1,0:T(8,128)(2,1)} %get-tuple-element.18), calls=%async_computation | async-start | bytes 4784128 | tf_op jit(solution)/shard_map/all_to_all | solution.py:360
  88.5 8.7 %copy-start.2 = (s32[1,1024]{1,0:T(1,128)S(1)}, s32[1,1024]{1,0:T(1,128)}, u32[]{:S(2)}) copy-start(s32[1,1024]{1,0:T(1,128)} %ids_ref.1) | copy-start | bytes 12292
  89.8 7.6 %collective-permute-start.3 = (f32[8,128]{1,0:T(8,128)}, f32[8,128]{1,0:T(8,128)S(1)}, u32[]{:S(2)}, u32[]{:S(2)}) collective-permute-start(f32[8,128]{1,0:T(8,128)} %hold.2), channel_id=1, source_target_pairs={{0,24},{8,0},{16,8},{24,16},{32,56},{40,32},{48,40},{56,48},{64,88... | collective-permute-start | bytes 12296 | tf_op jit(solution)/shard_map/ppermute | solution.py:296
  91.7 6.1 %collective-permute-start.2 = (f32[8,128]{1,0:T(8,128)}, f32[8,128]{1,0:T(8,128)S(1)}, u32[]{:S(2)}, u32[]{:S(2)}) collective-permute-start(f32[8,128]{1,0:T(8,128)} %hold.2), channel_id=1, source_target_pairs={{0,8},{8,16},{16,24},{24,0},{32,40},{40,48},{48,56},{56,32},{64,72... | collective-permute-start | bytes 12296 | tf_op jit(solution)/shard_map/ppermute | solution.py:296
  95.1 6.1 %collective-permute-start.1 = (f32[8,128]{1,0:T(8,128)}, f32[8,128]{1,0:T(8,128)S(1)}, u32[]{:S(2)}, u32[]{:S(2)}) collective-permute-start(f32[8,128]{1,0:T(8,128)} %hold.2), channel_id=1, source_target_pairs={{0,16},{8,24},{16,0},{24,8},{32,48},{40,56},{48,32},{56,40},{64,80... | collective-permute-start | bytes 12296 | tf_op jit(solution)/shard_map/ppermute | solution.py:296
  101.9 6.3 %collective-permute-start.4 = (f32[8,128]{1,0:T(8,128)S(1)}, f32[8,128]{1,0:T(8,128)S(1)}, u32[]{:S(2)}, u32[]{:S(2)}) collective-permute-start(f32[8,128]{1,0:T(8,128)S(1)} %add_add_fusion), channel_id=1, source_target_pairs={{0,0},{1,64},{2,128},{3,192},{4,256},{5,320},{6,384},{7,448},{8,8}... | collective-permute-start | bytes 12296 | tf_op jit(solution)/shard_map/ppermute | solution.py:361
  108.2 9.1 %copy-start.3 = (f32[8,128]{1,0:T(8,128)}, f32[8,128]{1,0:T(8,128)S(1)}, u32[]{:S(2)}) copy-start(f32[8,128]{1,0:T(8,128)S(1)} %collective-permute-done.4.gain_ref) | copy-start | bytes 12292
  117.3 1.4 copy-start.1
  139.8 43.1 %all-to-all-start.2 = ((bf16[8,1184,128]{2,1,0:T(8,128)(2,1)}), bf16[8,1184,128]{2,1,0:T(8,128)(2,1)S(1)}, u32[]{:S(2)}, u32[]{:S(2)}) async-start(bf16[8,1184,128]{2,1,0:T(8,128)(2,1)} %get-tuple-element.22), calls=%async_computation.2 | async-start | bytes 4849664 | tf_op jit(solution)/shard_map/all_to_all | solution.py:369
  151.6 6.2 %collective-permute-start.5 = (f32[1,128]{1,0:T(1,128)}, f32[1,128]{1,0:T(1,128)S(1)}, u32[]{:S(2)}, u32[]{:S(2)}) collective-permute-start(f32[1,128]{1,0:T(1,128)} %hold.3), channel_id=1, source_target_pairs={{0,0},{1,64},{2,128},{3,192},{4,256},{5,320},{6,384},{7,448},{8,8}... | collective-permute-start | bytes 1544 | tf_op jit(solution)/shard_map/ppermute | solution.py:371
  157.8 3.0 %collective-permute-start.6 = (f32[1,128]{1,0:T(1,128)S(1)}, f32[1,128]{1,0:T(1,128)S(1)}, u32[]{:S(2)}, u32[]{:S(2)}) collective-permute-start(f32[1,128]{1,0:T(1,128)S(1)} %collective-permute-done.5), channel_id=1, source_target_pairs={{0,1},{1,0},{2,3},{3,2},{4,5},{5,4},{6,7},{7,6},{8,9},{9,8},{10,11... | collective-permute-start | bytes 1544 | tf_op jit(solution)/shard_map/ppermute | solution.py:309
  160.8 20.7 %collective-permute-start.9 = (f32[1,128]{1,0:T(1,128)S(1)}, f32[1,128]{1,0:T(1,128)S(1)}, u32[]{:S(2)}, u32[]{:S(2)}) collective-permute-start(f32[1,128]{1,0:T(1,128)S(1)} %add.33), channel_id=1, source_target_pairs={{0,6},{1,7},{2,0},{3,1},{4,2},{5,3},{6,4},{7,5},{8,14},{9,15},{10,... | collective-permute-start | bytes 1544 | tf_op jit(solution)/shard_map/ppermute | solution.py:296
  171.2 10.3 %collective-permute-start.8 = (f32[1,128]{1,0:T(1,128)S(1)}, f32[1,128]{1,0:T(1,128)S(1)}, u32[]{:S(2)}, u32[]{:S(2)}) collective-permute-start(f32[1,128]{1,0:T(1,128)S(1)} %add.33), channel_id=1, source_target_pairs={{0,2},{1,3},{2,4},{3,5},{4,6},{5,7},{6,0},{7,1},{8,10},{9,11},{10,... | collective-permute-start | bytes 1544 | tf_op jit(solution)/shard_map/ppermute | solution.py:296
  173.1 9.3 %collective-permute-start.7 = (f32[1,128]{1,0:T(1,128)S(1)}, f32[1,128]{1,0:T(1,128)S(1)}, u32[]{:S(2)}, u32[]{:S(2)}) collective-permute-start(f32[1,128]{1,0:T(1,128)S(1)} %add.33), channel_id=1, source_target_pairs={{0,4},{1,5},{2,6},{3,7},{4,0},{5,1},{6,2},{7,3},{8,12},{9,13},{10,... | collective-permute-start | bytes 1544 | tf_op jit(solution)/shard_map/ppermute | solution.py:296
  182.9 1.4 copy-start

commit v4 on v3

--- a/solution.py
+++ b/solution.py
@@ -49,22 +49,23 @@
     return slice((c * 3 + n) * TOK, (c * 3 + n + 1) * TOK)
 
 
-def pack_kernel(q_ref, k_ref, v_ref, pay_ref, inv_q_ref, inv_k_ref, mark_ref, held, extra, sems):
+def pack_kernel(turn_ref, q_ref, k_ref, v_ref, pay_ref, inv_q_ref, inv_k_ref, mark_ref, held, extra, sems):
     loads = []
-    for n, ref in enumerate((q_ref, k_ref)):
+    for n, ref in enumerate((q_ref, k_ref, v_ref)):
         loads.append(pltpu.make_async_copy(ref, held.at[n], sems.at[n]))
         loads[n].start()
+    dest = [(g + N_SEQ - turn_ref[0]) % N_SEQ for g in range(N_SEQ)]
     copies = []
-    for s in range(N_SEQ):
-        for c in range(HEADS):
-            h = s * HEADS + c
-            for n, ref in enumerate((q_ref, k_ref, v_ref)):
+    for n in range(3):
+        loads[n].wait()
+        for g in range(N_SEQ):
+            for c in range(HEADS):
+                h = g * HEADS + c
                 copies.append(pltpu.make_async_copy(
-                    ref.at[:, h * HD:(h + 1) * HD], pay_ref.at[s, body(c, n)], sems.at[2 + len(copies)]))
+                    held.at[n, :, h * HD:(h + 1) * HD], pay_ref.at[dest[g], body(c, n)], sems.at[3 + len(copies)]))
                 copies[-1].start()
     rows = []
     for n, inv_ref in enumerate((inv_q_ref, inv_k_ref)):
-        loads[n].wait()
         total = jnp.zeros((TOK, HD), jnp.float32)
         for h in range(H):
             x = held[n, :, h * HD:(h + 1) * HD].astype(jnp.float32)
@@ -76,7 +77,7 @@
     mark_ref[...] = jnp.zeros_like(mark_ref)
     extra[...] = extra_rows(rows, EXTRA)
     for s in range(N_SEQ):
-        copies.append(pltpu.make_async_copy(extra, pay_ref.at[s, BODY:], sems.at[2 + len(copies)]))
+        copies.append(pltpu.make_async_copy(extra, pay_ref.at[s, BODY:], sems.at[3 + len(copies)]))
         copies[-1].start()
     for copy in copies:
         copy.wait()
@@ -226,40 +227,36 @@
         copy.wait()
 
 
-def final_kernel(q_ref, k_ref, inv_q_ref, inv_k_ref, pay_ref, dq_ref, dk_ref, dv_ref, held, outs, sems):
-    pairs = [(s, c, slice((s * HEADS + c) * HD, (s * HEADS + c + 1) * HD))
-             for s in range(N_SEQ) for c in range(HEADS)]
-    loads = [pltpu.make_async_copy(ref, held.at[n], sems.at[n]) for n, ref in enumerate((q_ref, k_ref))]
-    for load in loads:
-        load.start()
+def final_kernel(turn_ref, q_ref, k_ref, inv_q_ref, inv_k_ref, pay_ref, dq_ref, dk_ref, dv_ref, outs, sems):
+    src = [(g + N_SEQ - turn_ref[0]) % N_SEQ for g in range(N_SEQ)]
+    pairs = [(g, c, slice((g * HEADS + c) * HD, (g * HEADS + c + 1) * HD))
+             for g in range(N_SEQ) for c in range(HEADS)]
     copies = []
-    for s, c, cols in pairs:
-        copies.append(pltpu.make_async_copy(
-            pay_ref.at[s, body(c, 2)], dv_ref.at[:, cols], sems.at[2 + len(copies)]))
+
+    def send(n, ref):
+        copies.append(pltpu.make_async_copy(outs.at[n], ref, sems.at[n]))
         copies[-1].start()
-    extras = [pay_ref[s, BODY:].astype(jnp.float32) for s in range(N_SEQ)]
-    for n, (inv_ref, out_ref) in enumerate(((inv_q_ref, dq_ref), (inv_k_ref, dk_ref))):
-        loads[n].wait()
+
+    for g, c, cols in pairs:
+        outs[2, :, cols] = pay_ref[src[g], body(c, 2)]
+    send(2, dv_ref)
+    extras = [pay_ref[src[g], BODY:].astype(jnp.float32) for g in range(N_SEQ)]
+    for n, (ref, inv_ref, out_ref) in enumerate(((q_ref, inv_q_ref, dq_ref), (k_ref, inv_k_ref, dk_ref))):
         inv = inv_ref[...]
 
-        def parts(s, c, cols):
-            dhat = pay_ref[s, body(c, n)].astype(jnp.float32) * join3(extras[s], 2 * c + n)
-            return (dhat, held[n, :, cols].astype(jnp.float32) * inv)
+        def parts(g, c, cols):
+            dhat = pay_ref[src[g], body(c, n)].astype(jnp.float32) * join3(extras[g], 2 * c + n)
+            return (dhat, ref[:, cols].astype(jnp.float32) * inv)
 
         total = jnp.zeros((TOK, HD), jnp.float32)
         for pair in pairs:
             dhat, hat = parts(*pair)
             total = total + dhat * hat
         mean = jnp.sum(total, axis=1, keepdims=True) * (1.0 / WIDTH)
-        for s in range(N_SEQ):
-            for pair in pairs[s * HEADS:(s + 1) * HEADS]:
-                dhat, hat = parts(*pair)
-                outs[n, :, pair[2]] = (inv * (dhat - hat * mean)).astype(jnp.bfloat16)
-            if s % 4 == 3:
-                cols = slice((s - 3) * HEADS * HD, (s + 1) * HEADS * HD)
-                copies.append(pltpu.make_async_copy(
-                    outs.at[n, :, cols], out_ref.at[:, cols], sems.at[2 + len(copies)]))
-                copies[-1].start()
+        for pair in pairs:
+            dhat, hat = parts(*pair)
+            outs[n, :, pair[2]] = (inv * (dhat - hat * mean)).astype(jnp.bfloat16)
+        send(n, out_ref)
     for copy in copies:
         copy.wait()
 
@@ -271,7 +268,8 @@
 def hold(x, after):
     return pl.pallas_call(
         hold_kernel, out_shape=shape(x.shape, jnp.float32),
-        in_specs=[HERE, HERE], out_specs=HERE, name="hold", cost_estimate=pl.CostEstimate(flops=1 << 36, bytes_accessed=1 << 27, transcendentals=0),
+        in_specs=[HERE, HERE], out_specs=HERE,
+        compiler_params=params(1), name="hold", cost_estimate=pl.CostEstimate(flops=1 << 36, bytes_accessed=1 << 27, transcendentals=0),
     )(x, after)
 
 
@@ -288,8 +286,9 @@
 SCALARS = pl.BlockSpec(memory_space=pltpu.SMEM)
 
 
-def swapped():
-    return [((b * 8 + i) * 8 + s, (s * 8 + i) * 8 + b) for b in range(8) for i in range(8) for s in range(8)]
+def around(way):
+    return [((b * 8 + i) * 8 + s, ((b + way * s) % 8 * 8 + i) * 8 + s)
+            for b in range(8) for i in range(8) for s in range(8)]
 
 
 def sum_four(x, axis, pairs):
@@ -328,7 +327,7 @@
         in_specs=[SCALARS, SCALARS, HERE, HERE, HERE], out_specs=[THERE, HERE],
         scratch_shapes=[half] * 4 + [turn] * 2 + [full] * 2 + [
             pltpu.VMEM(back.shape, jnp.bfloat16), pltpu.SemaphoreType.DMA((N_SEQ,))],
-        compiler_params=params(60), name="attend",
+        compiler_params=params(44), name="attend",
     )(lo, hi, got, gain, ids)
 
 
@@ -342,23 +341,23 @@
 
 def local(q_in, k_in, v_in, gain_q, gain_k, clip_ids):
     place = lax.axis_index("dp") % 8
+    turn = (lax.axis_index("dp") // 8).astype(jnp.int32)[None]
     inv = shape((TOK, HD), jnp.float32)
-    pair = pltpu.VMEM((2, TOK, WIDTH), jnp.bfloat16)
+    three = pltpu.VMEM((3, TOK, WIDTH), jnp.bfloat16)
 
     row = spread(jnp.stack([gain_q, gain_k]))[None]
     rows = jnp.where(lax.broadcasted_iota(jnp.int32, (8, HD), 0) == place, row, 0.0)
-    rows = over_z(rows)
 
     pay, inv_q, inv_k, mark = pl.pallas_call(
         pack_kernel,
         out_shape=[shape((N_SEQ, BODY + EXTRA, HD)), inv, inv, shape((8, HD), jnp.float32)],
-        in_specs=[THERE] * 3, out_specs=[THERE, HERE, HERE, HERE],
-        scratch_shapes=[pair, pltpu.VMEM((EXTRA, HD), jnp.bfloat16),
-                        pltpu.SemaphoreType.DMA((2 + 3 * H + N_SEQ,))],
+        in_specs=[SCALARS] + [THERE] * 3, out_specs=[THERE, HERE, HERE, HERE],
+        scratch_shapes=[three, pltpu.VMEM((EXTRA, HD), jnp.bfloat16),
+                        pltpu.SemaphoreType.DMA((3 + 3 * H + N_SEQ,))],
         compiler_params=params(62), name="pack",
-    )(q_in, k_in, v_in)
+    )(turn, q_in, k_in, v_in)
     got = lax.all_to_all(pay, "seq", 0, 0, tiled=True)
-    rows = lax.ppermute(over_y(hold(rows, mark)), ("dp", "seq"), swapped())
+    rows = lax.ppermute(over_y(over_z(hold(rows, mark))), ("dp", "seq"), around(-1))
     lo, hi = windows(clip_ids)
     pay, part = attend_call(lo, hi, got, rows, clip_ids)
 
@@ -368,15 +367,16 @@
     pay, part = lax.optimization_barrier((pay, part))
     got = lax.all_to_all(pay, "seq", 0, 0, tiled=True)
     part = hold(part, part)
-    part = over_x(over_core(lax.ppermute(part, ("dp", "seq"), swapped())))[0]
+    part = over_x(over_core(lax.ppermute(part, ("dp", "seq"), around(1))))[0]
 
     out = shape((TOK, WIDTH))
     d_q, d_k, d_v = pl.pallas_call(
         final_kernel, out_shape=[out] * 3,
-        in_specs=[THERE, THERE, HERE, HERE, HERE], out_specs=[THERE] * 3,
-        scratch_shapes=[pair, pair, pltpu.SemaphoreType.DMA((2 + H + 4,))],
-        compiler_params=params(61), name="final",
-    )(q_in, k_in, inv_q, inv_k, got)
+        in_specs=[SCALARS] + [HERE] * 5, out_specs=[THERE] * 3,
+        scratch_shapes=[three, pltpu.SemaphoreType.DMA((3,))],
+        compiler_params=params(16), name="final",
+        cost_estimate=pl.CostEstimate(flops=1 << 34, bytes_accessed=1 << 25, transcendentals=0),
+    )(turn, q_in, k_in, inv_q, inv_k, got)
     return (d_q, d_k, d_v, part[0:SHARD], part[64:64 + SHARD])
 
 

time: 193 us -> 112 us (0.58)
  Pallas kernels: 94.5 us -> 17.4 us
  other arithmetic: 3.47 us -> 0.42 us
  starting transfers between devices: 59.5 us -> 61.9 us
    pallas_call x1, Pallas kernels: 74 us -> 4.07 us  [local(): pl.pallas_call(pack_kernel, out_shape=[shape((N_SEQ, BODY + EXTRA, HD)),...]
    ppermute x2, starting transfers between devices: 6.68 us -> 13 us  [the longest x1 8.24 us: local(): lax.ppermute(over_y(over_z(hold(rows, mark))), ('dp', 'seq'), around(-1))]
    ppermute x6, starting transfers between devices: 28 us -> 22.4 us  [sum_four(): one, two, three = (lax.ppermute(x, axis, pairs(k)) for k in (1, 2, 3))]
    all_to_all x2, waiting for transfers between devices: 9.11 us -> 4.42 us  [local(): got = lax.all_to_all(pay, 'seq', 0, 0, tiled=True)]
    all_to_all x2, starting transfers between devices: 18.5 us -> 22.6 us  [local(): got = lax.all_to_all(pay, 'seq', 0, 0, tiled=True)]
    pallas_call x1, Pallas kernels: 5.89 us -> 2.79 us  [local(): pl.pallas_call(final_kernel, out_shape=[out] * 3, in_specs=[SCALARS] + [H...]
    ppermute x1, waiting for transfers between devices: 0.01 us -> 2.72 us  [over_z(): return x + lax.ppermute(x, 'dp', [(d, d ^ 4) for d in range(64)])]
    pallas_call x2, Pallas kernels: 2.55 us -> 0.01 us  [hold(): pl.pallas_call(hold_kernel, out_shape=shape(x.shape, jnp.float32), in_spe...]
  transfers between devices with their start and end apart: 12 -> 12, of which waited for: 7 -> 8; matrix products, arithmetic and copies ran while one was open for 2% -> 1% of each run, Pallas kernels for 40% -> 0%
where the time goes in v4:
time: 112 us; the launch traced here: 111 us
  starting transfers between devices  61.9 us (55%)
  waiting for transfers between devices  19.8 us (18%)
  Pallas kernels  17.4 us (16%)
  blocking collectives  7.36 us (7%)
  local copies, waits for them, and re-layouts  3.39 us (3%)
    all_to_all x2, starting transfers between devices, local(): got = lax.all_to_all(pay, 'seq', 0, 0, tiled=True)  22.6 us
    ppermute x6, starting transfers between devices, sum_four(): one, two, three = (lax.ppermute(x, axis, pairs(k)) for k in (1, 2, 3))  22.4 us
    pallas_call x1, Pallas kernels, attend_call(): pl.pallas_call(attend_kernel, out_shape=[back, shape((8, HD), jnp.float32...  10.6 us
    ppermute x1, starting transfers between devices, local(): lax.ppermute(over_y(over_z(hold(rows, mark))), ('dp', 'seq'), around(-1))  8.24 us
    all_to_all x1, blocking collectives, local(): lax.all_to_all(part, 'dp', 0, 0, axis_index_groups=blocks, tiled=True)  7.36 us
    ppermute x1, waiting for transfers between devices, local(): part = over_x(over_core(lax.ppermute(part, ('dp', 'seq'), around(1))))[0]  6.27 us
    ppermute x6, waiting for transfers between devices, sum_four(): one, two, three = (lax.ppermute(x, axis, pairs(k)) for k in (1, 2, 3))  4.81 us
    ppermute x1, starting transfers between devices, local(): part = over_x(over_core(lax.ppermute(part, ('dp', 'seq'), around(1))))[0]  4.73 us
  transfers between devices with their start and end apart: 12, of which 8 were waited for; matrix products, arithmetic and copies ran while one was open for 1% of the time, Pallas kernels for 0%

profile of v4, /device:TPU:1, one launch (start us, length us, event | category | flops | bytes accessed | tf_op | source)
XLA Modules:
  0.0 111.2 jit_solution(13786634330305300329)
XLA Ops:
  0.6 4.1 %pack.1 = (bf16[8,1168,128]{2,1,0:T(8,128)(2,1)}, f32[128,128]{1,0:T(8,128)}, f32[128,128]{1,0:T(8,128)}, f32[8,128]{1,0:T(8,128)}) custom-call(s32[1]{0:T(128)} %bitcast.turn_ref, bf16[128,3072]{1,0:T(8,128)(2,1)} %q_ref.3, bf16[128,3072]{1,0:T(8,128)(2,1)} %k_ref.3, bf16[128,3072]{1,0:T(8,128)(2,1)} %v_ref.1), custom_call_target="tpu_custom_call" | custom-call | tf_op jit(solution)/shard_map/pack/pallas_call | solution.py:351
  4.7 0.0 copy-start.7
  4.7 0.0 copy-start.8
  4.7 0.0 copy-start.6
  4.8 10.5 %all-to-all-start = ((bf16[8,1168,128]{2,1,0:T(8,128)(2,1)}), bf16[8,1168,128]{2,1,0:T(8,128)(2,1)S(1)}, u32[]{:S(2)}, u32[]{:S(2)}) async-start(bf16[8,1168,128]{2,1,0:T(8,128)(2,1)} %get-tuple-element.18), calls=%async_computation | async-start | bytes 4784128 | tf_op jit(solution)/shard_map/all_to_all | solution.py:359
  15.3 0.0 copy-done.7
  15.3 0.0 copy-done.8
  15.3 0.1 pad_maximum_fusion
  15.4 0.1 broadcast_select_fusion.x_ref
  15.5 0.0 copy-done.6
  15.5 2.0 %collective-permute-start = (f32[8,128]{1,0:T(8,128)S(1)}, f32[8,128]{1,0:T(8,128)S(1)}, u32[]{:S(2)}, u32[]{:S(2)}) collective-permute-start(f32[8,128]{1,0:T(8,128)S(1)} %hold.2), channel_id=1, source_target_pairs={{0,32},{8,40},{16,48},{24,56},{32,0},{40,8},{48,16},{56,24},{64,96... | collective-permute-start | bytes 12296 | tf_op jit(solution)/shard_map/ppermute | solution.py:300
  17.5 2.7 %collective-permute-done = f32[8,128]{1,0:T(8,128)S(1)} collective-permute-done((f32[8,128]{1,0:T(8,128)S(1)}, f32[8,128]{1,0:T(8,128)S(1)}, u32[]{:S(2)}, u32[]{:S(2)}) %collective-permute-start) | collective-permute-done | bytes 4128 | tf_op jit(solution)/shard_map/ppermute | solution.py:300
  20.3 1.9 %collective-permute-start.3 = (f32[8,128]{1,0:T(8,128)S(1)}, f32[8,128]{1,0:T(8,128)S(1)}, u32[]{:S(2)}, u32[]{:S(2)}) collective-permute-start(f32[8,128]{1,0:T(8,128)S(1)} %add.30), channel_id=1, source_target_pairs={{0,24},{8,0},{16,8},{24,16},{32,56},{40,32},{48,40},{56,48},{64,88... | collective-permute-start | bytes 12296 | tf_op jit(solution)/shard_map/ppermute | solution.py:295
  22.2 3.4 %collective-permute-start.2 = (f32[8,128]{1,0:T(8,128)S(1)}, f32[8,128]{1,0:T(8,128)S(1)}, u32[]{:S(2)}, u32[]{:S(2)}) collective-permute-start(f32[8,128]{1,0:T(8,128)S(1)} %add.30), channel_id=1, source_target_pairs={{0,8},{8,16},{16,24},{24,0},{32,40},{40,48},{48,56},{56,32},{64,72... | collective-permute-start | bytes 12296 | tf_op jit(solution)/shard_map/ppermute | solution.py:295
  25.6 1.9 %collective-permute-start.1 = (f32[8,128]{1,0:T(8,128)S(1)}, f32[8,128]{1,0:T(8,128)S(1)}, u32[]{:S(2)}, u32[]{:S(2)}) collective-permute-start(f32[8,128]{1,0:T(8,128)S(1)} %add.30), channel_id=1, source_target_pairs={{0,16},{8,24},{16,0},{24,8},{32,48},{40,56},{48,32},{56,40},{64,80... | collective-permute-start | bytes 12296 | tf_op jit(solution)/shard_map/ppermute | solution.py:295
  27.5 0.0 copy-done.3
  27.5 0.1 slice.18
  27.6 0.1 slice.19
  27.7 0.0 collective-permute-done.3
  27.7 0.1 collective-permute-done.2
  27.7 3.7 %collective-permute-done.1 = f32[8,128]{1,0:T(8,128)S(1)} collective-permute-done((f32[8,128]{1,0:T(8,128)S(1)}, f32[8,128]{1,0:T(8,128)S(1)}, u32[]{:S(2)}, u32[]{:S(2)}) %collective-permute-start.1) | collective-permute-done | bytes 4128 | tf_op jit(solution)/shard_map/ppermute | solution.py:295
  31.4 8.2 %collective-permute-start.4 = (f32[8,128]{1,0:T(8,128)S(1)}, f32[8,128]{1,0:T(8,128)S(1)}, u32[]{:S(2)}, u32[]{:S(2)}) collective-permute-start(f32[8,128]{1,0:T(8,128)S(1)} %add_add_fusion), channel_id=1, source_target_pairs={{0,0},{1,449},{2,386},{3,323},{4,260},{5,197},{6,134},{7,71},{8,8}... | collective-permute-start | bytes 12296 | tf_op jit(solution)/shard_map/ppermute | solution.py:360
  39.7 0.2 convert_reduce_fusion
  39.9 0.5 collective-permute-done.4.gain_ref
  40.4 4.4 %all-to-all-done.pay_ref = bf16[8,1168,128]{2,1,0:T(8,128)(2,1)S(1)} async-done(((bf16[8,1168,128]{2,1,0:T(8,128)(2,1)}), bf16[8,1168,128]{2,1,0:T(8,128)(2,1)S(1)}, u32[]{:S(2)}, u32[]{:S(2)}) %all-to-all-start) | async-done | bytes 2392096 | tf_op jit(solution)/shard_map/all_to_all | solution.py:359
  44.8 10.6 %attend.1 = (bf16[8,1184,128]{2,1,0:T(8,128)(2,1)S(1)}, f32[8,128]{1,0:T(8,128)S(1)}) custom-call(s32[4]{0:T(128)S(1)} %get-tuple-element.28.lo_ref, s32[4]{0:T(128)S(1)} %get-tuple-element.27.hi_ref, bf16[8,1168,128]{2,1,0:T(8,128)(2,1)S(1)} %all-to-all-done.pay_ref, f32[8,128]{1,0:T(8,128)S(1)} %collective-permute-done.4.gain_ref, s32[1,1024]{1,0:T(1,128)S(1)} %copy-done.3), custom_call_target="tpu_custom_call" | custom-call | tf_op jit(solution)/shard_map/attend/pallas_call | solution.py:325
  55.4 0.0 copy-start
  55.4 1.5 %copy-done = bf16[8,1184,128]{2,1,0:T(8,128)(2,1)} copy-done((bf16[8,1184,128]{2,1,0:T(8,128)(2,1)}, bf16[8,1184,128]{2,1,0:T(8,128)(2,1)S(1)}, u32[]{:S(2)}) %copy-start) | copy-done | bytes 2424856
  56.9 7.4 %all_to_all.19 = f32[8,1,128]{2,1,0:T(1,128)S(1)} all-to-all(f32[8,1,128]{2,1,0:T(1,128)S(1)} %bitcast.13), channel_id=1, replica_groups={{0,8,16,24,32,40,48,56},{64,72,80,88,96,104,112,120},{128,136,144,152,1..., dimensions={0} | all-to-all | bytes 8192 | tf_op jit(solution)/shard_map/all_to_all | solution.py:365
  64.2 12.0 %all-to-all-start.2 = ((bf16[8,1184,128]{2,1,0:T(8,128)(2,1)}), bf16[8,1184,128]{2,1,0:T(8,128)(2,1)S(1)}, u32[]{:S(2)}, u32[]{:S(2)}) async-start(bf16[8,1184,128]{2,1,0:T(8,128)(2,1)} %copy-done), calls=%async_computation.2 | async-start | bytes 4849664 | tf_op jit(solution)/shard_map/all_to_all | solution.py:368
  76.3 4.7 %collective-permute-start.5 = (f32[1,128]{1,0:T(1,128)S(1)}, f32[1,128]{1,0:T(1,128)S(1)}, u32[]{:S(2)}, u32[]{:S(2)}) collective-permute-start(f32[1,128]{1,0:T(1,128)S(1)} %hold.3), channel_id=1, source_target_pairs={{0,0},{1,65},{2,130},{3,195},{4,260},{5,325},{6,390},{7,455},{8,8}... | collective-permute-start | bytes 1544 | tf_op jit(solution)/shard_map/ppermute | solution.py:370
  81.0 6.3 %collective-permute-done.5 = f32[1,128]{1,0:T(1,128)S(1)} collective-permute-done((f32[1,128]{1,0:T(1,128)S(1)}, f32[1,128]{1,0:T(1,128)S(1)}, u32[]{:S(2)}, u32[]{:S(2)}) %collective-permute-start.5) | collective-permute-done | bytes 544 | tf_op jit(solution)/shard_map/ppermute | solution.py:370
  87.3 1.9 %collective-permute-start.6 = (f32[1,128]{1,0:T(1,128)S(1)}, f32[1,128]{1,0:T(1,128)S(1)}, u32[]{:S(2)}, u32[]{:S(2)}) collective-permute-start(f32[1,128]{1,0:T(1,128)S(1)} %collective-permute-done.5), channel_id=1, source_target_pairs={{0,1},{1,0},{2,3},{3,2},{4,5},{5,4},{6,7},{7,6},{8,9},{9,8},{10,11... | collective-permute-start | bytes 1544 | tf_op jit(solution)/shard_map/ppermute | solution.py:308
  89.2 1.1 collective-permute-done.6
  90.3 6.3 %collective-permute-start.9 = (f32[1,128]{1,0:T(1,128)S(1)}, f32[1,128]{1,0:T(1,128)S(1)}, u32[]{:S(2)}, u32[]{:S(2)}) collective-permute-start(f32[1,128]{1,0:T(1,128)S(1)} %add.34), channel_id=1, source_target_pairs={{0,6},{1,7},{2,0},{3,1},{4,2},{5,3},{6,4},{7,5},{8,14},{9,15},{10,... | collective-permute-start | bytes 1544 | tf_op jit(solution)/shard_map/ppermute | solution.py:295
  96.6 1.9 %collective-permute-start.8 = (f32[1,128]{1,0:T(1,128)S(1)}, f32[1,128]{1,0:T(1,128)S(1)}, u32[]{:S(2)}, u32[]{:S(2)}) collective-permute-start(f32[1,128]{1,0:T(1,128)S(1)} %add.34), channel_id=1, source_target_pairs={{0,2},{1,3},{2,4},{3,5},{4,6},{5,7},{6,0},{7,1},{8,10},{9,11},{10,... | collective-permute-start | bytes 1544 | tf_op jit(solution)/shard_map/ppermute | solution.py:295
  98.5 7.0 %collective-permute-start.7 = (f32[1,128]{1,0:T(1,128)S(1)}, f32[1,128]{1,0:T(1,128)S(1)}, u32[]{:S(2)}, u32[]{:S(2)}) collective-permute-start(f32[1,128]{1,0:T(1,128)S(1)} %add.34), channel_id=1, source_target_pairs={{0,4},{1,5},{2,6},{3,7},{4,0},{5,1},{6,2},{7,3},{8,12},{9,13},{10,... | collective-permute-start | bytes 1544 | tf_op jit(solution)/shard_map/ppermute | solution.py:295
  105.5 0.0 collective-permute-done.9
  105.5 0.0 collective-permute-done.8
  105.5 1.1 collective-permute-done.7
  106.6 0.6 slice_bitcast_fusion
  107.2 0.0 all-to-all-done.2.pay_ref
  107.2 0.0 copy-done.1
  107.2 0.0 copy-done.4
  107.2 0.0 copy-done.5
  107.2 0.0 copy-start.2
  107.2 1.1 %copy-done.2 = bf16[128,3072]{1,0:T(8,128)(2,1)S(1)} copy-done((bf16[128,3072]{1,0:T(8,128)(2,1)S(1)}, bf16[128,3072]{1,0:T(8,128)(2,1)}, u32[]{:S(2)}) %copy-start.2) | copy-done | bytes 786456
  108.4 2.8 %final.1 = (bf16[128,3072]{1,0:T(8,128)(2,1)}, bf16[128,3072]{1,0:T(8,128)(2,1)}, bf16[128,3072]{1,0:T(8,128)(2,1)}) custom-call(s32[1]{0:T(128)} %bitcast.turn_ref, bf16[128,3072]{1,0:T(8,128)(2,1)S(1)} %copy-done.1, bf16[128,3072]{1,0:T(8,128)(2,1)S(1)} %copy-done.2, f32[128,128]{1,0:T(8,128)S(1)} %copy-done.4, f32[128,128]{1,0:T(8,128)S(1)} %copy-done.5, ...), custom_call_target="tpu_custom_call" | custom-call | flops 17179869184 | bytes 33554432 | tf_op jit(solution)/shard_map/final/pallas_call | solution.py:373
  (13 shorter events, 0.1 us)
Async XLA Ops:
  4.7 10.6 %copy-start.7 = (f32[48]{0:T(128)S(1)}, f32[48]{0:T(128)}, u32[]{:S(2)}) copy-start(f32[48]{0:T(128)} %param.10) | copy-start | bytes 580
  4.7 10.6 %copy-start.8 = (f32[48]{0:T(128)S(1)}, f32[48]{0:T(128)}, u32[]{:S(2)}) copy-start(f32[48]{0:T(128)} %param.9) | copy-start | bytes 580
  4.7 10.7 %copy-start.6 = (f32[8,128]{1,0:T(8,128)S(1)}, f32[8,128]{1,0:T(8,128)}, u32[]{:S(2)}) copy-start(f32[8,128]{1,0:T(8,128)} %get-tuple-element.19.after_ref) | copy-start | bytes 12292
  4.8 40.1 %all-to-all-start = ((bf16[8,1168,128]{2,1,0:T(8,128)(2,1)}), bf16[8,1168,128]{2,1,0:T(8,128)(2,1)S(1)}, u32[]{:S(2)}, u32[]{:S(2)}) async-start(bf16[8,1168,128]{2,1,0:T(8,128)(2,1)} %get-tuple-element.18), calls=%async_computation | async-start | bytes 4784128 | tf_op jit(solution)/shard_map/all_to_all | solution.py:359
  15.5 12.0 %copy-start.3 = (s32[1,1024]{1,0:T(1,128)S(1)}, s32[1,1024]{1,0:T(1,128)}, u32[]{:S(2)}) copy-start(s32[1,1024]{1,0:T(1,128)} %ids_ref.1) | copy-start | bytes 12292
  15.5 4.8 %collective-permute-start = (f32[8,128]{1,0:T(8,128)S(1)}, f32[8,128]{1,0:T(8,128)S(1)}, u32[]{:S(2)}, u32[]{:S(2)}) collective-permute-start(f32[8,128]{1,0:T(8,128)S(1)} %hold.2), channel_id=1, source_target_pairs={{0,32},{8,40},{16,48},{24,56},{32,0},{40,8},{48,16},{56,24},{64,96... | collective-permute-start | bytes 12296 | tf_op jit(solution)/shard_map/ppermute | solution.py:300
  20.3 7.4 %collective-permute-start.3 = (f32[8,128]{1,0:T(8,128)S(1)}, f32[8,128]{1,0:T(8,128)S(1)}, u32[]{:S(2)}, u32[]{:S(2)}) collective-permute-start(f32[8,128]{1,0:T(8,128)S(1)} %add.30), channel_id=1, source_target_pairs={{0,24},{8,0},{16,8},{24,16},{32,56},{40,32},{48,40},{56,48},{64,88... | collective-permute-start | bytes 12296 | tf_op jit(solution)/shard_map/ppermute | solution.py:295
  22.2 5.6 %collective-permute-start.2 = (f32[8,128]{1,0:T(8,128)S(1)}, f32[8,128]{1,0:T(8,128)S(1)}, u32[]{:S(2)}, u32[]{:S(2)}) collective-permute-start(f32[8,128]{1,0:T(8,128)S(1)} %add.30), channel_id=1, source_target_pairs={{0,8},{8,16},{16,24},{24,0},{32,40},{40,48},{48,56},{56,32},{64,72... | collective-permute-start | bytes 12296 | tf_op jit(solution)/shard_map/ppermute | solution.py:295
  25.6 5.9 %collective-permute-start.1 = (f32[8,128]{1,0:T(8,128)S(1)}, f32[8,128]{1,0:T(8,128)S(1)}, u32[]{:S(2)}, u32[]{:S(2)}) collective-permute-start(f32[8,128]{1,0:T(8,128)S(1)} %add.30), channel_id=1, source_target_pairs={{0,16},{8,24},{16,0},{24,8},{32,48},{40,56},{48,32},{56,40},{64,80... | collective-permute-start | bytes 12296 | tf_op jit(solution)/shard_map/ppermute | solution.py:295
  31.4 9.0 %collective-permute-start.4 = (f32[8,128]{1,0:T(8,128)S(1)}, f32[8,128]{1,0:T(8,128)S(1)}, u32[]{:S(2)}, u32[]{:S(2)}) collective-permute-start(f32[8,128]{1,0:T(8,128)S(1)} %add_add_fusion), channel_id=1, source_target_pairs={{0,0},{1,449},{2,386},{3,323},{4,260},{5,197},{6,134},{7,71},{8,8}... | collective-permute-start | bytes 12296 | tf_op jit(solution)/shard_map/ppermute | solution.py:360
  55.4 1.5 %copy-start = (bf16[8,1184,128]{2,1,0:T(8,128)(2,1)}, bf16[8,1184,128]{2,1,0:T(8,128)(2,1)S(1)}, u32[]{:S(2)}) copy-start(bf16[8,1184,128]{2,1,0:T(8,128)(2,1)S(1)} %get-tuple-element.22) | copy-start | bytes 7274500
  64.2 43.0 %all-to-all-start.2 = ((bf16[8,1184,128]{2,1,0:T(8,128)(2,1)}), bf16[8,1184,128]{2,1,0:T(8,128)(2,1)S(1)}, u32[]{:S(2)}, u32[]{:S(2)}) async-start(bf16[8,1184,128]{2,1,0:T(8,128)(2,1)} %copy-done), calls=%async_computation.2 | async-start | bytes 4849664 | tf_op jit(solution)/shard_map/all_to_all | solution.py:368
  76.3 30.9 %copy-start.1 = (bf16[128,3072]{1,0:T(8,128)(2,1)S(1)}, bf16[128,3072]{1,0:T(8,128)(2,1)}, u32[]{:S(2)}) copy-start(bf16[128,3072]{1,0:T(8,128)(2,1)} %q_ref.3) | copy-start | bytes 2359300
  76.3 30.9 %copy-start.4 = (f32[128,128]{1,0:T(8,128)S(1)}, f32[128,128]{1,0:T(8,128)}, u32[]{:S(2)}) copy-start(f32[128,128]{1,0:T(8,128)} %get-tuple-element.16.inv_q_ref) | copy-start | bytes 196612
  76.3 30.9 %copy-start.5 = (f32[128,128]{1,0:T(8,128)S(1)}, f32[128,128]{1,0:T(8,128)}, u32[]{:S(2)}) copy-start(f32[128,128]{1,0:T(8,128)} %get-tuple-element.17.inv_k_ref) | copy-start | bytes 196612
  76.3 11.0 %collective-permute-start.5 = (f32[1,128]{1,0:T(1,128)S(1)}, f32[1,128]{1,0:T(1,128)S(1)}, u32[]{:S(2)}, u32[]{:S(2)}) collective-permute-start(f32[1,128]{1,0:T(1,128)S(1)} %hold.3), channel_id=1, source_target_pairs={{0,0},{1,65},{2,130},{3,195},{4,260},{5,325},{6,390},{7,455},{8,8}... | collective-permute-start | bytes 1544 | tf_op jit(solution)/shard_map/ppermute | solution.py:370
  87.3 3.0 %collective-permute-start.6 = (f32[1,128]{1,0:T(1,128)S(1)}, f32[1,128]{1,0:T(1,128)S(1)}, u32[]{:S(2)}, u32[]{:S(2)}) collective-permute-start(f32[1,128]{1,0:T(1,128)S(1)} %collective-permute-done.5), channel_id=1, source_target_pairs={{0,1},{1,0},{2,3},{3,2},{4,5},{5,4},{6,7},{7,6},{8,9},{9,8},{10,11... | collective-permute-start | bytes 1544 | tf_op jit(solution)/shard_map/ppermute | solution.py:308
  90.3 15.2 %collective-permute-start.9 = (f32[1,128]{1,0:T(1,128)S(1)}, f32[1,128]{1,0:T(1,128)S(1)}, u32[]{:S(2)}, u32[]{:S(2)}) collective-permute-start(f32[1,128]{1,0:T(1,128)S(1)} %add.34), channel_id=1, source_target_pairs={{0,6},{1,7},{2,0},{3,1},{4,2},{5,3},{6,4},{7,5},{8,14},{9,15},{10,... | collective-permute-start | bytes 1544 | tf_op jit(solution)/shard_map/ppermute | solution.py:295
  96.6 8.9 %collective-permute-start.8 = (f32[1,128]{1,0:T(1,128)S(1)}, f32[1,128]{1,0:T(1,128)S(1)}, u32[]{:S(2)}, u32[]{:S(2)}) collective-permute-start(f32[1,128]{1,0:T(1,128)S(1)} %add.34), channel_id=1, source_target_pairs={{0,2},{1,3},{2,4},{3,5},{4,6},{5,7},{6,0},{7,1},{8,10},{9,11},{10,... | collective-permute-start | bytes 1544 | tf_op jit(solution)/shard_map/ppermute | solution.py:295
  98.5 8.1 %collective-permute-start.7 = (f32[1,128]{1,0:T(1,128)S(1)}, f32[1,128]{1,0:T(1,128)S(1)}, u32[]{:S(2)}, u32[]{:S(2)}) collective-permute-start(f32[1,128]{1,0:T(1,128)S(1)} %add.34), channel_id=1, source_target_pairs={{0,4},{1,5},{2,6},{3,7},{4,0},{5,1},{6,2},{7,3},{8,12},{9,13},{10,... | collective-permute-start | bytes 1544 | tf_op jit(solution)/shard_map/ppermute | solution.py:295
  107.2 1.1 %copy-start.2 = (bf16[128,3072]{1,0:T(8,128)(2,1)S(1)}, bf16[128,3072]{1,0:T(8,128)(2,1)}, u32[]{:S(2)}) copy-start(bf16[128,3072]{1,0:T(8,128)(2,1)} %k_ref.3) | copy-start | bytes 2359300

commit v5 on v4

--- a/solution.py
+++ b/solution.py
@@ -13,13 +13,15 @@
 G = TOK * N_SEQ
 WIDTH = H * HD
 BQ = 256
-WINDOWS = (512, 640, 768, 1024)
+PAIR = 1
+WINDOWS = (384, 512, 640, 768, 896, 1024)
 EXTRA = 16
 BODY = 3 * TOK * HEADS
 EPS = 1e-06
 SCALE = HD ** (-0.5)
 LOG2E = 1.4426950408889634
 SHARD = 48
+CUTS = 4
 
 
 def split3(x):
@@ -49,20 +51,22 @@
     return slice((c * 3 + n) * TOK, (c * 3 + n + 1) * TOK)
 
 
-def pack_kernel(turn_ref, q_ref, k_ref, v_ref, pay_ref, inv_q_ref, inv_k_ref, mark_ref, held, extra, sems):
+def pack_kernel(turn_ref, q_ref, k_ref, v_ref, pay_ref, inv_q_ref, inv_k_ref, mark_ref, held, extra, load_sems, sems):
+    wide = WIDTH // CUTS
     loads = []
-    for n, ref in enumerate((q_ref, k_ref, v_ref)):
-        loads.append(pltpu.make_async_copy(ref, held.at[n], sems.at[n]))
-        loads[n].start()
-    dest = [(g + N_SEQ - turn_ref[0]) % N_SEQ for g in range(N_SEQ)]
+    for t in range(CUTS):
+        cols = slice(t * wide, (t + 1) * wide)
+        for n, ref in enumerate((q_ref, k_ref, v_ref)):
+            loads.append(pltpu.make_async_copy(ref.at[:, cols], held.at[n, :, cols], load_sems.at[len(loads)]))
+            loads[-1].start()
     copies = []
-    for n in range(3):
-        loads[n].wait()
-        for g in range(N_SEQ):
-            for c in range(HEADS):
-                h = g * HEADS + c
+    for t in range(CUTS):
+        for n in range(3):
+            loads[3 * t + n].wait()
+            for h in range(t * H // CUTS, (t + 1) * H // CUTS):
+                dest = (h // HEADS + N_SEQ - turn_ref[0]) % N_SEQ
                 copies.append(pltpu.make_async_copy(
-                    held.at[n, :, h * HD:(h + 1) * HD], pay_ref.at[dest[g], body(c, n)], sems.at[3 + len(copies)]))
+                    held.at[n, :, h * HD:(h + 1) * HD], pay_ref.at[dest, body(h % HEADS, n)], sems.at[len(copies)]))
                 copies[-1].start()
     rows = []
     for n, inv_ref in enumerate((inv_q_ref, inv_k_ref)):
@@ -77,7 +81,7 @@
     mark_ref[...] = jnp.zeros_like(mark_ref)
     extra[...] = extra_rows(rows, EXTRA)
     for s in range(N_SEQ):
-        copies.append(pltpu.make_async_copy(extra, pay_ref.at[s, BODY:], sems.at[3 + len(copies)]))
+        copies.append(pltpu.make_async_copy(extra, pay_ref.at[s, BODY:], sems.at[len(copies)]))
         copies[-1].start()
     for copy in copies:
         copy.wait()
@@ -146,52 +150,58 @@
     acc_k[...] = jnp.zeros_like(acc_k)
     acc_v[...] = jnp.zeros_like(acc_v)
 
-    def block(b, first, width):
-        first = pl.multiple_of(first, TOK)
-        rows = pl.ds(pl.multiple_of(b * BQ, BQ), BQ)
-        keys = pl.ds(first, width)
-        own = [column(ids_ref[:, pl.ds(pl.multiple_of(b * BQ + t, HD), HD)])[:, 0:1] for t in range(0, BQ, HD)]
-        same = jnp.concatenate(own, axis=0) == ids_ref[:, keys]
-        qb = [qn[c, rows] for c in range(HEADS)]
-        kb = [kn[c, keys] for c in range(HEADS)]
-        vb = [vv[c, keys] for c in range(HEADS)]
+    def blocks(b, first, width):
+        units = [(t, c) for t in range(PAIR) for c in range(HEADS)]
+        start = [pl.multiple_of(f, TOK) for f in first]
+        rows = [pl.ds(pl.multiple_of((b * PAIR + t) * BQ, BQ), BQ) for t in range(PAIR)]
+        keys = [pl.ds(f, width) for f in start]
+        same = []
+        for t in range(PAIR):
+            own = [column(ids_ref[:, pl.ds(pl.multiple_of((b * PAIR + t) * BQ + r, HD), HD)])[:, 0:1]
+                   for r in range(0, BQ, HD)]
+            same.append(jnp.concatenate(own, axis=0) == ids_ref[:, keys[t]])
+        qb = {(t, c): qn[c, rows[t]] for t, c in units}
+        kb = {(t, c): kn[c, keys[t]] for t, c in units}
+        vb = {(t, c): vv[c, keys[t]] for t, c in units}
         val = {}
 
-        def score(c):
-            val["s", c] = nt(qb[c], kb[c])
-
-        def soft(c):
-            s = jnp.where(same, val["s", c], -1e30)
+        def score(u):
+            val["s", u] = nt(qb[u], kb[u])
+
+        def soft(u):
+            s = jnp.where(same[u[0]], val["s", u], -1e30)
             top = jnp.max(s, axis=1, keepdims=True)
             e = jnp.exp2((s - top) * (SCALE * LOG2E))
-            val["p", c] = e * (1.0 / jnp.sum(e, axis=1, keepdims=True))
-            val["pb", c] = val["p", c].astype(jnp.bfloat16)
-
-        def mix(c):
-            val["a", c] = nn(val["pb", c], vb[c]).astype(jnp.bfloat16)
-
-        def back(c):
-            val["dp", c] = nt(val["a", c], vb[c])
-
-        def less(c):
-            p, dp = val["p", c], val["dp", c]
+            val["p", u] = e * (1.0 / jnp.sum(e, axis=1, keepdims=True))
+            val["pb", u] = val["p", u].astype(jnp.bfloat16)
+
+        def mix(u):
+            val["a", u] = nn(val["pb", u], vb[u]).astype(jnp.bfloat16)
+
+        def back(u):
+            val["dp", u] = nt(val["a", u], vb[u])
+
+        def less(u):
+            p, dp = val["p", u], val["dp", u]
             delta = jnp.sum(p * dp, axis=1, keepdims=True)
-            val["ds", c] = (p * (dp - delta) * SCALE).astype(jnp.bfloat16)
-
-        def values(c):
-            acc_v[c, :, keys] += nn(jnp.transpose(val["a", c]), val["pb", c])
-
-        def grads(c):
-            dq[c, rows] = nn(val["ds", c], kb[c]).astype(jnp.bfloat16)
-            acc_k[c, :, keys] += nn(jnp.transpose(qb[c]), val["ds", c])
+            val["ds", u] = (p * (dp - delta) * SCALE).astype(jnp.bfloat16)
+
+        def values(u):
+            acc_v[u[1], :, keys[u[0]]] += nn(jnp.transpose(val["a", u]), val["pb", u])
+
+        def grads(u):
+            dq[u[1], rows[u[0]]] = nn(val["ds", u], kb[u]).astype(jnp.bfloat16)
+            acc_k[u[1], :, keys[u[0]]] += nn(jnp.transpose(qb[u]), val["ds", u])
 
         for stage in (score, soft, mix, back, less, values, grads):
-            for c in range(HEADS):
-                stage(c)
+            for u in units:
+                stage(u)
 
     def step(b, carry):
-        low = lo_ref[b] // TOK * TOK
-        span = hi_ref[b] - low
+        low = [lo_ref[b * PAIR + t] // TOK * TOK for t in range(PAIR)]
+        span = hi_ref[b * PAIR] - low[0]
+        for t in range(1, PAIR):
+            span = jnp.maximum(span, hi_ref[b * PAIR + t] - low[t])
         done = None
         for width in WINDOWS:
             fits = span <= width
@@ -200,10 +210,10 @@
 
             @pl.when(now)
             def _():
-                block(b, jnp.minimum(low, G - width), width)
+                blocks(b, [jnp.minimum(f, G - width) for f in low], width)
         return carry
 
-    lax.fori_loop(0, G // BQ, step, 0)
+    lax.fori_loop(0, G // BQ // PAIR, step, 0)
 
     copies = []
     for j in range(N_SEQ):
@@ -353,11 +363,11 @@
         out_shape=[shape((N_SEQ, BODY + EXTRA, HD)), inv, inv, shape((8, HD), jnp.float32)],
         in_specs=[SCALARS] + [THERE] * 3, out_specs=[THERE, HERE, HERE, HERE],
         scratch_shapes=[three, pltpu.VMEM((EXTRA, HD), jnp.bfloat16),
-                        pltpu.SemaphoreType.DMA((3 + 3 * H + N_SEQ,))],
+                        pltpu.SemaphoreType.DMA((3 * CUTS,)), pltpu.SemaphoreType.DMA((3 * H + N_SEQ,))],
         compiler_params=params(62), name="pack",
     )(turn, q_in, k_in, v_in)
     got = lax.all_to_all(pay, "seq", 0, 0, tiled=True)
-    rows = lax.ppermute(over_y(over_z(hold(rows, mark))), ("dp", "seq"), around(-1))
+    rows = lax.ppermute(over_y(hold(over_z(rows), mark)), ("dp", "seq"), around(-1))
     lo, hi = windows(clip_ids)
     pay, part = attend_call(lo, hi, got, rows, clip_ids)
 

time: 112 us -> 111 us (level)
  starting transfers between devices: 61.9 us -> 57.1 us
  Pallas kernels: 17.4 us -> 19.8 us
    all_to_all x2, starting transfers between devices: 22.6 us -> 14.1 us  [local(): got = lax.all_to_all(pay, 'seq', 0, 0, tiled=True)]
    all_to_all x2, waiting for transfers between devices: 4.42 us -> 8.16 us  [local(): got = lax.all_to_all(pay, 'seq', 0, 0, tiled=True)]
    ppermute x1, waiting for transfers between devices: 2.72 us -> 0.01 us  [over_z(): return x + lax.ppermute(x, 'dp', [(d, d ^ 4) for d in range(64)])]
    ppermute x1, starting transfers between devices: 2.04 us -> 4.36 us  [over_z(): return x + lax.ppermute(x, 'dp', [(d, d ^ 4) for d in range(64)])]
    pallas_call x1, Pallas kernels: 10.6 us -> 12.8 us  [attend_call(): pl.pallas_call(attend_kernel, out_shape=[back, shape((8, HD), jnp.float32...]
    ppermute x6, starting transfers between devices: 22.4 us -> 24.3 us  [sum_four(): one, two, three = (lax.ppermute(x, axis, pairs(k)) for k in (1, 2, 3))]
    ppermute x1, starting transfers between devices: 4.73 us -> 3.21 us  [local(): part = over_x(over_core(lax.ppermute(part, ('dp', 'seq'), around(1))))[0]]
    ppermute x1, waiting for transfers between devices: 6.27 us -> 5.09 us  [local(): part = over_x(over_core(lax.ppermute(part, ('dp', 'seq'), around(1))))[0]]
  transfers between devices with their start and end apart: 12 -> 12, of which waited for: 8 -> 8; matrix products, arithmetic and copies ran while one was open for 1% -> 1% of each run, Pallas kernels for 0% -> 4%
where the time goes in v5:
time: 111 us; the launch traced here: 110 us
  starting transfers between devices  57.1 us (51%)
  waiting for transfers between devices  20.2 us (18%)
  Pallas kernels  19.8 us (18%)
  blocking collectives  7.77 us (7%)
  local copies, waits for them, and re-layouts  3.37 us (3%)
  other arithmetic  1.16 us (1%)
    ppermute x6, starting transfers between devices, sum_four(): one, two, three = (lax.ppermute(x, axis, pairs(k)) for k in (1, 2, 3))  24.3 us
    all_to_all x2, starting transfers between devices, local(): got = lax.all_to_all(pay, 'seq', 0, 0, tiled=True)  14.1 us
    pallas_call x1, Pallas kernels, attend_call(): pl.pallas_call(attend_kernel, out_shape=[back, shape((8, HD), jnp.float32...  12.8 us
    ppermute x1, starting transfers between devices, local(): lax.ppermute(over_y(hold(over_z(rows), mark)), ('dp', 'seq'), around(-1))  9.21 us
    all_to_all x2, waiting for transfers between devices, local(): got = lax.all_to_all(pay, 'seq', 0, 0, tiled=True)  8.16 us
    all_to_all x1, blocking collectives, local(): lax.all_to_all(part, 'dp', 0, 0, axis_index_groups=blocks, tiled=True)  7.77 us
    ppermute x6, waiting for transfers between devices, sum_four(): one, two, three = (lax.ppermute(x, axis, pairs(k)) for k in (1, 2, 3))  5.32 us
    ppermute x1, waiting for transfers between devices, local(): part = over_x(over_core(lax.ppermute(part, ('dp', 'seq'), around(1))))[0]  5.09 us
  transfers between devices with their start and end apart: 12, of which 8 were waited for; matrix products, arithmetic and copies ran while one was open for 1% of the time, Pallas kernels for 4%

profile of v5, /device:TPU:1, one launch (start us, length us, event | category | flops | bytes accessed | tf_op | source)
XLA Modules:
  0.0 110.4 jit_solution(15674712030899581797)
XLA Ops:
  0.7 0.8 pad_maximum_fusion
  1.4 0.1 broadcast_select_fusion
  1.5 4.4 %collective-permute-start = (f32[8,128]{1,0:T(8,128)S(1)}, f32[8,128]{1,0:T(8,128)S(1)}, u32[]{:S(2)}, u32[]{:S(2)}) collective-permute-start(f32[8,128]{1,0:T(8,128)S(1)} %broadcast_select_fusion), channel_id=1, source_target_pairs={{0,32},{8,40},{16,48},{24,56},{32,0},{40,8},{48,16},{56,24},{64,96... | collective-permute-start | bytes 12296 | tf_op jit(solution)/shard_map/ppermute | solution.py:310
  5.9 4.2 %pack.1 = (bf16[8,1168,128]{2,1,0:T(8,128)(2,1)}, f32[128,128]{1,0:T(8,128)}, f32[128,128]{1,0:T(8,128)}, f32[8,128]{1,0:T(8,128)}) custom-call(s32[1]{0:T(128)} %bitcast.turn_ref, bf16[128,3072]{1,0:T(8,128)(2,1)} %q_ref.3, bf16[128,3072]{1,0:T(8,128)(2,1)} %k_ref.3, bf16[128,3072]{1,0:T(8,128)(2,1)} %v_ref.1), custom_call_target="tpu_custom_call" | custom-call | tf_op jit(solution)/shard_map/pack/pallas_call | solution.py:361
  10.1 0.0 copy-start.6
  10.1 8.0 %all-to-all-start = ((bf16[8,1168,128]{2,1,0:T(8,128)(2,1)}), bf16[8,1168,128]{2,1,0:T(8,128)(2,1)S(1)}, u32[]{:S(2)}, u32[]{:S(2)}) async-start(bf16[8,1168,128]{2,1,0:T(8,128)(2,1)} %get-tuple-element.18), calls=%async_computation | async-start | bytes 4784128 | tf_op jit(solution)/shard_map/all_to_all | solution.py:369
  18.1 0.0 collective-permute-done
  18.1 0.1 fusion.x_ref
  18.2 0.0 copy-done.6
  18.2 0.0 copy-start.3
  18.2 2.1 %collective-permute-start.3 = (f32[8,128]{1,0:T(8,128)S(1)}, f32[8,128]{1,0:T(8,128)S(1)}, u32[]{:S(2)}, u32[]{:S(2)}) collective-permute-start(f32[8,128]{1,0:T(8,128)S(1)} %hold.2), channel_id=1, source_target_pairs={{0,24},{8,0},{16,8},{24,16},{32,56},{40,32},{48,40},{56,48},{64,88... | collective-permute-start | bytes 12296 | tf_op jit(solution)/shard_map/ppermute | solution.py:305
  20.3 3.4 %collective-permute-start.2 = (f32[8,128]{1,0:T(8,128)S(1)}, f32[8,128]{1,0:T(8,128)S(1)}, u32[]{:S(2)}, u32[]{:S(2)}) collective-permute-start(f32[8,128]{1,0:T(8,128)S(1)} %hold.2), channel_id=1, source_target_pairs={{0,8},{8,16},{16,24},{24,0},{32,40},{40,48},{48,56},{56,32},{64,72... | collective-permute-start | bytes 12296 | tf_op jit(solution)/shard_map/ppermute | solution.py:305
  23.6 2.1 %collective-permute-start.1 = (f32[8,128]{1,0:T(8,128)S(1)}, f32[8,128]{1,0:T(8,128)S(1)}, u32[]{:S(2)}, u32[]{:S(2)}) collective-permute-start(f32[8,128]{1,0:T(8,128)S(1)} %hold.2), channel_id=1, source_target_pairs={{0,16},{8,24},{16,0},{24,8},{32,48},{40,56},{48,32},{56,40},{64,80... | collective-permute-start | bytes 12296 | tf_op jit(solution)/shard_map/ppermute | solution.py:305
  25.7 0.0 copy-done.3
  25.8 0.1 slice.18
  25.9 0.1 slice.19
  25.9 0.0 collective-permute-done.3
  26.0 0.2 collective-permute-done.2
  26.1 3.4 %collective-permute-done.1 = f32[8,128]{1,0:T(8,128)S(1)} collective-permute-done((f32[8,128]{1,0:T(8,128)S(1)}, f32[8,128]{1,0:T(8,128)S(1)}, u32[]{:S(2)}, u32[]{:S(2)}) %collective-permute-start.1) | collective-permute-done | bytes 4128 | tf_op jit(solution)/shard_map/ppermute | solution.py:305
  29.5 9.2 %collective-permute-start.4 = (f32[8,128]{1,0:T(8,128)S(1)}, f32[8,128]{1,0:T(8,128)S(1)}, u32[]{:S(2)}, u32[]{:S(2)}) collective-permute-start(f32[8,128]{1,0:T(8,128)S(1)} %add_add_fusion), channel_id=1, source_target_pairs={{0,0},{1,449},{2,386},{3,323},{4,260},{5,197},{6,134},{7,71},{8,8}... | collective-permute-start | bytes 12296 | tf_op jit(solution)/shard_map/ppermute | solution.py:370
  38.7 0.2 convert_reduce_fusion
  38.9 0.5 collective-permute-done.4.gain_ref
  39.5 8.2 %all-to-all-done.pay_ref = bf16[8,1168,128]{2,1,0:T(8,128)(2,1)S(1)} async-done(((bf16[8,1168,128]{2,1,0:T(8,128)(2,1)}), bf16[8,1168,128]{2,1,0:T(8,128)(2,1)S(1)}, u32[]{:S(2)}, u32[]{:S(2)}) %all-to-all-start) | async-done | bytes 2392096 | tf_op jit(solution)/shard_map/all_to_all | solution.py:369
  47.6 12.8 %attend.1 = (bf16[8,1184,128]{2,1,0:T(8,128)(2,1)S(1)}, f32[8,128]{1,0:T(8,128)S(1)}) custom-call(s32[4]{0:T(128)S(1)} %get-tuple-element.28.lo_ref, s32[4]{0:T(128)S(1)} %get-tuple-element.27.hi_ref, bf16[8,1168,128]{2,1,0:T(8,128)(2,1)S(1)} %all-to-all-done.pay_ref, f32[8,128]{1,0:T(8,128)S(1)} %collective-permute-done.4.gain_ref, s32[1,1024]{1,0:T(1,128)S(1)} %copy-done.3), custom_call_target="tpu_custom_call" | custom-call | tf_op jit(solution)/shard_map/attend/pallas_call | solution.py:335
  60.4 0.0 copy-start
  60.4 1.4 %copy-done = bf16[8,1184,128]{2,1,0:T(8,128)(2,1)} copy-done((bf16[8,1184,128]{2,1,0:T(8,128)(2,1)}, bf16[8,1184,128]{2,1,0:T(8,128)(2,1)S(1)}, u32[]{:S(2)}) %copy-start) | copy-done | bytes 2424856
  61.8 7.8 %all_to_all.19 = f32[8,1,128]{2,1,0:T(1,128)S(1)} all-to-all(f32[8,1,128]{2,1,0:T(1,128)S(1)} %bitcast.13), channel_id=1, replica_groups={{0,8,16,24,32,40,48,56},{64,72,80,88,96,104,112,120},{128,136,144,152,1..., dimensions={0} | all-to-all | bytes 8192 | tf_op jit(solution)/shard_map/all_to_all | solution.py:375
  69.6 6.2 %all-to-all-start.2 = ((bf16[8,1184,128]{2,1,0:T(8,128)(2,1)}), bf16[8,1184,128]{2,1,0:T(8,128)(2,1)S(1)}, u32[]{:S(2)}, u32[]{:S(2)}) async-start(bf16[8,1184,128]{2,1,0:T(8,128)(2,1)} %copy-done), calls=%async_computation.2 | async-start | bytes 4849664 | tf_op jit(solution)/shard_map/all_to_all | solution.py:378
  75.8 0.0 copy-start.4
  75.8 0.0 copy-start.5
  75.8 3.2 %collective-permute-start.5 = (f32[1,128]{1,0:T(1,128)S(1)}, f32[1,128]{1,0:T(1,128)S(1)}, u32[]{:S(2)}, u32[]{:S(2)}) collective-permute-start(f32[1,128]{1,0:T(1,128)S(1)} %hold.3), channel_id=1, source_target_pairs={{0,0},{1,65},{2,130},{3,195},{4,260},{5,325},{6,390},{7,455},{8,8}... | collective-permute-start | bytes 1544 | tf_op jit(solution)/shard_map/ppermute | solution.py:380
  79.1 5.1 %collective-permute-done.5 = f32[1,128]{1,0:T(1,128)S(1)} collective-permute-done((f32[1,128]{1,0:T(1,128)S(1)}, f32[1,128]{1,0:T(1,128)S(1)}, u32[]{:S(2)}, u32[]{:S(2)}) %collective-permute-start.5) | collective-permute-done | bytes 544 | tf_op jit(solution)/shard_map/ppermute | solution.py:380
  84.1 1.9 %collective-permute-start.6 = (f32[1,128]{1,0:T(1,128)S(1)}, f32[1,128]{1,0:T(1,128)S(1)}, u32[]{:S(2)}, u32[]{:S(2)}) collective-permute-start(f32[1,128]{1,0:T(1,128)S(1)} %collective-permute-done.5), channel_id=1, source_target_pairs={{0,1},{1,0},{2,3},{3,2},{4,5},{5,4},{6,7},{7,6},{8,9},{9,8},{10,11... | collective-permute-start | bytes 1544 | tf_op jit(solution)/shard_map/ppermute | solution.py:318
  86.1 1.1 collective-permute-done.6
  87.2 7.6 %collective-permute-start.9 = (f32[1,128]{1,0:T(1,128)S(1)}, f32[1,128]{1,0:T(1,128)S(1)}, u32[]{:S(2)}, u32[]{:S(2)}) collective-permute-start(f32[1,128]{1,0:T(1,128)S(1)} %add.34), channel_id=1, source_target_pairs={{0,6},{1,7},{2,0},{3,1},{4,2},{5,3},{6,4},{7,5},{8,14},{9,15},{10,... | collective-permute-start | bytes 1544 | tf_op jit(solution)/shard_map/ppermute | solution.py:305
  94.7 1.9 %collective-permute-start.8 = (f32[1,128]{1,0:T(1,128)S(1)}, f32[1,128]{1,0:T(1,128)S(1)}, u32[]{:S(2)}, u32[]{:S(2)}) collective-permute-start(f32[1,128]{1,0:T(1,128)S(1)} %add.34), channel_id=1, source_target_pairs={{0,2},{1,3},{2,4},{3,5},{4,6},{5,7},{6,0},{7,1},{8,10},{9,11},{10,... | collective-permute-start | bytes 1544 | tf_op jit(solution)/shard_map/ppermute | solution.py:305
  96.6 7.2 %collective-permute-start.7 = (f32[1,128]{1,0:T(1,128)S(1)}, f32[1,128]{1,0:T(1,128)S(1)}, u32[]{:S(2)}, u32[]{:S(2)}) collective-permute-start(f32[1,128]{1,0:T(1,128)S(1)} %add.34), channel_id=1, source_target_pairs={{0,4},{1,5},{2,6},{3,7},{4,0},{5,1},{6,2},{7,3},{8,12},{9,13},{10,... | collective-permute-start | bytes 1544 | tf_op jit(solution)/shard_map/ppermute | solution.py:305
  103.9 0.2 collective-permute-done.9
  104.1 0.0 collective-permute-done.8
  104.1 1.5 %collective-permute-done.7 = f32[1,128]{1,0:T(1,128)S(1)} collective-permute-done((f32[1,128]{1,0:T(1,128)S(1)}, f32[1,128]{1,0:T(1,128)S(1)}, u32[]{:S(2)}, u32[]{:S(2)}) %collective-permute-start.7) | collective-permute-done | bytes 544 | tf_op jit(solution)/shard_map/ppermute | solution.py:305
  105.7 0.6 slice_bitcast_fusion
  106.2 0.0 all-to-all-done.2.pay_ref
  106.3 0.0 copy-done.1
  106.3 0.0 copy-done.4
  106.3 0.0 copy-done.5
  106.3 0.0 copy-start.2
  106.3 1.1 %copy-done.2 = bf16[128,3072]{1,0:T(8,128)(2,1)S(1)} copy-done((bf16[128,3072]{1,0:T(8,128)(2,1)S(1)}, bf16[128,3072]{1,0:T(8,128)(2,1)}, u32[]{:S(2)}) %copy-start.2) | copy-done | bytes 786456
  107.4 2.8 %final.1 = (bf16[128,3072]{1,0:T(8,128)(2,1)}, bf16[128,3072]{1,0:T(8,128)(2,1)}, bf16[128,3072]{1,0:T(8,128)(2,1)}) custom-call(s32[1]{0:T(128)} %bitcast.turn_ref, bf16[128,3072]{1,0:T(8,128)(2,1)S(1)} %copy-done.1, bf16[128,3072]{1,0:T(8,128)(2,1)S(1)} %copy-done.2, f32[128,128]{1,0:T(8,128)S(1)} %copy-done.4, f32[128,128]{1,0:T(8,128)S(1)} %copy-done.5, ...), custom_call_target="tpu_custom_call" | custom-call | flops 17179869184 | bytes 33554432 | tf_op jit(solution)/shard_map/final/pallas_call | solution.py:383
  (9 shorter events, 0.1 us)
Async XLA Ops:
  1.5 16.6 %collective-permute-start = (f32[8,128]{1,0:T(8,128)S(1)}, f32[8,128]{1,0:T(8,128)S(1)}, u32[]{:S(2)}, u32[]{:S(2)}) collective-permute-start(f32[8,128]{1,0:T(8,128)S(1)} %broadcast_select_fusion), channel_id=1, source_target_pairs={{0,32},{8,40},{16,48},{24,56},{32,0},{40,8},{48,16},{56,24},{64,96... | collective-permute-start | bytes 12296 | tf_op jit(solution)/shard_map/ppermute | solution.py:310
  10.1 8.0 %copy-start.6 = (f32[8,128]{1,0:T(8,128)S(1)}, f32[8,128]{1,0:T(8,128)}, u32[]{:S(2)}) copy-start(f32[8,128]{1,0:T(8,128)} %get-tuple-element.19.after_ref) | copy-start | bytes 12292
  10.1 37.5 %all-to-all-start = ((bf16[8,1168,128]{2,1,0:T(8,128)(2,1)}), bf16[8,1168,128]{2,1,0:T(8,128)(2,1)S(1)}, u32[]{:S(2)}, u32[]{:S(2)}) async-start(bf16[8,1168,128]{2,1,0:T(8,128)(2,1)} %get-tuple-element.18), calls=%async_computation | async-start | bytes 4784128 | tf_op jit(solution)/shard_map/all_to_all | solution.py:369
  18.2 7.6 %copy-start.3 = (s32[1,1024]{1,0:T(1,128)S(1)}, s32[1,1024]{1,0:T(1,128)}, u32[]{:S(2)}) copy-start(s32[1,1024]{1,0:T(1,128)} %ids_ref.1) | copy-start | bytes 12292
  18.2 7.8 %collective-permute-start.3 = (f32[8,128]{1,0:T(8,128)S(1)}, f32[8,128]{1,0:T(8,128)S(1)}, u32[]{:S(2)}, u32[]{:S(2)}) collective-permute-start(f32[8,128]{1,0:T(8,128)S(1)} %hold.2), channel_id=1, source_target_pairs={{0,24},{8,0},{16,8},{24,16},{32,56},{40,32},{48,40},{56,48},{64,88... | collective-permute-start | bytes 12296 | tf_op jit(solution)/shard_map/ppermute | solution.py:305
  20.3 5.9 %collective-permute-start.2 = (f32[8,128]{1,0:T(8,128)S(1)}, f32[8,128]{1,0:T(8,128)S(1)}, u32[]{:S(2)}, u32[]{:S(2)}) collective-permute-start(f32[8,128]{1,0:T(8,128)S(1)} %hold.2), channel_id=1, source_target_pairs={{0,8},{8,16},{16,24},{24,0},{32,40},{40,48},{48,56},{56,32},{64,72... | collective-permute-start | bytes 12296 | tf_op jit(solution)/shard_map/ppermute | solution.py:305
  23.6 5.9 %collective-permute-start.1 = (f32[8,128]{1,0:T(8,128)S(1)}, f32[8,128]{1,0:T(8,128)S(1)}, u32[]{:S(2)}, u32[]{:S(2)}) collective-permute-start(f32[8,128]{1,0:T(8,128)S(1)} %hold.2), channel_id=1, source_target_pairs={{0,16},{8,24},{16,0},{24,8},{32,48},{40,56},{48,32},{56,40},{64,80... | collective-permute-start | bytes 12296 | tf_op jit(solution)/shard_map/ppermute | solution.py:305
  29.5 10.0 %collective-permute-start.4 = (f32[8,128]{1,0:T(8,128)S(1)}, f32[8,128]{1,0:T(8,128)S(1)}, u32[]{:S(2)}, u32[]{:S(2)}) collective-permute-start(f32[8,128]{1,0:T(8,128)S(1)} %add_add_fusion), channel_id=1, source_target_pairs={{0,0},{1,449},{2,386},{3,323},{4,260},{5,197},{6,134},{7,71},{8,8}... | collective-permute-start | bytes 12296 | tf_op jit(solution)/shard_map/ppermute | solution.py:370
  60.4 1.5 %copy-start = (bf16[8,1184,128]{2,1,0:T(8,128)(2,1)}, bf16[8,1184,128]{2,1,0:T(8,128)(2,1)S(1)}, u32[]{:S(2)}) copy-start(bf16[8,1184,128]{2,1,0:T(8,128)(2,1)S(1)} %get-tuple-element.22) | copy-start | bytes 7274500
  69.6 36.6 %all-to-all-start.2 = ((bf16[8,1184,128]{2,1,0:T(8,128)(2,1)}), bf16[8,1184,128]{2,1,0:T(8,128)(2,1)S(1)}, u32[]{:S(2)}, u32[]{:S(2)}) async-start(bf16[8,1184,128]{2,1,0:T(8,128)(2,1)} %copy-done), calls=%async_computation.2 | async-start | bytes 4849664 | tf_op jit(solution)/shard_map/all_to_all | solution.py:378
  75.8 30.4 %copy-start.1 = (bf16[128,3072]{1,0:T(8,128)(2,1)S(1)}, bf16[128,3072]{1,0:T(8,128)(2,1)}, u32[]{:S(2)}) copy-start(bf16[128,3072]{1,0:T(8,128)(2,1)} %q_ref.3) | copy-start | bytes 2359300
  75.8 30.4 %copy-start.4 = (f32[128,128]{1,0:T(8,128)S(1)}, f32[128,128]{1,0:T(8,128)}, u32[]{:S(2)}) copy-start(f32[128,128]{1,0:T(8,128)} %get-tuple-element.16.inv_q_ref) | copy-start | bytes 196612
  75.8 30.4 %copy-start.5 = (f32[128,128]{1,0:T(8,128)S(1)}, f32[128,128]{1,0:T(8,128)}, u32[]{:S(2)}) copy-start(f32[128,128]{1,0:T(8,128)} %get-tuple-element.17.inv_k_ref) | copy-start | bytes 196612
  75.8 8.3 %collective-permute-start.5 = (f32[1,128]{1,0:T(1,128)S(1)}, f32[1,128]{1,0:T(1,128)S(1)}, u32[]{:S(2)}, u32[]{:S(2)}) collective-permute-start(f32[1,128]{1,0:T(1,128)S(1)} %hold.3), channel_id=1, source_target_pairs={{0,0},{1,65},{2,130},{3,195},{4,260},{5,325},{6,390},{7,455},{8,8}... | collective-permute-start | bytes 1544 | tf_op jit(solution)/shard_map/ppermute | solution.py:380
  84.1 3.0 %collective-permute-start.6 = (f32[1,128]{1,0:T(1,128)S(1)}, f32[1,128]{1,0:T(1,128)S(1)}, u32[]{:S(2)}, u32[]{:S(2)}) collective-permute-start(f32[1,128]{1,0:T(1,128)S(1)} %collective-permute-done.5), channel_id=1, source_target_pairs={{0,1},{1,0},{2,3},{3,2},{4,5},{5,4},{6,7},{7,6},{8,9},{9,8},{10,11... | collective-permute-start | bytes 1544 | tf_op jit(solution)/shard_map/ppermute | solution.py:318
  87.2 17.0 %collective-permute-start.9 = (f32[1,128]{1,0:T(1,128)S(1)}, f32[1,128]{1,0:T(1,128)S(1)}, u32[]{:S(2)}, u32[]{:S(2)}) collective-permute-start(f32[1,128]{1,0:T(1,128)S(1)} %add.34), channel_id=1, source_target_pairs={{0,6},{1,7},{2,0},{3,1},{4,2},{5,3},{6,4},{7,5},{8,14},{9,15},{10,... | collective-permute-start | bytes 1544 | tf_op jit(solution)/shard_map/ppermute | solution.py:305
  94.7 9.4 %collective-permute-start.8 = (f32[1,128]{1,0:T(1,128)S(1)}, f32[1,128]{1,0:T(1,128)S(1)}, u32[]{:S(2)}, u32[]{:S(2)}) collective-permute-start(f32[1,128]{1,0:T(1,128)S(1)} %add.34), channel_id=1, source_target_pairs={{0,2},{1,3},{2,4},{3,5},{4,6},{5,7},{6,0},{7,1},{8,10},{9,11},{10,... | collective-permute-start | bytes 1544 | tf_op jit(solution)/shard_map/ppermute | solution.py:305
  96.6 9.0 %collective-permute-start.7 = (f32[1,128]{1,0:T(1,128)S(1)}, f32[1,128]{1,0:T(1,128)S(1)}, u32[]{:S(2)}, u32[]{:S(2)}) collective-permute-start(f32[1,128]{1,0:T(1,128)S(1)} %add.34), channel_id=1, source_target_pairs={{0,4},{1,5},{2,6},{3,7},{4,0},{5,1},{6,2},{7,3},{8,12},{9,13},{10,... | collective-permute-start | bytes 1544 | tf_op jit(solution)/shard_map/ppermute | solution.py:305
  106.3 1.1 %copy-start.2 = (bf16[128,3072]{1,0:T(8,128)(2,1)S(1)}, bf16[128,3072]{1,0:T(8,128)(2,1)}, u32[]{:S(2)}) copy-start(bf16[128,3072]{1,0:T(8,128)(2,1)} %k_ref.3) | copy-start | bytes 2359300

commit v6 on v5

--- a/solution.py
+++ b/solution.py
@@ -371,13 +371,13 @@
     lo, hi = windows(clip_ids)
     pay, part = attend_call(lo, hi, got, rows, clip_ids)
 
-    blocks = [list(range(b, b + 8)) for b in range(0, 64, 8)]
-    part = lax.all_to_all(part, "dp", 0, 0, axis_index_groups=blocks, tiled=True)
-    part = jnp.sum(part, axis=0, keepdims=True)
-    pay, part = lax.optimization_barrier((pay, part))
     got = lax.all_to_all(pay, "seq", 0, 0, tiled=True)
-    part = hold(part, part)
-    part = over_x(over_core(lax.ppermute(part, ("dp", "seq"), around(1))))[0]
+    part = over_y(hold(over_z(part), part))
+    part = lax.dynamic_slice_in_dim(part, place, 1, 0)
+    part = lax.ppermute(part, ("dp", "seq"), around(1))
+    part, got = lax.optimization_barrier((part, got))
+    part = lax.all_to_all(jnp.broadcast_to(part, (N_SEQ, HD))[:, None], "seq", 0, 0, tiled=True)
+    part = jnp.sum(part, axis=(0, 1))
 
     out = shape((TOK, WIDTH))
     d_q, d_k, d_v = pl.pallas_call(

time: 111 us -> 110 us (level); the launches traced: 110 us -> 108 us
  waiting for transfers between devices: 20.2 us -> 30.8 us
  blocking collectives: 7.77 us -> 0 us
  starting transfers between devices: 57.1 us -> 51.3 us
    all_to_all x1 -> x0, blocking collectives: 7.77 us -> none  [local(): lax.all_to_all(part, 'dp', 0, 0, axis_index_groups=blocks, tiled=True)]
    all_to_all x2, waiting for transfers between devices: 8.16 us -> 15.5 us  [local(): got = lax.all_to_all(pay, 'seq', 0, 0, tiled=True)]
    ppermute x6, starting transfers between devices: 24.3 us -> 17.8 us  [sum_four(): one, two, three = (lax.ppermute(x, axis, pairs(k)) for k in (1, 2, 3))]
    all_to_all x0 -> x1, starting transfers between devices: none -> 4.1 us  [local(): lax.all_to_all(jnp.broadcast_to(part, (N_SEQ, HD))[:, None], 'seq', 0, 0,...]
    ppermute x2 -> x1, starting transfers between devices: 5.12 us -> 2.77 us  [local(): part = lax.ppermute(part, ('dp', 'seq'), around(1))]
    ppermute x1 -> x2, starting transfers between devices: 4.36 us -> 6.27 us  [over_z(): return x + lax.ppermute(x, 'dp', [(d, d ^ 4) for d in range(64)])]
    all_to_all x2, starting transfers between devices: 14.1 us -> 12.4 us  [local(): got = lax.all_to_all(pay, 'seq', 0, 0, tiled=True)]
    ppermute x6, waiting for transfers between devices: 5.32 us -> 6.96 us  [sum_four(): one, two, three = (lax.ppermute(x, axis, pairs(k)) for k in (1, 2, 3))]
  transfers between devices with their start and end apart: 12 -> 13, of which waited for: 8 -> 7; matrix products, arithmetic and copies ran while one was open for 1% -> 0% of each run, Pallas kernels for 4% -> 7%
where the time goes in v6:
time: 110 us; the launch traced here: 108 us
  starting transfers between devices  51.3 us (47%)
  waiting for transfers between devices  30.8 us (28%)
  Pallas kernels  19.7 us (18%)
  local copies, waits for them, and re-layouts  3.99 us (4%)
  other arithmetic  1.15 us (1%)
    ppermute x6, starting transfers between devices, sum_four(): one, two, three = (lax.ppermute(x, axis, pairs(k)) for k in (1, 2, 3))  17.8 us
    all_to_all x2, waiting for transfers between devices, local(): got = lax.all_to_all(pay, 'seq', 0, 0, tiled=True)  15.5 us
    pallas_call x1, Pallas kernels, attend_call(): pl.pallas_call(attend_kernel, out_shape=[back, shape((8, HD), jnp.float32...  12.7 us
    all_to_all x2, starting transfers between devices, local(): got = lax.all_to_all(pay, 'seq', 0, 0, tiled=True)  12.4 us
    ppermute x1, starting transfers between devices, local(): lax.ppermute(over_y(hold(over_z(rows), mark)), ('dp', 'seq'), around(-1))  8 us
    ppermute x1, waiting for transfers between devices, local(): part = lax.ppermute(part, ('dp', 'seq'), around(1))  7.18 us
    ppermute x6, waiting for transfers between devices, sum_four(): one, two, three = (lax.ppermute(x, axis, pairs(k)) for k in (1, 2, 3))  6.96 us
    ppermute x2, starting transfers between devices, over_z(): return x + lax.ppermute(x, 'dp', [(d, d ^ 4) for d in range(64)])  6.27 us
  transfers between devices with their start and end apart: 13, of which 7 were waited for; matrix products, arithmetic and copies ran while one was open for 0% of the time, Pallas kernels for 7%

profile of v6, /device:TPU:1, one launch (start us, length us, event | category | flops | bytes accessed | tf_op | source)
XLA Modules:
  0.0 107.9 jit_solution(14454941249610953917)
XLA Ops:
  0.7 0.8 pad_maximum_fusion
  1.4 0.1 broadcast_select_fusion
  1.5 4.4 %collective-permute-start = (f32[8,128]{1,0:T(8,128)S(1)}, f32[8,128]{1,0:T(8,128)S(1)}, u32[]{:S(2)}, u32[]{:S(2)}) collective-permute-start(f32[8,128]{1,0:T(8,128)S(1)} %broadcast_select_fusion), channel_id=1, source_target_pairs={{0,32},{8,40},{16,48},{24,56},{32,0},{40,8},{48,16},{56,24},{64,96... | collective-permute-start | bytes 12296 | tf_op jit(solution)/shard_map/ppermute | solution.py:310
  5.9 4.2 %pack.1 = (bf16[8,1168,128]{2,1,0:T(8,128)(2,1)}, f32[128,128]{1,0:T(8,128)}, f32[128,128]{1,0:T(8,128)}, f32[8,128]{1,0:T(8,128)}) custom-call(s32[1]{0:T(128)} %bitcast.turn_ref, bf16[128,3072]{1,0:T(8,128)(2,1)} %q_ref.3, bf16[128,3072]{1,0:T(8,128)(2,1)} %k_ref.3, bf16[128,3072]{1,0:T(8,128)(2,1)} %v_ref.1), custom_call_target="tpu_custom_call" | custom-call | tf_op jit(solution)/shard_map/pack/pallas_call | solution.py:361
  10.1 0.0 copy-start.6
  10.1 8.0 %all-to-all-start = ((bf16[8,1168,128]{2,1,0:T(8,128)(2,1)}), bf16[8,1168,128]{2,1,0:T(8,128)(2,1)S(1)}, u32[]{:S(2)}, u32[]{:S(2)}) async-start(bf16[8,1168,128]{2,1,0:T(8,128)(2,1)} %get-tuple-element.18), calls=%async_computation | async-start | bytes 4784128 | tf_op jit(solution)/shard_map/all_to_all | solution.py:369
  18.1 0.0 collective-permute-done
  18.1 0.1 fusion.x_ref
  18.2 0.0 copy-done.6
  18.2 2.0 %collective-permute-start.2 = (f32[8,128]{1,0:T(8,128)S(1)}, f32[8,128]{1,0:T(8,128)S(1)}, u32[]{:S(2)}, u32[]{:S(2)}) collective-permute-start(f32[8,128]{1,0:T(8,128)S(1)} %hold.2), channel_id=1, source_target_pairs={{0,8},{8,16},{16,24},{24,0},{32,40},{40,48},{48,56},{56,32},{64,72... | collective-permute-start | bytes 12296 | tf_op jit(solution)/shard_map/ppermute | solution.py:305
  20.2 4.6 %collective-permute-start.3 = (f32[8,128]{1,0:T(8,128)S(1)}, f32[8,128]{1,0:T(8,128)S(1)}, u32[]{:S(2)}, u32[]{:S(2)}) collective-permute-start(f32[8,128]{1,0:T(8,128)S(1)} %hold.2), channel_id=1, source_target_pairs={{0,24},{8,0},{16,8},{24,16},{32,56},{40,32},{48,40},{56,48},{64,88... | collective-permute-start | bytes 12296 | tf_op jit(solution)/shard_map/ppermute | solution.py:305
  24.9 1.9 %collective-permute-start.1 = (f32[8,128]{1,0:T(8,128)S(1)}, f32[8,128]{1,0:T(8,128)S(1)}, u32[]{:S(2)}, u32[]{:S(2)}) collective-permute-start(f32[8,128]{1,0:T(8,128)S(1)} %hold.2), channel_id=1, source_target_pairs={{0,16},{8,24},{16,0},{24,8},{32,48},{40,56},{48,32},{56,40},{64,80... | collective-permute-start | bytes 12296 | tf_op jit(solution)/shard_map/ppermute | solution.py:305
  26.8 0.0 copy-done.3
  26.8 0.1 slice.13
  26.9 0.1 slice.12
  27.0 0.0 collective-permute-done.2
  27.0 0.0 collective-permute-done.3
  27.0 3.7 %collective-permute-done.1 = f32[8,128]{1,0:T(8,128)S(1)} collective-permute-done((f32[8,128]{1,0:T(8,128)S(1)}, f32[8,128]{1,0:T(8,128)S(1)}, u32[]{:S(2)}, u32[]{:S(2)}) %collective-permute-start.1) | collective-permute-done | bytes 4128 | tf_op jit(solution)/shard_map/ppermute | solution.py:305
  30.7 8.0 %collective-permute-start.4 = (f32[8,128]{1,0:T(8,128)S(1)}, f32[8,128]{1,0:T(8,128)S(1)}, u32[]{:S(2)}, u32[]{:S(2)}) collective-permute-start(f32[8,128]{1,0:T(8,128)S(1)} %add_add_fusion.1), channel_id=1, source_target_pairs={{0,0},{1,449},{2,386},{3,323},{4,260},{5,197},{6,134},{7,71},{8,8}... | collective-permute-start | bytes 12296 | tf_op jit(solution)/shard_map/ppermute | solution.py:370
  38.7 0.2 convert_reduce_fusion
  38.9 0.5 collective-permute-done.4.gain_ref
  39.5 8.2 %all-to-all-done.pay_ref = bf16[8,1168,128]{2,1,0:T(8,128)(2,1)S(1)} async-done(((bf16[8,1168,128]{2,1,0:T(8,128)(2,1)}), bf16[8,1168,128]{2,1,0:T(8,128)(2,1)S(1)}, u32[]{:S(2)}, u32[]{:S(2)}) %all-to-all-start) | async-done | bytes 2392096 | tf_op jit(solution)/shard_map/all_to_all | solution.py:369
  47.6 12.7 %attend.1 = (bf16[8,1184,128]{2,1,0:T(8,128)(2,1)S(1)}, f32[8,128]{1,0:T(8,128)S(1)}) custom-call(s32[4]{0:T(128)S(1)} %get-tuple-element.28.lo_ref, s32[4]{0:T(128)S(1)} %get-tuple-element.27.hi_ref, bf16[8,1168,128]{2,1,0:T(8,128)(2,1)S(1)} %all-to-all-done.pay_ref, f32[8,128]{1,0:T(8,128)S(1)} %collective-permute-done.4.gain_ref, s32[1,1024]{1,0:T(1,128)S(1)} %copy-done.3), custom_call_target="tpu_custom_call" | custom-call | tf_op jit(solution)/shard_map/attend/pallas_call | solution.py:335
  60.3 1.5 %copy-done = bf16[8,1184,128]{2,1,0:T(8,128)(2,1)} copy-done((bf16[8,1184,128]{2,1,0:T(8,128)(2,1)}, bf16[8,1184,128]{2,1,0:T(8,128)(2,1)S(1)}, u32[]{:S(2)}) %copy-start) | copy-done | bytes 2424856
  61.8 1.9 %collective-permute-start.5 = (f32[8,128]{1,0:T(8,128)S(1)}, f32[8,128]{1,0:T(8,128)S(1)}, u32[]{:S(2)}, u32[]{:S(2)}) collective-permute-start(f32[8,128]{1,0:T(8,128)S(1)} %get-tuple-element.20.after_ref), channel_id=1, source_target_pairs={{0,32},{8,40},{16,48},{24,56},{32,0},{40,8},{48,16},{56,24},{64,96... | collective-permute-start | bytes 12296 | tf_op jit(solution)/shard_map/ppermute | solution.py:310
  63.7 4.4 %all-to-all-start.1 = ((bf16[8,1184,128]{2,1,0:T(8,128)(2,1)}), bf16[8,1184,128]{2,1,0:T(8,128)(2,1)S(1)}, u32[]{:S(2)}, u32[]{:S(2)}) async-start(bf16[8,1184,128]{2,1,0:T(8,128)(2,1)} %copy-done), calls=%async_computation.1 | async-start | bytes 4849664 | tf_op jit(solution)/shard_map/all_to_all | solution.py:374
  68.1 0.0 collective-permute-done.5
  68.1 0.0 copy-start.1
  68.1 0.0 copy-start.4
  68.1 0.0 copy-start.5
  68.2 2.4 %collective-permute-start.7 = (f32[8,128]{1,0:T(8,128)S(1)}, f32[8,128]{1,0:T(8,128)S(1)}, u32[]{:S(2)}, u32[]{:S(2)}) collective-permute-start(f32[8,128]{1,0:T(8,128)S(1)} %hold.3), channel_id=1, source_target_pairs={{0,8},{8,16},{16,24},{24,0},{32,40},{40,48},{48,56},{56,32},{64,72... | collective-permute-start | bytes 12296 | tf_op jit(solution)/shard_map/ppermute | solution.py:305
  70.6 4.2 %collective-permute-start.8 = (f32[8,128]{1,0:T(8,128)S(1)}, f32[8,128]{1,0:T(8,128)S(1)}, u32[]{:S(2)}, u32[]{:S(2)}) collective-permute-start(f32[8,128]{1,0:T(8,128)S(1)} %hold.3), channel_id=1, source_target_pairs={{0,24},{8,0},{16,8},{24,16},{32,56},{40,32},{48,40},{56,48},{64,88... | collective-permute-start | bytes 12296 | tf_op jit(solution)/shard_map/ppermute | solution.py:305
  74.8 2.6 %collective-permute-start.6 = (f32[8,128]{1,0:T(8,128)S(1)}, f32[8,128]{1,0:T(8,128)S(1)}, u32[]{:S(2)}, u32[]{:S(2)}) collective-permute-start(f32[8,128]{1,0:T(8,128)S(1)} %hold.3), channel_id=1, source_target_pairs={{0,16},{8,24},{16,0},{24,8},{32,48},{40,56},{48,32},{56,40},{64,80... | collective-permute-start | bytes 12296 | tf_op jit(solution)/shard_map/ppermute | solution.py:305
  77.4 0.0 collective-permute-done.7
  77.4 0.0 collective-permute-done.8
  77.4 3.2 %collective-permute-done.6 = f32[8,128]{1,0:T(8,128)S(1)} collective-permute-done((f32[8,128]{1,0:T(8,128)S(1)}, f32[8,128]{1,0:T(8,128)S(1)}, u32[]{:S(2)}, u32[]{:S(2)}) %collective-permute-start.6) | collective-permute-done | bytes 4128 | tf_op jit(solution)/shard_map/ppermute | solution.py:305
  80.7 2.8 %collective-permute-start.9 = (f32[1,128]{1,0:T(1,128)S(1)}, f32[1,128]{1,0:T(1,128)S(1)}, u32[]{:S(2)}, u32[]{:S(2)}) collective-permute-start(f32[1,128]{1,0:T(1,128)S(1)} %constant_dynamic-slice_fusion), channel_id=1, source_target_pairs={{0,0},{1,65},{2,130},{3,195},{4,260},{5,325},{6,390},{7,455},{8,8}... | collective-permute-start | bytes 1544 | tf_op jit(solution)/shard_map/ppermute | solution.py:377
  83.5 7.2 %collective-permute-done.9 = f32[1,128]{1,0:T(1,128)S(1)} collective-permute-done((f32[1,128]{1,0:T(1,128)S(1)}, f32[1,128]{1,0:T(1,128)S(1)}, u32[]{:S(2)}, u32[]{:S(2)}) %collective-permute-start.9) | collective-permute-done | bytes 544 | tf_op jit(solution)/shard_map/ppermute | solution.py:377
  90.6 7.3 %all-to-all-done.1.pay_ref = bf16[8,1184,128]{2,1,0:T(8,128)(2,1)S(1)} async-done(((bf16[8,1184,128]{2,1,0:T(8,128)(2,1)}), bf16[8,1184,128]{2,1,0:T(8,128)(2,1)S(1)}, u32[]{:S(2)}, u32[]{:S(2)}) %all-to-all-start.1) | async-done | bytes 2424864 | tf_op jit(solution)/shard_map/all_to_all | solution.py:374
  98.0 0.6 broadcast_in_dim_broadcast_in_dim.2
  98.6 4.1 %all-to-all-start.2 = ((f32[8,1,128]{2,1,0:T(1,128)}), f32[8,1,128]{2,1,0:T(1,128)S(1)}, u32[]{:S(2)}, u32[]{:S(2)}) async-start(f32[8,1,128]{2,1,0:T(1,128)} %broadcast_in_dim_broadcast_in_dim.2), calls=%async_computation.2 | async-start | bytes 8192 | tf_op jit(solution)/shard_map/all_to_all | solution.py:379
  102.7 0.0 copy-done.4
  102.7 0.0 copy-done.5
  102.7 0.0 copy-start.2
  102.7 1.1 %copy-done.2 = bf16[128,3072]{1,0:T(8,128)(2,1)S(1)} copy-done((bf16[128,3072]{1,0:T(8,128)(2,1)S(1)}, bf16[128,3072]{1,0:T(8,128)(2,1)}, u32[]{:S(2)}) %copy-start.2) | copy-done | bytes 786456
  103.8 2.8 %final.1 = (bf16[128,3072]{1,0:T(8,128)(2,1)}, bf16[128,3072]{1,0:T(8,128)(2,1)}, bf16[128,3072]{1,0:T(8,128)(2,1)}) custom-call(s32[1]{0:T(128)} %bitcast.turn_ref, bf16[128,3072]{1,0:T(8,128)(2,1)S(1)} %copy-done.1, bf16[128,3072]{1,0:T(8,128)(2,1)S(1)} %copy-done.2, f32[128,128]{1,0:T(8,128)S(1)} %copy-done.4, f32[128,128]{1,0:T(8,128)S(1)} %copy-done.5, ...), custom_call_target="tpu_custom_call" | custom-call | flops 17179869184 | bytes 33554432 | tf_op jit(solution)/shard_map/final/pallas_call | solution.py:383
  106.6 0.6 all-to-all-done.2
  107.3 0.6 fusion.1
  (12 shorter events, 0.1 us)
Async XLA Ops:
  1.5 16.6 %collective-permute-start = (f32[8,128]{1,0:T(8,128)S(1)}, f32[8,128]{1,0:T(8,128)S(1)}, u32[]{:S(2)}, u32[]{:S(2)}) collective-permute-start(f32[8,128]{1,0:T(8,128)S(1)} %broadcast_select_fusion), channel_id=1, source_target_pairs={{0,32},{8,40},{16,48},{24,56},{32,0},{40,8},{48,16},{56,24},{64,96... | collective-permute-start | bytes 12296 | tf_op jit(solution)/shard_map/ppermute | solution.py:310
  10.1 8.0 %copy-start.6 = (f32[8,128]{1,0:T(8,128)S(1)}, f32[8,128]{1,0:T(8,128)}, u32[]{:S(2)}) copy-start(f32[8,128]{1,0:T(8,128)} %get-tuple-element.19.after_ref) | copy-start | bytes 12292
  10.1 37.5 %all-to-all-start = ((bf16[8,1168,128]{2,1,0:T(8,128)(2,1)}), bf16[8,1168,128]{2,1,0:T(8,128)(2,1)S(1)}, u32[]{:S(2)}, u32[]{:S(2)}) async-start(bf16[8,1168,128]{2,1,0:T(8,128)(2,1)} %get-tuple-element.18), calls=%async_computation | async-start | bytes 4784128 | tf_op jit(solution)/shard_map/all_to_all | solution.py:369
  18.2 8.6 %copy-start.3 = (s32[1,1024]{1,0:T(1,128)S(1)}, s32[1,1024]{1,0:T(1,128)}, u32[]{:S(2)}) copy-start(s32[1,1024]{1,0:T(1,128)} %ids_ref.1) | copy-start | bytes 12292
  18.2 8.8 %collective-permute-start.2 = (f32[8,128]{1,0:T(8,128)S(1)}, f32[8,128]{1,0:T(8,128)S(1)}, u32[]{:S(2)}, u32[]{:S(2)}) collective-permute-start(f32[8,128]{1,0:T(8,128)S(1)} %hold.2), channel_id=1, source_target_pairs={{0,8},{8,16},{16,24},{24,0},{32,40},{40,48},{48,56},{56,32},{64,72... | collective-permute-start | bytes 12296 | tf_op jit(solution)/shard_map/ppermute | solution.py:305
  20.2 6.7 %collective-permute-start.3 = (f32[8,128]{1,0:T(8,128)S(1)}, f32[8,128]{1,0:T(8,128)S(1)}, u32[]{:S(2)}, u32[]{:S(2)}) collective-permute-start(f32[8,128]{1,0:T(8,128)S(1)} %hold.2), channel_id=1, source_target_pairs={{0,24},{8,0},{16,8},{24,16},{32,56},{40,32},{48,40},{56,48},{64,88... | collective-permute-start | bytes 12296 | tf_op jit(solution)/shard_map/ppermute | solution.py:305
  24.9 5.9 %collective-permute-start.1 = (f32[8,128]{1,0:T(8,128)S(1)}, f32[8,128]{1,0:T(8,128)S(1)}, u32[]{:S(2)}, u32[]{:S(2)}) collective-permute-start(f32[8,128]{1,0:T(8,128)S(1)} %hold.2), channel_id=1, source_target_pairs={{0,16},{8,24},{16,0},{24,8},{32,48},{40,56},{48,32},{56,40},{64,80... | collective-permute-start | bytes 12296 | tf_op jit(solution)/shard_map/ppermute | solution.py:305
  30.7 8.7 %collective-permute-start.4 = (f32[8,128]{1,0:T(8,128)S(1)}, f32[8,128]{1,0:T(8,128)S(1)}, u32[]{:S(2)}, u32[]{:S(2)}) collective-permute-start(f32[8,128]{1,0:T(8,128)S(1)} %add_add_fusion.1), channel_id=1, source_target_pairs={{0,0},{1,449},{2,386},{3,323},{4,260},{5,197},{6,134},{7,71},{8,8}... | collective-permute-start | bytes 12296 | tf_op jit(solution)/shard_map/ppermute | solution.py:370
  60.3 1.5 %copy-start = (bf16[8,1184,128]{2,1,0:T(8,128)(2,1)}, bf16[8,1184,128]{2,1,0:T(8,128)(2,1)S(1)}, u32[]{:S(2)}) copy-start(bf16[8,1184,128]{2,1,0:T(8,128)(2,1)S(1)} %get-tuple-element.21) | copy-start | bytes 7274500
  61.8 6.3 %collective-permute-start.5 = (f32[8,128]{1,0:T(8,128)S(1)}, f32[8,128]{1,0:T(8,128)S(1)}, u32[]{:S(2)}, u32[]{:S(2)}) collective-permute-start(f32[8,128]{1,0:T(8,128)S(1)} %get-tuple-element.20.after_ref), channel_id=1, source_target_pairs={{0,32},{8,40},{16,48},{24,56},{32,0},{40,8},{48,16},{56,24},{64,96... | collective-permute-start | bytes 12296 | tf_op jit(solution)/shard_map/ppermute | solution.py:310
  63.7 34.3 %all-to-all-start.1 = ((bf16[8,1184,128]{2,1,0:T(8,128)(2,1)}), bf16[8,1184,128]{2,1,0:T(8,128)(2,1)S(1)}, u32[]{:S(2)}, u32[]{:S(2)}) async-start(bf16[8,1184,128]{2,1,0:T(8,128)(2,1)} %copy-done), calls=%async_computation.1 | async-start | bytes 4849664 | tf_op jit(solution)/shard_map/all_to_all | solution.py:374
  68.1 34.6 %copy-start.1 = (bf16[128,3072]{1,0:T(8,128)(2,1)S(1)}, bf16[128,3072]{1,0:T(8,128)(2,1)}, u32[]{:S(2)}) copy-start(bf16[128,3072]{1,0:T(8,128)(2,1)} %q_ref.3) | copy-start | bytes 2359300
  68.1 34.5 %copy-start.4 = (f32[128,128]{1,0:T(8,128)S(1)}, f32[128,128]{1,0:T(8,128)}, u32[]{:S(2)}) copy-start(f32[128,128]{1,0:T(8,128)} %get-tuple-element.16.inv_q_ref) | copy-start | bytes 196612
  68.1 34.5 %copy-start.5 = (f32[128,128]{1,0:T(8,128)S(1)}, f32[128,128]{1,0:T(8,128)}, u32[]{:S(2)}) copy-start(f32[128,128]{1,0:T(8,128)} %get-tuple-element.17.inv_k_ref) | copy-start | bytes 196612
  68.2 9.2 %collective-permute-start.7 = (f32[8,128]{1,0:T(8,128)S(1)}, f32[8,128]{1,0:T(8,128)S(1)}, u32[]{:S(2)}, u32[]{:S(2)}) collective-permute-start(f32[8,128]{1,0:T(8,128)S(1)} %hold.3), channel_id=1, source_target_pairs={{0,8},{8,16},{16,24},{24,0},{32,40},{40,48},{48,56},{56,32},{64,72... | collective-permute-start | bytes 12296 | tf_op jit(solution)/shard_map/ppermute | solution.py:305
  70.6 6.8 %collective-permute-start.8 = (f32[8,128]{1,0:T(8,128)S(1)}, f32[8,128]{1,0:T(8,128)S(1)}, u32[]{:S(2)}, u32[]{:S(2)}) collective-permute-start(f32[8,128]{1,0:T(8,128)S(1)} %hold.3), channel_id=1, source_target_pairs={{0,24},{8,0},{16,8},{24,16},{32,56},{40,32},{48,40},{56,48},{64,88... | collective-permute-start | bytes 12296 | tf_op jit(solution)/shard_map/ppermute | solution.py:305
  74.8 5.9 %collective-permute-start.6 = (f32[8,128]{1,0:T(8,128)S(1)}, f32[8,128]{1,0:T(8,128)S(1)}, u32[]{:S(2)}, u32[]{:S(2)}) collective-permute-start(f32[8,128]{1,0:T(8,128)S(1)} %hold.3), channel_id=1, source_target_pairs={{0,16},{8,24},{16,0},{24,8},{32,48},{40,56},{48,32},{56,40},{64,80... | collective-permute-start | bytes 12296 | tf_op jit(solution)/shard_map/ppermute | solution.py:305
  80.7 10.0 %collective-permute-start.9 = (f32[1,128]{1,0:T(1,128)S(1)}, f32[1,128]{1,0:T(1,128)S(1)}, u32[]{:S(2)}, u32[]{:S(2)}) collective-permute-start(f32[1,128]{1,0:T(1,128)S(1)} %constant_dynamic-slice_fusion), channel_id=1, source_target_pairs={{0,0},{1,65},{2,130},{3,195},{4,260},{5,325},{6,390},{7,455},{8,8}... | collective-permute-start | bytes 1544 | tf_op jit(solution)/shard_map/ppermute | solution.py:377
  98.6 8.7 %all-to-all-start.2 = ((f32[8,1,128]{2,1,0:T(1,128)}), f32[8,1,128]{2,1,0:T(1,128)S(1)}, u32[]{:S(2)}, u32[]{:S(2)}) async-start(f32[8,1,128]{2,1,0:T(1,128)} %broadcast_in_dim_broadcast_in_dim.2), calls=%async_computation.2 | async-start | bytes 8192 | tf_op jit(solution)/shard_map/all_to_all | solution.py:379
  102.7 1.1 %copy-start.2 = (bf16[128,3072]{1,0:T(8,128)(2,1)S(1)}, bf16[128,3072]{1,0:T(8,128)(2,1)}, u32[]{:S(2)}) copy-start(bf16[128,3072]{1,0:T(8,128)(2,1)} %k_ref.3) | copy-start | bytes 2359300

commit v7 on v6

--- a/solution.py
+++ b/solution.py
@@ -51,7 +51,8 @@
     return slice((c * 3 + n) * TOK, (c * 3 + n + 1) * TOK)
 
 
-def pack_kernel(turn_ref, q_ref, k_ref, v_ref, pay_ref, inv_q_ref, inv_k_ref, mark_ref, held, extra, load_sems, sems):
+def pack_kernel(turn_ref, q_ref, k_ref, v_ref, gain_q_ref, gain_k_ref, pay_ref, inv_q_ref, inv_k_ref, rows_ref,
+                held, extra, one, two, load_sems, sems):
     wide = WIDTH // CUTS
     loads = []
     for t in range(CUTS):
@@ -64,7 +65,7 @@
         for n in range(3):
             loads[3 * t + n].wait()
             for h in range(t * H // CUTS, (t + 1) * H // CUTS):
-                dest = (h // HEADS + N_SEQ - turn_ref[0]) % N_SEQ
+                dest = (h // HEADS + N_SEQ - turn_ref[0] // 8) % N_SEQ
                 copies.append(pltpu.make_async_copy(
                     held.at[n, :, h * HD:(h + 1) * HD], pay_ref.at[dest, body(h % HEADS, n)], sems.at[len(copies)]))
                 copies[-1].start()
@@ -78,7 +79,12 @@
         inv = jnp.broadcast_to(inv, (TOK, HD))
         inv_ref[...] = inv
         rows.append(jnp.transpose(inv)[0:1])
-    mark_ref[...] = jnp.zeros_like(mark_ref)
+    one[...] = jnp.zeros_like(one)
+    two[...] = jnp.zeros_like(two)
+    one[0:1, 0:SHARD] = gain_q_ref[...]
+    two[0:1, 0:SHARD] = gain_k_ref[...]
+    row = (one[...] + pltpu.roll(two[...], 64, 1))[0:1]
+    rows_ref[...] = jnp.where(lax.broadcasted_iota(jnp.int32, (8, HD), 0) == turn_ref[0] % 8, row, 0.0)
     extra[...] = extra_rows(rows, EXTRA)
     for s in range(N_SEQ):
         copies.append(pltpu.make_async_copy(extra, pay_ref.at[s, BODY:], sems.at[len(copies)]))
@@ -238,7 +244,7 @@
 
 
 def final_kernel(turn_ref, q_ref, k_ref, inv_q_ref, inv_k_ref, pay_ref, dq_ref, dk_ref, dv_ref, outs, sems):
-    src = [(g + N_SEQ - turn_ref[0]) % N_SEQ for g in range(N_SEQ)]
+    src = [(g + N_SEQ - turn_ref[0] // 8) % N_SEQ for g in range(N_SEQ)]
     pairs = [(g, c, slice((g * HEADS + c) * HD, (g * HEADS + c + 1) * HD))
              for g in range(N_SEQ) for c in range(HEADS)]
     copies = []
@@ -320,11 +326,6 @@
 
 def over_x(x):
     return sum_four(x, "seq", lambda k: [(s, (s + 2 * k) % 8) for s in range(8)])
-
-
-def spread(pair):
-    pad = jnp.zeros(pair.shape[:-2] + (16,), jnp.float32)
-    return jnp.concatenate([pair[..., 0, :], pad, pair[..., 1, :], pad], axis=-1)
 
 
 def attend_call(lo, hi, got, gain, ids):
@@ -351,32 +352,31 @@
 
 def local(q_in, k_in, v_in, gain_q, gain_k, clip_ids):
     place = lax.axis_index("dp") % 8
-    turn = (lax.axis_index("dp") // 8).astype(jnp.int32)[None]
+    turn = lax.axis_index("dp").astype(jnp.int32)[None]
     inv = shape((TOK, HD), jnp.float32)
     three = pltpu.VMEM((3, TOK, WIDTH), jnp.bfloat16)
-
-    row = spread(jnp.stack([gain_q, gain_k]))[None]
-    rows = jnp.where(lax.broadcasted_iota(jnp.int32, (8, HD), 0) == place, row, 0.0)
-
-    pay, inv_q, inv_k, mark = pl.pallas_call(
+    row = pltpu.VMEM((8, HD), jnp.float32)
+
+    pay, inv_q, inv_k, rows = pl.pallas_call(
         pack_kernel,
         out_shape=[shape((N_SEQ, BODY + EXTRA, HD)), inv, inv, shape((8, HD), jnp.float32)],
-        in_specs=[SCALARS] + [THERE] * 3, out_specs=[THERE, HERE, HERE, HERE],
-        scratch_shapes=[three, pltpu.VMEM((EXTRA, HD), jnp.bfloat16),
+        in_specs=[SCALARS] + [THERE] * 3 + [HERE] * 2, out_specs=[THERE, HERE, HERE, HERE],
+        scratch_shapes=[three, pltpu.VMEM((EXTRA, HD), jnp.bfloat16), row, row,
                         pltpu.SemaphoreType.DMA((3 * CUTS,)), pltpu.SemaphoreType.DMA((3 * H + N_SEQ,))],
         compiler_params=params(62), name="pack",
-    )(turn, q_in, k_in, v_in)
+    )(turn, q_in, k_in, v_in, gain_q[None], gain_k[None])
     got = lax.all_to_all(pay, "seq", 0, 0, tiled=True)
-    rows = lax.ppermute(over_y(hold(over_z(rows), mark)), ("dp", "seq"), around(-1))
+    rows = lax.ppermute(over_y(hold(over_z(rows), rows)), ("dp", "seq"), around(-1))
     lo, hi = windows(clip_ids)
     pay, part = attend_call(lo, hi, got, rows, clip_ids)
 
     got = lax.all_to_all(pay, "seq", 0, 0, tiled=True)
-    part = over_y(hold(over_z(part), part))
+    part = over_y(over_z(hold(part, part)))
     part = lax.dynamic_slice_in_dim(part, place, 1, 0)
     part = lax.ppermute(part, ("dp", "seq"), around(1))
+    part = jnp.broadcast_to(part, (N_SEQ, HD))[:, None]
     part, got = lax.optimization_barrier((part, got))
-    part = lax.all_to_all(jnp.broadcast_to(part, (N_SEQ, HD))[:, None], "seq", 0, 0, tiled=True)
+    part = lax.all_to_all(part, "seq", 0, 0, tiled=True)
     part = jnp.sum(part, axis=(0, 1))
 
     out = shape((TOK, WIDTH))

time: 110 us -> 111 us (level); the launches traced: 108 us -> 111 us
  starting transfers between devices: 51.3 us -> 56.1 us
  waiting for transfers between devices: 30.8 us -> 28.8 us
    all_to_all x1, starting transfers between devices: 4.1 us -> 8.85 us  [local(): part = lax.all_to_all(part, 'seq', 0, 0, tiled=True)]
    all_to_all x2, waiting for transfers between devices: 15.5 us -> 12.4 us  [local(): got = lax.all_to_all(pay, 'seq', 0, 0, tiled=True)]
    ppermute x2, starting transfers between devices: 6.27 us -> 8.15 us  [over_z(): return x + lax.ppermute(x, 'dp', [(d, d ^ 4) for d in range(64)])]
    ppermute x2, waiting for transfers between devices: 0.01 us -> 1.28 us  [over_z(): return x + lax.ppermute(x, 'dp', [(d, d ^ 4) for d in range(64)])]
  transfers between devices with their start and end apart: 13 -> 13, of which waited for: 7 -> 8; matrix products, arithmetic and copies ran while one was open for 0% -> 0% of each run, Pallas kernels for 7% -> 3%
where the time goes in v7:
time: 111 us
  starting transfers between devices  56.1 us (51%)
  waiting for transfers between devices  28.8 us (26%)
  Pallas kernels  20.4 us (18%)
  local copies, waits for them, and re-layouts  3.98 us (4%)
    ppermute x6, starting transfers between devices, sum_four(): one, two, three = (lax.ppermute(x, axis, pairs(k)) for k in (1, 2, 3))  16.8 us
    pallas_call x1, Pallas kernels, attend_call(): pl.pallas_call(attend_kernel, out_shape=[back, shape((8, HD), jnp.float32...  12.7 us
    all_to_all x2, waiting for transfers between devices, local(): got = lax.all_to_all(pay, 'seq', 0, 0, tiled=True)  12.4 us
    all_to_all x2, starting transfers between devices, local(): got = lax.all_to_all(pay, 'seq', 0, 0, tiled=True)  12.4 us
    all_to_all x1, starting transfers between devices, local(): part = lax.all_to_all(part, 'seq', 0, 0, tiled=True)  8.85 us
    ppermute x2, starting transfers between devices, over_z(): return x + lax.ppermute(x, 'dp', [(d, d ^ 4) for d in range(64)])  8.15 us
    ppermute x1, starting transfers between devices, local(): lax.ppermute(over_y(hold(over_z(rows), rows)), ('dp', 'seq'), around(-1))  8.04 us
    ppermute x6, waiting for transfers between devices, sum_four(): one, two, three = (lax.ppermute(x, axis, pairs(k)) for k in (1, 2, 3))  7.62 us
  transfers between devices with their start and end apart: 13, of which 8 were waited for; matrix products, arithmetic and copies ran while one was open for 0% of the time, Pallas kernels for 3%

profile of v7, /device:TPU:1, one launch (start us, length us, event | category | flops | bytes accessed | tf_op | source)
XLA Modules:
  0.0 110.5 jit_solution(183748650952821398)
XLA Ops:
  0.6 4.9 %pack.1 = (bf16[8,1168,128]{2,1,0:T(8,128)(2,1)}, f32[128,128]{1,0:T(8,128)}, f32[128,128]{1,0:T(8,128)}, f32[8,128]{1,0:T(8,128)}) custom-call(s32[1]{0:T(128)} %bitcast.turn_ref, bf16[128,3072]{1,0:T(8,128)(2,1)} %q_ref.3, bf16[128,3072]{1,0:T(8,128)(2,1)} %k_ref.3, bf16[128,3072]{1,0:T(8,128)(2,1)} %v_ref.1, f32[1,48]{1,0:T(1,128)} %bitcast.10, ...), custom_call_target="tpu_custom_call" | custom-call | tf_op jit(solution)/shard_map/pack/pallas_call | solution.py:360
  5.6 0.0 copy-start.4
  5.6 4.4 %collective-permute-start = (f32[8,128]{1,0:T(8,128)}, f32[8,128]{1,0:T(8,128)S(1)}, u32[]{:S(2)}, u32[]{:S(2)}) collective-permute-start(f32[8,128]{1,0:T(8,128)} %get-tuple-element.19.after_ref), channel_id=1, source_target_pairs={{0,32},{8,40},{16,48},{24,56},{32,0},{40,8},{48,16},{56,24},{64,96... | collective-permute-start | bytes 12296 | tf_op jit(solution)/shard_map/ppermute | solution.py:316
  10.0 8.0 %all-to-all-start = ((bf16[8,1168,128]{2,1,0:T(8,128)(2,1)}), bf16[8,1168,128]{2,1,0:T(8,128)(2,1)S(1)}, u32[]{:S(2)}, u32[]{:S(2)}) async-start(bf16[8,1168,128]{2,1,0:T(8,128)(2,1)} %get-tuple-element.18), calls=%async_computation | async-start | bytes 4784128 | tf_op jit(solution)/shard_map/all_to_all | solution.py:368
  17.9 0.0 collective-permute-done
  17.9 0.0 copy-done.4
  17.9 0.0 copy-start.3
  18.0 1.9 %collective-permute-start.2 = (f32[8,128]{1,0:T(8,128)S(1)}, f32[8,128]{1,0:T(8,128)S(1)}, u32[]{:S(2)}, u32[]{:S(2)}) collective-permute-start(f32[8,128]{1,0:T(8,128)S(1)} %hold.2), channel_id=1, source_target_pairs={{0,8},{8,16},{16,24},{24,0},{32,40},{40,48},{48,56},{56,32},{64,72... | collective-permute-start | bytes 12296 | tf_op jit(solution)/shard_map/ppermute | solution.py:311
  19.9 4.6 %collective-permute-start.3 = (f32[8,128]{1,0:T(8,128)S(1)}, f32[8,128]{1,0:T(8,128)S(1)}, u32[]{:S(2)}, u32[]{:S(2)}) collective-permute-start(f32[8,128]{1,0:T(8,128)S(1)} %hold.2), channel_id=1, source_target_pairs={{0,24},{8,0},{16,8},{24,16},{32,56},{40,32},{48,40},{56,48},{64,88... | collective-permute-start | bytes 12296 | tf_op jit(solution)/shard_map/ppermute | solution.py:311
  24.5 1.9 %collective-permute-start.1 = (f32[8,128]{1,0:T(8,128)S(1)}, f32[8,128]{1,0:T(8,128)S(1)}, u32[]{:S(2)}, u32[]{:S(2)}) collective-permute-start(f32[8,128]{1,0:T(8,128)S(1)} %hold.2), channel_id=1, source_target_pairs={{0,16},{8,24},{16,0},{24,8},{32,48},{40,56},{48,32},{56,40},{64,80... | collective-permute-start | bytes 12296 | tf_op jit(solution)/shard_map/ppermute | solution.py:311
  26.4 0.0 copy-done.3
  26.4 0.1 slice.13
  26.5 0.1 slice.12
  26.6 0.0 collective-permute-done.2
  26.6 0.0 collective-permute-done.3
  26.6 3.7 %collective-permute-done.1 = f32[8,128]{1,0:T(8,128)S(1)} collective-permute-done((f32[8,128]{1,0:T(8,128)S(1)}, f32[8,128]{1,0:T(8,128)S(1)}, u32[]{:S(2)}, u32[]{:S(2)}) %collective-permute-start.1) | collective-permute-done | bytes 4128 | tf_op jit(solution)/shard_map/ppermute | solution.py:311
  30.3 8.0 %collective-permute-start.4 = (f32[8,128]{1,0:T(8,128)S(1)}, f32[8,128]{1,0:T(8,128)S(1)}, u32[]{:S(2)}, u32[]{:S(2)}) collective-permute-start(f32[8,128]{1,0:T(8,128)S(1)} %add_add_fusion.1), channel_id=1, source_target_pairs={{0,0},{1,449},{2,386},{3,323},{4,260},{5,197},{6,134},{7,71},{8,8}... | collective-permute-start | bytes 12296 | tf_op jit(solution)/shard_map/ppermute | solution.py:369
  38.4 0.2 convert_reduce_fusion
  38.6 0.5 collective-permute-done.4.gain_ref
  39.1 8.3 %all-to-all-done.pay_ref = bf16[8,1168,128]{2,1,0:T(8,128)(2,1)S(1)} async-done(((bf16[8,1168,128]{2,1,0:T(8,128)(2,1)}), bf16[8,1168,128]{2,1,0:T(8,128)(2,1)S(1)}, u32[]{:S(2)}, u32[]{:S(2)}) %all-to-all-start) | async-done | bytes 2392096 | tf_op jit(solution)/shard_map/all_to_all | solution.py:368
  47.4 12.7 %attend.1 = (bf16[8,1184,128]{2,1,0:T(8,128)(2,1)S(1)}, f32[8,128]{1,0:T(8,128)S(1)}) custom-call(s32[4]{0:T(128)S(1)} %get-tuple-element.28.lo_ref, s32[4]{0:T(128)S(1)} %get-tuple-element.27.hi_ref, bf16[8,1168,128]{2,1,0:T(8,128)(2,1)S(1)} %all-to-all-done.pay_ref, f32[8,128]{1,0:T(8,128)S(1)} %collective-permute-done.4.gain_ref, s32[1,1024]{1,0:T(1,128)S(1)} %copy-done.3), custom_call_target="tpu_custom_call" | custom-call | tf_op jit(solution)/shard_map/attend/pallas_call | solution.py:336
  60.2 0.0 copy-start
  60.2 1.5 %copy-done = bf16[8,1184,128]{2,1,0:T(8,128)(2,1)} copy-done((bf16[8,1184,128]{2,1,0:T(8,128)(2,1)}, bf16[8,1184,128]{2,1,0:T(8,128)(2,1)S(1)}, u32[]{:S(2)}) %copy-start) | copy-done | bytes 2424856
  61.6 4.4 %all-to-all-start.1 = ((bf16[8,1184,128]{2,1,0:T(8,128)(2,1)}), bf16[8,1184,128]{2,1,0:T(8,128)(2,1)S(1)}, u32[]{:S(2)}, u32[]{:S(2)}) async-start(bf16[8,1184,128]{2,1,0:T(8,128)(2,1)} %copy-done), calls=%async_computation.1 | async-start | bytes 4849664 | tf_op jit(solution)/shard_map/all_to_all | solution.py:373
  66.0 0.0 copy-start.1
  66.0 0.0 copy-start.5
  66.0 0.0 copy-start.6
  66.0 3.8 %collective-permute-start.5 = (f32[8,128]{1,0:T(8,128)S(1)}, f32[8,128]{1,0:T(8,128)S(1)}, u32[]{:S(2)}, u32[]{:S(2)}) collective-permute-start(f32[8,128]{1,0:T(8,128)S(1)} %hold.3), channel_id=1, source_target_pairs={{0,32},{8,40},{16,48},{24,56},{32,0},{40,8},{48,16},{56,24},{64,96... | collective-permute-start | bytes 12296 | tf_op jit(solution)/shard_map/ppermute | solution.py:316
  69.8 1.3 %collective-permute-done.5 = f32[8,128]{1,0:T(8,128)S(1)} collective-permute-done((f32[8,128]{1,0:T(8,128)S(1)}, f32[8,128]{1,0:T(8,128)S(1)}, u32[]{:S(2)}, u32[]{:S(2)}) %collective-permute-start.5) | collective-permute-done | bytes 4128 | tf_op jit(solution)/shard_map/ppermute | solution.py:316
  71.1 1.9 %collective-permute-start.7 = (f32[8,128]{1,0:T(8,128)S(1)}, f32[8,128]{1,0:T(8,128)S(1)}, u32[]{:S(2)}, u32[]{:S(2)}) collective-permute-start(f32[8,128]{1,0:T(8,128)S(1)} %add.35), channel_id=1, source_target_pairs={{0,8},{8,16},{16,24},{24,0},{32,40},{40,48},{48,56},{56,32},{64,72... | collective-permute-start | bytes 12296 | tf_op jit(solution)/shard_map/ppermute | solution.py:311
  73.0 4.6 %collective-permute-start.8 = (f32[8,128]{1,0:T(8,128)S(1)}, f32[8,128]{1,0:T(8,128)S(1)}, u32[]{:S(2)}, u32[]{:S(2)}) collective-permute-start(f32[8,128]{1,0:T(8,128)S(1)} %add.35), channel_id=1, source_target_pairs={{0,24},{8,0},{16,8},{24,16},{32,56},{40,32},{48,40},{56,48},{64,88... | collective-permute-start | bytes 12296 | tf_op jit(solution)/shard_map/ppermute | solution.py:311
  77.6 1.9 %collective-permute-start.6 = (f32[8,128]{1,0:T(8,128)S(1)}, f32[8,128]{1,0:T(8,128)S(1)}, u32[]{:S(2)}, u32[]{:S(2)}) collective-permute-start(f32[8,128]{1,0:T(8,128)S(1)} %add.35), channel_id=1, source_target_pairs={{0,16},{8,24},{16,0},{24,8},{32,48},{40,56},{48,32},{56,40},{64,80... | collective-permute-start | bytes 12296 | tf_op jit(solution)/shard_map/ppermute | solution.py:311
  79.5 0.0 collective-permute-done.7
  79.6 0.0 collective-permute-done.8
  79.6 3.9 %collective-permute-done.6 = f32[8,128]{1,0:T(8,128)S(1)} collective-permute-done((f32[8,128]{1,0:T(8,128)S(1)}, f32[8,128]{1,0:T(8,128)S(1)}, u32[]{:S(2)}, u32[]{:S(2)}) %collective-permute-start.6) | collective-permute-done | bytes 4128 | tf_op jit(solution)/shard_map/ppermute | solution.py:311
  83.5 1.9 %collective-permute-start.9 = (f32[1,128]{1,0:T(1,128)S(1)}, f32[1,128]{1,0:T(1,128)S(1)}, u32[]{:S(2)}, u32[]{:S(2)}) collective-permute-start(f32[1,128]{1,0:T(1,128)S(1)} %constant_dynamic-slice_fusion), channel_id=1, source_target_pairs={{0,0},{1,65},{2,130},{3,195},{4,260},{5,325},{6,390},{7,455},{8,8}... | collective-permute-start | bytes 1544 | tf_op jit(solution)/shard_map/ppermute | solution.py:376
  85.4 6.4 %collective-permute-done.9 = f32[1,128]{1,0:T(1,128)S(1)} collective-permute-done((f32[1,128]{1,0:T(1,128)S(1)}, f32[1,128]{1,0:T(1,128)S(1)}, u32[]{:S(2)}, u32[]{:S(2)}) %collective-permute-start.9) | collective-permute-done | bytes 544 | tf_op jit(solution)/shard_map/ppermute | solution.py:376
  91.9 4.0 %all-to-all-done.1.pay_ref = bf16[8,1184,128]{2,1,0:T(8,128)(2,1)S(1)} async-done(((bf16[8,1184,128]{2,1,0:T(8,128)(2,1)}), bf16[8,1184,128]{2,1,0:T(8,128)(2,1)S(1)}, u32[]{:S(2)}, u32[]{:S(2)}) %all-to-all-start.1) | async-done | bytes 2424864 | tf_op jit(solution)/shard_map/all_to_all | solution.py:373
  95.9 0.6 broadcast_in_dim_broadcast_in_dim.2
  96.5 8.8 %all-to-all-start.2 = ((f32[8,1,128]{2,1,0:T(1,128)}), f32[8,1,128]{2,1,0:T(1,128)S(1)}, u32[]{:S(2)}, u32[]{:S(2)}) async-start(f32[8,1,128]{2,1,0:T(1,128)} %broadcast_in_dim_broadcast_in_dim.2), calls=%async_computation.2 | async-start | bytes 8192 | tf_op jit(solution)/shard_map/all_to_all | solution.py:379
  105.3 0.0 copy-done.1
  105.3 0.0 copy-done.5
  105.3 0.0 copy-done.6
  105.3 0.0 copy-start.2
  105.4 1.1 %copy-done.2 = bf16[128,3072]{1,0:T(8,128)(2,1)S(1)} copy-done((bf16[128,3072]{1,0:T(8,128)(2,1)S(1)}, bf16[128,3072]{1,0:T(8,128)(2,1)}, u32[]{:S(2)}) %copy-start.2) | copy-done | bytes 786456
  106.5 2.8 %final.1 = (bf16[128,3072]{1,0:T(8,128)(2,1)}, bf16[128,3072]{1,0:T(8,128)(2,1)}, bf16[128,3072]{1,0:T(8,128)(2,1)}) custom-call(s32[1]{0:T(128)} %bitcast.turn_ref, bf16[128,3072]{1,0:T(8,128)(2,1)S(1)} %copy-done.1, bf16[128,3072]{1,0:T(8,128)(2,1)S(1)} %copy-done.2, f32[128,128]{1,0:T(8,128)S(1)} %copy-done.5, f32[128,128]{1,0:T(8,128)S(1)} %copy-done.6, ...), custom_call_target="tpu_custom_call" | custom-call | flops 17179869184 | bytes 33554432 | tf_op jit(solution)/shard_map/final/pallas_call | solution.py:383
  109.3 0.6 all-to-all-done.2
  109.9 0.6 fusion
  (8 shorter events, 0.0 us)
Async XLA Ops:
  5.6 12.4 %copy-start.4 = (f32[8,128]{1,0:T(8,128)S(1)}, f32[8,128]{1,0:T(8,128)}, u32[]{:S(2)}) copy-start(f32[8,128]{1,0:T(8,128)} %get-tuple-element.19.after_ref) | copy-start | bytes 12292
  5.6 12.3 %collective-permute-start = (f32[8,128]{1,0:T(8,128)}, f32[8,128]{1,0:T(8,128)S(1)}, u32[]{:S(2)}, u32[]{:S(2)}) collective-permute-start(f32[8,128]{1,0:T(8,128)} %get-tuple-element.19.after_ref), channel_id=1, source_target_pairs={{0,32},{8,40},{16,48},{24,56},{32,0},{40,8},{48,16},{56,24},{64,96... | collective-permute-start | bytes 12296 | tf_op jit(solution)/shard_map/ppermute | solution.py:316
  10.0 37.5 %all-to-all-start = ((bf16[8,1168,128]{2,1,0:T(8,128)(2,1)}), bf16[8,1168,128]{2,1,0:T(8,128)(2,1)S(1)}, u32[]{:S(2)}, u32[]{:S(2)}) async-start(bf16[8,1168,128]{2,1,0:T(8,128)(2,1)} %get-tuple-element.18), calls=%async_computation | async-start | bytes 4784128 | tf_op jit(solution)/shard_map/all_to_all | solution.py:368
  17.9 8.5 %copy-start.3 = (s32[1,1024]{1,0:T(1,128)S(1)}, s32[1,1024]{1,0:T(1,128)}, u32[]{:S(2)}) copy-start(s32[1,1024]{1,0:T(1,128)} %ids_ref.1) | copy-start | bytes 12292
  18.0 8.6 %collective-permute-start.2 = (f32[8,128]{1,0:T(8,128)S(1)}, f32[8,128]{1,0:T(8,128)S(1)}, u32[]{:S(2)}, u32[]{:S(2)}) collective-permute-start(f32[8,128]{1,0:T(8,128)S(1)} %hold.2), channel_id=1, source_target_pairs={{0,8},{8,16},{16,24},{24,0},{32,40},{40,48},{48,56},{56,32},{64,72... | collective-permute-start | bytes 12296 | tf_op jit(solution)/shard_map/ppermute | solution.py:311
  19.9 6.7 %collective-permute-start.3 = (f32[8,128]{1,0:T(8,128)S(1)}, f32[8,128]{1,0:T(8,128)S(1)}, u32[]{:S(2)}, u32[]{:S(2)}) collective-permute-start(f32[8,128]{1,0:T(8,128)S(1)} %hold.2), channel_id=1, source_target_pairs={{0,24},{8,0},{16,8},{24,16},{32,56},{40,32},{48,40},{56,48},{64,88... | collective-permute-start | bytes 12296 | tf_op jit(solution)/shard_map/ppermute | solution.py:311
  24.5 5.9 %collective-permute-start.1 = (f32[8,128]{1,0:T(8,128)S(1)}, f32[8,128]{1,0:T(8,128)S(1)}, u32[]{:S(2)}, u32[]{:S(2)}) collective-permute-start(f32[8,128]{1,0:T(8,128)S(1)} %hold.2), channel_id=1, source_target_pairs={{0,16},{8,24},{16,0},{24,8},{32,48},{40,56},{48,32},{56,40},{64,80... | collective-permute-start | bytes 12296 | tf_op jit(solution)/shard_map/ppermute | solution.py:311
  30.3 8.8 %collective-permute-start.4 = (f32[8,128]{1,0:T(8,128)S(1)}, f32[8,128]{1,0:T(8,128)S(1)}, u32[]{:S(2)}, u32[]{:S(2)}) collective-permute-start(f32[8,128]{1,0:T(8,128)S(1)} %add_add_fusion.1), channel_id=1, source_target_pairs={{0,0},{1,449},{2,386},{3,323},{4,260},{5,197},{6,134},{7,71},{8,8}... | collective-permute-start | bytes 12296 | tf_op jit(solution)/shard_map/ppermute | solution.py:369
  60.2 1.5 %copy-start = (bf16[8,1184,128]{2,1,0:T(8,128)(2,1)}, bf16[8,1184,128]{2,1,0:T(8,128)(2,1)S(1)}, u32[]{:S(2)}) copy-start(bf16[8,1184,128]{2,1,0:T(8,128)(2,1)S(1)} %get-tuple-element.21) | copy-start | bytes 7274500
  61.6 34.3 %all-to-all-start.1 = ((bf16[8,1184,128]{2,1,0:T(8,128)(2,1)}), bf16[8,1184,128]{2,1,0:T(8,128)(2,1)S(1)}, u32[]{:S(2)}, u32[]{:S(2)}) async-start(bf16[8,1184,128]{2,1,0:T(8,128)(2,1)} %copy-done), calls=%async_computation.1 | async-start | bytes 4849664 | tf_op jit(solution)/shard_map/all_to_all | solution.py:373
  66.0 39.3 %copy-start.1 = (bf16[128,3072]{1,0:T(8,128)(2,1)S(1)}, bf16[128,3072]{1,0:T(8,128)(2,1)}, u32[]{:S(2)}) copy-start(bf16[128,3072]{1,0:T(8,128)(2,1)} %q_ref.3) | copy-start | bytes 2359300
  66.0 39.3 %copy-start.5 = (f32[128,128]{1,0:T(8,128)S(1)}, f32[128,128]{1,0:T(8,128)}, u32[]{:S(2)}) copy-start(f32[128,128]{1,0:T(8,128)} %get-tuple-element.16.inv_q_ref) | copy-start | bytes 196612
  66.0 39.3 %copy-start.6 = (f32[128,128]{1,0:T(8,128)S(1)}, f32[128,128]{1,0:T(8,128)}, u32[]{:S(2)}) copy-start(f32[128,128]{1,0:T(8,128)} %get-tuple-element.17.inv_k_ref) | copy-start | bytes 196612
  66.0 5.1 %collective-permute-start.5 = (f32[8,128]{1,0:T(8,128)S(1)}, f32[8,128]{1,0:T(8,128)S(1)}, u32[]{:S(2)}, u32[]{:S(2)}) collective-permute-start(f32[8,128]{1,0:T(8,128)S(1)} %hold.3), channel_id=1, source_target_pairs={{0,32},{8,40},{16,48},{24,56},{32,0},{40,8},{48,16},{56,24},{64,96... | collective-permute-start | bytes 12296 | tf_op jit(solution)/shard_map/ppermute | solution.py:316
  71.1 8.4 %collective-permute-start.7 = (f32[8,128]{1,0:T(8,128)S(1)}, f32[8,128]{1,0:T(8,128)S(1)}, u32[]{:S(2)}, u32[]{:S(2)}) collective-permute-start(f32[8,128]{1,0:T(8,128)S(1)} %add.35), channel_id=1, source_target_pairs={{0,8},{8,16},{16,24},{24,0},{32,40},{40,48},{48,56},{56,32},{64,72... | collective-permute-start | bytes 12296 | tf_op jit(solution)/shard_map/ppermute | solution.py:311
  73.0 6.5 %collective-permute-start.8 = (f32[8,128]{1,0:T(8,128)S(1)}, f32[8,128]{1,0:T(8,128)S(1)}, u32[]{:S(2)}, u32[]{:S(2)}) collective-permute-start(f32[8,128]{1,0:T(8,128)S(1)} %add.35), channel_id=1, source_target_pairs={{0,24},{8,0},{16,8},{24,16},{32,56},{40,32},{48,40},{56,48},{64,88... | collective-permute-start | bytes 12296 | tf_op jit(solution)/shard_map/ppermute | solution.py:311
  77.6 5.9 %collective-permute-start.6 = (f32[8,128]{1,0:T(8,128)S(1)}, f32[8,128]{1,0:T(8,128)S(1)}, u32[]{:S(2)}, u32[]{:S(2)}) collective-permute-start(f32[8,128]{1,0:T(8,128)S(1)} %add.35), channel_id=1, source_target_pairs={{0,16},{8,24},{16,0},{24,8},{32,48},{40,56},{48,32},{56,40},{64,80... | collective-permute-start | bytes 12296 | tf_op jit(solution)/shard_map/ppermute | solution.py:311
  83.5 8.4 %collective-permute-start.9 = (f32[1,128]{1,0:T(1,128)S(1)}, f32[1,128]{1,0:T(1,128)S(1)}, u32[]{:S(2)}, u32[]{:S(2)}) collective-permute-start(f32[1,128]{1,0:T(1,128)S(1)} %constant_dynamic-slice_fusion), channel_id=1, source_target_pairs={{0,0},{1,65},{2,130},{3,195},{4,260},{5,325},{6,390},{7,455},{8,8}... | collective-permute-start | bytes 1544 | tf_op jit(solution)/shard_map/ppermute | solution.py:376
  96.5 13.4 %all-to-all-start.2 = ((f32[8,1,128]{2,1,0:T(1,128)}), f32[8,1,128]{2,1,0:T(1,128)S(1)}, u32[]{:S(2)}, u32[]{:S(2)}) async-start(f32[8,1,128]{2,1,0:T(1,128)} %broadcast_in_dim_broadcast_in_dim.2), calls=%async_computation.2 | async-start | bytes 8192 | tf_op jit(solution)/shard_map/all_to_all | solution.py:379
  105.3 1.1 %copy-start.2 = (bf16[128,3072]{1,0:T(8,128)(2,1)S(1)}, bf16[128,3072]{1,0:T(8,128)(2,1)}, u32[]{:S(2)}) copy-start(bf16[128,3072]{1,0:T(8,128)(2,1)} %k_ref.3) | copy-start | bytes 2359300
